TPU v7x, 256 devices: a whole 4x4x8 slice. The times are simulated.
256 devices in a mesh: req: 8 (over x, core), ctx: 32 (over y, z).
Axes of the slice: x: 4, y: 4, z: 8, core: 2. Of those that a mesh axis runs over, the one named last changes fastest.
Arguments:
- suffix_hidden: bfloat16 [8, 2048, 7168], P('req', 'ctx'), may hold values from -6 to 6
- kv_down: bfloat16 [7168, 576], P('ctx'), may hold values from -0.0625 to 0.0625
- kv_gain: float32 [512], replicated, may hold values from 0.25 to 1.75
- queries: bfloat16 [8, 2048, 64, 576], P('req', 'ctx'), may hold values from -300 to 300
- pool: bfloat16 [96, 32, 576], P('req', 'ctx'), may hold values from -4 to 4
- hit_holder: int32 [8, 8], replicated, may hold values from 0 to 7, as said below
- hit_slot: int32 [8, 8], replicated, may hold values from 0 to 11, as said below
- hit_count: int32 [8], replicated, may hold values from 4 to 8, as said below
Outputs:
- attended: bfloat16 [8, 2048, 64, 512], P('req', 'ctx')
Inputs may be any that keep to these rules, and one draw needn't show every extreme that they name: `hit_holder`: entry j of request r is used when j < hit_count[r]. Of one request's used entries at most 2 name the same holder, and some request has 2 on one holder. Unused entries are in range and ignored. `hit_slot`: two used entries of one request never name the same holder and place. `hit_count`: some request has 8.
All inputs are finite; a program needn't handle non-finite values.
Results may differ from a plain program's by a relative error of at most 0.0065.
Values may be sent and summed in bfloat16 or wider, within the bound.
No kernel may reach another device: no remote copies, remote signals or barrier semaphores. Data moves between devices by JAX's collectives and lax.ppermute only.
A program may use at most 64 MiB of HBM per device.

v0:
```python
import math

import jax
import jax.numpy as jnp
from jax import lax
from jax.sharding import PartitionSpec as P

PAGE = 32
CAP = 2


score_scale = 192.0 ** (-0.5)
rope_base = 10000.0
norm_eps = 1e-06


def rotate(rope_part, positions):
    half = rope_part.shape[1] // 2
    steps = jnp.arange(half, dtype=jnp.float32) * (2.0 / rope_part.shape[1])
    freqs = jnp.exp(-steps * jnp.log(rope_base))
    angles = positions[:, None] * freqs[None, :]
    cosine = jnp.cos(angles)
    sine = jnp.sin(angles)
    first = rope_part[:, :half]
    second = rope_part[:, half:]
    return jnp.concatenate([first * cosine - second * sine, second * cosine + first * sine], 1)


def finish_keys(latent, kv_gain, start):
    width = kv_gain.shape[0]
    compressed = latent[:, :width]
    mean_square = jnp.mean(compressed * compressed, axis=1, keepdims=True)
    normed = compressed * lax.rsqrt(mean_square + norm_eps) * kv_gain
    positions = (start + jnp.arange(latent.shape[0], dtype=jnp.int32)).astype(jnp.float32)
    return jnp.concatenate([normed, rotate(latent[:, width:], positions)], 1).astype(jnp.bfloat16)


def absorb(carry, key_rows, allowed, query_rows, value_width):
    running_peak, running_total, accum = carry
    scores = (
        lax.dot_general(
            key_rows, query_rows, (((1,), (1,)), ((), ())), preferred_element_type=jnp.float32
        )
        * score_scale
    )
    peak = jnp.maximum(running_peak, jnp.max(jnp.where(allowed, scores, -1e30), axis=0))
    weights = jnp.where(allowed, jnp.exp(scores - peak[None, :]), 0.0)
    factor = jnp.exp(running_peak - peak)
    total = running_total * factor + jnp.sum(weights, axis=0)
    update = lax.dot_general(
        weights.astype(jnp.bfloat16),
        key_rows[:, :value_width],
        (((0,), (0,)), ((), ())),
        preferred_element_type=jnp.float32,
    )
    return (peak, total, accum * factor[:, None] + update)


def shards(suffix_hidden, kv_down, kv_gain, queries, pool, hit_holder, hit_slot, hit_count):
    req_index = lax.axis_index("req")
    ctx_index = lax.axis_index("ctx")
    ctx_size = lax.axis_size("ctx")
    hidden = suffix_hidden[0]
    tokens_dev = hidden.shape[0]
    requests = hit_holder.shape[0]
    list_len = hit_holder.shape[1]
    page_part = pool.shape[1]
    latent_width = pool.shape[2]
    value_width = kv_gain.shape[0]
    heads = queries.shape[2]
    entry_ids = jnp.arange(list_len, dtype=jnp.int32)
    used = entry_ids[None, :] < hit_count[:, None]
    earlier = (
        (hit_holder[:, :, None] == hit_holder[:, None, :])
        & used[:, None, :]
        & (entry_ids[None, None, :] < entry_ids[None, :, None])
    )
    rank = jnp.sum(earlier.astype(jnp.int32), axis=2)
    cap_ids = jnp.arange(CAP, dtype=jnp.int32)
    pick = (
        used[:, None, :]
        & (hit_holder[:, None, :] == req_index)
        & (rank[:, None, :] == cap_ids[None, :, None])
    )
    source_place = jnp.sum(jnp.where(pick, hit_slot[:, None, :], 0), axis=2)
    present = jnp.any(pick, axis=2)
    outgoing = jnp.take(pool, source_place.reshape(-1), axis=0).reshape(
        requests, CAP, page_part, latent_width
    )
    outgoing = jnp.where(present[:, :, None, None], outgoing, jnp.zeros_like(outgoing))
    incoming = lax.all_to_all(outgoing, "req", split_axis=0, concat_axis=0, tiled=True)
    mine_holder = lax.dynamic_index_in_dim(hit_holder, req_index, 0, keepdims=False)
    mine_rank = lax.dynamic_index_in_dim(rank, req_index, 0, keepdims=False)
    mine_used = lax.dynamic_index_in_dim(used, req_index, 0, keepdims=False)
    mine_count = lax.dynamic_index_in_dim(hit_count, req_index, 0, keepdims=False)
    holder_ids = jnp.arange(requests, dtype=jnp.int32)
    match = (
        mine_used[None, None, :]
        & (mine_holder[None, None, :] == holder_ids[:, None, None])
        & (mine_rank[None, None, :] == cap_ids[None, :, None])
    )
    filled = jnp.any(match, axis=2)
    cache = incoming
    cache_ok = filled[:, :, None].reshape(-1)
    cache = cache.reshape(-1, latent_width)
    latent = jnp.dot(
        hidden,
        lax.all_gather(kv_down, "ctx", axis=0, tiled=True),
        preferred_element_type=jnp.float32,
    )
    fresh = finish_keys(latent, kv_gain, mine_count * PAGE + ctx_index * tokens_dev)
    key_block = jnp.concatenate([fresh, cache], 0)
    block_len = key_block.shape[0]
    query_rows = queries[0].reshape(-1, latent_width)
    row_count = query_rows.shape[0]
    query_pos = ctx_index * tokens_dev + jnp.arange(row_count, dtype=jnp.int32) // heads
    gathered = lax.all_gather(key_block, "ctx", axis=0, tiled=True)
    group = math.gcd(ctx_size, 8)
    group_count = ctx_size // group
    grouped = gathered.reshape(group_count, group * block_len, latent_width)
    local_ids = jnp.arange(block_len, dtype=jnp.int32)
    is_fresh = local_ids < tokens_dev
    row_ok = jnp.concatenate([jnp.zeros((tokens_dev,), jnp.bool_), cache_ok])
    shard_ids = jnp.arange(group, dtype=jnp.int32)

    def one_group(state, operands):
        keys_here, first_shard = operands
        anchors = first_shard + shard_ids
        key_pos = (anchors[:, None] * tokens_dev + local_ids[None, :]).reshape(-1)
        fresh_rows = jnp.broadcast_to(is_fresh[None, :], (group, block_len)).reshape(-1)
        cache_rows = jnp.broadcast_to(row_ok[None, :], (group, block_len)).reshape(-1)
        allowed = cache_rows[:, None] | fresh_rows[:, None] & (
            key_pos[:, None] <= query_pos[None, :]
        )
        return (absorb(state, keys_here, allowed, query_rows, value_width), None)

    firsts = jnp.arange(group_count, dtype=jnp.int32) * group
    start_state = (
        jnp.full((row_count,), -1e30, jnp.float32),
        jnp.zeros((row_count,), jnp.float32),
        jnp.zeros((row_count, value_width), jnp.float32),
    )
    final_state, unused = lax.scan(one_group, start_state, (grouped, firsts))
    final_peak, final_total, final_accum = final_state
    return (
        (final_accum / final_total[:, None])
        .astype(jnp.bfloat16)
        .reshape(1, tokens_dev, heads, value_width)
    )


def solution(mesh):
    in_specs = (
        P("req", "ctx", None),
        P("ctx", None),
        P(),
        P("req", "ctx", None, None),
        P("req", "ctx", None),
        P(),
        P(),
        P(),
    )
    out_specs = P("req", "ctx", None, None)
    return jax.shard_map(shards, mesh=mesh, in_specs=in_specs, out_specs=out_specs, check_vma=False)
```

profile of v0, /device:TPU:8, one launch (start us, length us, event | category | flops | bytes accessed | tf_op | source)
XLA Modules:
  0.0 312.4 jit_solution(7644577905150984146)
XLA Ops:
  6.5 0.7 all-gather.3.cloned.1.call-update
  7.3 0.8 compare_and_fusion
  8.0 1.0 convert_reduce_fusion
  9.1 0.8 select_reduce_fusion.1
  10.1 0.2 fusion.39
  10.5 1.3 gather_fusion
  11.8 0.7 broadcast_select_fusion.1
  12.5 4.3 %all-to-all-start = ((bf16[8,2,1,576]{3,1,2,0:T(2,128)(2,1)}), bf16[8,2,1,576]{3,1,2,0:T(2,128)(2,1)S(1)}, u32[]{:S(2)}, u32[]{:S(2)}) async-start(bf16[8,2,1,576]{3,1,2,0:T(2,128)(2,1)} %broadcast_select_fusion.1), calls=%async_computation | async-start | bytes 40960 | tf_op jit(solution)/shard_map/all_to_all | solution.py:91
  16.9 1.3 dynamic_slice.29
  18.8 3.4 %all-to-all-done = bf16[8,2,1,576]{3,1,2,0:T(2,128)(2,1)S(1)} async-done(((bf16[8,2,1,576]{3,1,2,0:T(2,128)(2,1)}), bf16[8,2,1,576]{3,1,2,0:T(2,128)(2,1)S(1)}, u32[]{:S(2)}, u32[]{:S(2)}) %all-to-all-start) | async-done | bytes 18464 | tf_op jit(solution)/shard_map/all_to_all | solution.py:91
  22.2 91.6 %all-gather.3.cloned.1.call-done = bf16[7168,576]{1,0:T(8,128)(2,1)} async-done(((bf16[224,576]{1,0:T(8,128)(2,1)}), bf16[7168,576]{1,0:T(8,128)(2,1)}) %all-gather.3.cloned.1.call-update) | async-done | bytes 8257552 | tf_op jit(solution)/shard_map/all_gather | solution.py:108
  113.8 5.2 %fusion.28 = f32[64,576]{1,0:T(8,128)S(1)} fusion(bf16[7168,576]{1,0:T(8,128)(2,1)} %all-gather.3.cloned.1.call-done, bf16[1,64,7168]{2,1,0:T(8,128)(2,1)S(1)} %copy-done), kind=kOutput, calls=%fused_computation.40 | convolution fusion | flops 528482304 | bytes 9322496 | tf_op jit(solution)/shard_map/dot_general | solution.py:106
  119.0 0.1 multiply_reduce_fusion
  119.3 0.2 fusion.35
  119.8 0.7 pad_maximum_fusion
  120.6 0.7 fusion.41
  121.3 0.1 and_reduce_fusion
  121.8 76.3 %all-gather.5.cloned.1.call-done = bf16[2560,576]{1,0:T(8,128)(2,1)} async-done(((bf16[80,576]{1,0:T(8,128)(2,1)}), bf16[2560,576]{1,0:T(8,128)(2,1)}) %all-gather.5.cloned.1.call-update) | async-done | bytes 2949136 | tf_op jit(solution)/shard_map/all_gather | solution.py:117
  198.1 102.3 %while.15 = (s32[]{:T(128)}, f32[4096]{0:T(1024)S(1)}, f32[4096]{0:T(1024)S(1)}, f32[4096,512]{1,0:T(8,128)}, pred[80]{0:T(512)(128)(4,1)S(1)}, /*index=5*/s32[4...) while((s32[]{:T(128)}, f32[4096]{0:T(1024)S(1)}, ...), condition=%wide.region_8.9_spmd.clone, body=%wide.region_5.8_spmd.clone.sunk | while | flops 5763032064 | bytes 114894088 | solution.py:143
  198.1 0.6 dynamic_slice.43
  198.7 0.6 fusion.62
  199.7 1.4 dynamic-slice_bitcast_fusion.3
  201.1 7.5 %select_reduce_fusion.3 = (f32[4096]{0:T(1024)S(1)}, f32[640,4096]{1,0:T(8,128)S(1)}) fusion(s32[4096]{0:T(1024)S(1)} %fusion.61, s32[640]{0:T(1024)S(1)} %add.168, pred[640]{0:T(1024)(128)(4,1)S(1)} %and.155, pred[640]{0:T(1024)(128)(4,1)S(1)} %or.44, bf16[640,576]{1,0:T(8,128)(2,1)S(1)} %dynamic-slice_bitcast_fusion.3, ...), kind=kOutput, calls=%fused_computation.6.clone.1 | convolution fusion | flops 3035623424 | bytes 15978240 | tf_op jit(solution)/shard_map/while/body/eval_jaxpr/dot_general | solution.py:41
  208.7 4.5 %fusion.63 = f32[4096]{0:T(1024)S(1)} fusion(f32[640,4096]{1,0:T(8,128)S(1)} %get-tuple-element.198, f32[4096]{0:T(1024)S(1)} %select_maximum_fusion.2, s32[4096]{0:T(1024)S(1)} %fusion.61, s32[640]{0:T(1024)S(1)} %add.168, pred[640]{0:T(1024)(128)(4,1)S(1)} %and.155, pred[640]{0:T(1024)(128)(4,1)S(1)} %or.44), kind=kLoop, calls=%fused_computation.11.clone.1 | loop fusion | flops 18345984 | bytes 10538752 | tf_op jit(solution)/shard_map/while/body/eval_jaxpr/reduce_sum | solution.py:49
  213.2 7.2 %fusion.65 = f32[4096,512]{1,0:T(8,128)S(1)} fusion(f32[4096,512]{1,0:T(8,128)S(1)} %bitcast.35, f32[640,4096]{1,0:T(8,128)S(1)} %get-tuple-element.198, f32[4096]{0:T(1024)S(1)} %select_maximum_fusion.2, s32[4096]{0:T(1024)S(1)} %fusion.61, s32[640]{0:T(1024)S(1)} %add.168, pred[640]{0:T(1024)(128)(4,1)S(1)} %and.155, pred[640]{0:T(1024)(128)(4,1)S(1)} %or.44, ...), kind=kOutput, calls=%fused_computation.9.clone.1 | convolution fusion | flops 2708996096 | bytes 27973632 | tf_op jit(solution)/shard_map/while/body/eval_jaxpr/dot_general | solution.py:50
  220.5 3.2 %copy-done.1 = f32[4096,512]{1,0:T(8,128)} copy-done((f32[4096,512]{1,0:T(8,128)}, f32[4096,512]{1,0:T(8,128)S(1)}, u32[]{:S(2)}) %copy-start.1) | copy-done | bytes 8388632 | tf_op jit(solution)/shard_map/while
  223.7 0.6 dynamic_slice.43
  224.3 0.6 fusion.62
  225.3 1.4 dynamic-slice_bitcast_fusion.3
  226.7 7.5 %select_reduce_fusion.3 = (f32[4096]{0:T(1024)S(1)}, f32[640,4096]{1,0:T(8,128)S(1)}) fusion(s32[4096]{0:T(1024)S(1)} %fusion.61, s32[640]{0:T(1024)S(1)} %add.168, pred[640]{0:T(1024)(128)(4,1)S(1)} %and.155, pred[640]{0:T(1024)(128)(4,1)S(1)} %or.44, bf16[640,576]{1,0:T(8,128)(2,1)S(1)} %dynamic-slice_bitcast_fusion.3, ...), kind=kOutput, calls=%fused_computation.6.clone.1 | convolution fusion | flops 3035623424 | bytes 15978240 | tf_op jit(solution)/shard_map/while/body/eval_jaxpr/dot_general | solution.py:41
  234.2 4.5 %fusion.63 = f32[4096]{0:T(1024)S(1)} fusion(f32[640,4096]{1,0:T(8,128)S(1)} %get-tuple-element.198, f32[4096]{0:T(1024)S(1)} %select_maximum_fusion.2, s32[4096]{0:T(1024)S(1)} %fusion.61, s32[640]{0:T(1024)S(1)} %add.168, pred[640]{0:T(1024)(128)(4,1)S(1)} %and.155, pred[640]{0:T(1024)(128)(4,1)S(1)} %or.44), kind=kLoop, calls=%fused_computation.11.clone.1 | loop fusion | flops 18345984 | bytes 10538752 | tf_op jit(solution)/shard_map/while/body/eval_jaxpr/reduce_sum | solution.py:49
  238.8 7.2 %fusion.65 = f32[4096,512]{1,0:T(8,128)S(1)} fusion(f32[4096,512]{1,0:T(8,128)S(1)} %bitcast.35, f32[640,4096]{1,0:T(8,128)S(1)} %get-tuple-element.198, f32[4096]{0:T(1024)S(1)} %select_maximum_fusion.2, s32[4096]{0:T(1024)S(1)} %fusion.61, s32[640]{0:T(1024)S(1)} %add.168, pred[640]{0:T(1024)(128)(4,1)S(1)} %and.155, pred[640]{0:T(1024)(128)(4,1)S(1)} %or.44, ...), kind=kOutput, calls=%fused_computation.9.clone.1 | convolution fusion | flops 2708996096 | bytes 27973632 | tf_op jit(solution)/shard_map/while/body/eval_jaxpr/dot_general | solution.py:50
  246.1 3.2 %copy-done.1 = f32[4096,512]{1,0:T(8,128)} copy-done((f32[4096,512]{1,0:T(8,128)}, f32[4096,512]{1,0:T(8,128)S(1)}, u32[]{:S(2)}) %copy-start.1) | copy-done | bytes 8388632 | tf_op jit(solution)/shard_map/while
  249.3 0.6 dynamic_slice.43
  249.9 0.6 fusion.62
  250.9 1.4 dynamic-slice_bitcast_fusion.3
  252.3 7.5 %select_reduce_fusion.3 = (f32[4096]{0:T(1024)S(1)}, f32[640,4096]{1,0:T(8,128)S(1)}) fusion(s32[4096]{0:T(1024)S(1)} %fusion.61, s32[640]{0:T(1024)S(1)} %add.168, pred[640]{0:T(1024)(128)(4,1)S(1)} %and.155, pred[640]{0:T(1024)(128)(4,1)S(1)} %or.44, bf16[640,576]{1,0:T(8,128)(2,1)S(1)} %dynamic-slice_bitcast_fusion.3, ...), kind=kOutput, calls=%fused_computation.6.clone.1 | convolution fusion | flops 3035623424 | bytes 15978240 | tf_op jit(solution)/shard_map/while/body/eval_jaxpr/dot_general | solution.py:41
  259.8 4.5 %fusion.63 = f32[4096]{0:T(1024)S(1)} fusion(f32[640,4096]{1,0:T(8,128)S(1)} %get-tuple-element.198, f32[4096]{0:T(1024)S(1)} %select_maximum_fusion.2, s32[4096]{0:T(1024)S(1)} %fusion.61, s32[640]{0:T(1024)S(1)} %add.168, pred[640]{0:T(1024)(128)(4,1)S(1)} %and.155, pred[640]{0:T(1024)(128)(4,1)S(1)} %or.44), kind=kLoop, calls=%fused_computation.11.clone.1 | loop fusion | flops 18345984 | bytes 10538752 | tf_op jit(solution)/shard_map/while/body/eval_jaxpr/reduce_sum | solution.py:49
  264.4 7.2 %fusion.65 = f32[4096,512]{1,0:T(8,128)S(1)} fusion(f32[4096,512]{1,0:T(8,128)S(1)} %bitcast.35, f32[640,4096]{1,0:T(8,128)S(1)} %get-tuple-element.198, f32[4096]{0:T(1024)S(1)} %select_maximum_fusion.2, s32[4096]{0:T(1024)S(1)} %fusion.61, s32[640]{0:T(1024)S(1)} %add.168, pred[640]{0:T(1024)(128)(4,1)S(1)} %and.155, pred[640]{0:T(1024)(128)(4,1)S(1)} %or.44, ...), kind=kOutput, calls=%fused_computation.9.clone.1 | convolution fusion | flops 2708996096 | bytes 27973632 | tf_op jit(solution)/shard_map/while/body/eval_jaxpr/dot_general | solution.py:50
  271.7 3.2 %copy-done.1 = f32[4096,512]{1,0:T(8,128)} copy-done((f32[4096,512]{1,0:T(8,128)}, f32[4096,512]{1,0:T(8,128)S(1)}, u32[]{:S(2)}) %copy-start.1) | copy-done | bytes 8388632 | tf_op jit(solution)/shard_map/while
  274.9 0.6 dynamic_slice.43
  275.4 0.6 fusion.62
  276.5 1.4 dynamic-slice_bitcast_fusion.3
  277.9 7.5 %select_reduce_fusion.3 = (f32[4096]{0:T(1024)S(1)}, f32[640,4096]{1,0:T(8,128)S(1)}) fusion(s32[4096]{0:T(1024)S(1)} %fusion.61, s32[640]{0:T(1024)S(1)} %add.168, pred[640]{0:T(1024)(128)(4,1)S(1)} %and.155, pred[640]{0:T(1024)(128)(4,1)S(1)} %or.44, bf16[640,576]{1,0:T(8,128)(2,1)S(1)} %dynamic-slice_bitcast_fusion.3, ...), kind=kOutput, calls=%fused_computation.6.clone.1 | convolution fusion | flops 3035623424 | bytes 15978240 | tf_op jit(solution)/shard_map/while/body/eval_jaxpr/dot_general | solution.py:41
  285.4 4.5 %fusion.63 = f32[4096]{0:T(1024)S(1)} fusion(f32[640,4096]{1,0:T(8,128)S(1)} %get-tuple-element.198, f32[4096]{0:T(1024)S(1)} %select_maximum_fusion.2, s32[4096]{0:T(1024)S(1)} %fusion.61, s32[640]{0:T(1024)S(1)} %add.168, pred[640]{0:T(1024)(128)(4,1)S(1)} %and.155, pred[640]{0:T(1024)(128)(4,1)S(1)} %or.44), kind=kLoop, calls=%fused_computation.11.clone.1 | loop fusion | flops 18345984 | bytes 10538752 | tf_op jit(solution)/shard_map/while/body/eval_jaxpr/reduce_sum | solution.py:49
  290.0 7.2 %fusion.65 = f32[4096,512]{1,0:T(8,128)S(1)} fusion(f32[4096,512]{1,0:T(8,128)S(1)} %bitcast.35, f32[640,4096]{1,0:T(8,128)S(1)} %get-tuple-element.198, f32[4096]{0:T(1024)S(1)} %select_maximum_fusion.2, s32[4096]{0:T(1024)S(1)} %fusion.61, s32[640]{0:T(1024)S(1)} %add.168, pred[640]{0:T(1024)(128)(4,1)S(1)} %and.155, pred[640]{0:T(1024)(128)(4,1)S(1)} %or.44, ...), kind=kOutput, calls=%fused_computation.9.clone.1 | convolution fusion | flops 2708996096 | bytes 27973632 | tf_op jit(solution)/shard_map/while/body/eval_jaxpr/dot_general | solution.py:50
  297.2 3.2 %copy-done.1 = f32[4096,512]{1,0:T(8,128)} copy-done((f32[4096,512]{1,0:T(8,128)}, f32[4096,512]{1,0:T(8,128)S(1)}, u32[]{:S(2)}) %copy-start.1) | copy-done | bytes 8388632 | tf_op jit(solution)/shard_map/while
  300.4 5.2 %divide_convert_fusion = bf16[4096,512]{1,0:T(8,128)(2,1)} fusion(f32[4096,512]{1,0:T(8,128)} %get-tuple-element.68, f32[4096]{0:T(1024)S(1)} %get-tuple-element.69), kind=kLoop, calls=%fused_computation.39 | loop fusion | flops 4194304 | bytes 12599296 | tf_op jit(solution)/shard_map/convert_element_type | solution.py:147
  (104 shorter events, 2.9 us)
Async XLA Ops:
  6.5 107.3 %copy-start = (bf16[1,64,7168]{2,1,0:T(8,128)(2,1)S(1)}, bf16[1,64,7168]{2,1,0:T(8,128)(2,1)}, u32[]{:S(2)}) copy-start(bf16[1,64,7168]{2,1,0:T(8,128)(2,1)} %param.10) | copy-start | bytes 2752516
  6.5 107.3 %all-gather.3.cloned.1.call-start = ((), (), s32[]{:S(2)}) async-start(), calls=%async_computation.1 | async-start | bytes 9461760 | tf_op jit(solution)/shard_map/all_gather | solution.py:108
  12.5 9.7 %all-to-all-start = ((bf16[8,2,1,576]{3,1,2,0:T(2,128)(2,1)}), bf16[8,2,1,576]{3,1,2,0:T(2,128)(2,1)S(1)}, u32[]{:S(2)}, u32[]{:S(2)}) async-start(bf16[8,2,1,576]{3,1,2,0:T(2,128)(2,1)} %broadcast_select_fusion.1), calls=%async_computation | async-start | bytes 40960 | tf_op jit(solution)/shard_map/all_to_all | solution.py:91
  16.8 181.3 %all-gather.5.cloned.1.call-start = ((), (), s32[]{:S(2)}) async-start(), calls=%async_computation.2 | async-start | bytes 3379200 | tf_op jit(solution)/shard_map/all_gather | solution.py:117
  22.2 97.5 %copy-start.2 = (f32[512]{0:T(512)S(1)}, f32[512]{0:T(512)}, u32[]{:S(2)}) copy-start(f32[512]{0:T(512)} %param.12) | copy-start | bytes 6148
  199.7 13.5 %slice-start = ((s8[8388608]{0:T(1024)(128)(4,1)}), s8[4194304]{0:T(1024)(128)(4,1)S(1)}, s32[]{:S(2)}) async-start(s8[8388608]{0:T(1024)(128)(4,1)} %bitcast.34), calls=%async_computation.3 | async-start | bytes 8388608 | tf_op jit(solution)/shard_map/while
  201.1 12.1 %slice-start.1 = ((s8[8388608]{0:T(1024)(128)(4,1)}), s8[4194304]{0:T(1024)(128)(4,1)S(1)}, s32[]{:S(2)}) async-start(s8[8388608]{0:T(1024)(128)(4,1)} %bitcast.34), calls=%async_computation.4 | async-start | bytes 8388608 | tf_op jit(solution)/shard_map/while
  220.5 3.2 %copy-start.1 = (f32[4096,512]{1,0:T(8,128)}, f32[4096,512]{1,0:T(8,128)S(1)}, u32[]{:S(2)}) copy-start(f32[4096,512]{1,0:T(8,128)S(1)} %fusion.65) | copy-start | bytes 25165828 | tf_op jit(solution)/shard_map/while
  225.3 13.5 %slice-start = ((s8[8388608]{0:T(1024)(128)(4,1)}), s8[4194304]{0:T(1024)(128)(4,1)S(1)}, s32[]{:S(2)}) async-start(s8[8388608]{0:T(1024)(128)(4,1)} %bitcast.34), calls=%async_computation.3 | async-start | bytes 8388608 | tf_op jit(solution)/shard_map/while
  226.7 12.1 %slice-start.1 = ((s8[8388608]{0:T(1024)(128)(4,1)}), s8[4194304]{0:T(1024)(128)(4,1)S(1)}, s32[]{:S(2)}) async-start(s8[8388608]{0:T(1024)(128)(4,1)} %bitcast.34), calls=%async_computation.4 | async-start | bytes 8388608 | tf_op jit(solution)/shard_map/while
  246.1 3.2 %copy-start.1 = (f32[4096,512]{1,0:T(8,128)}, f32[4096,512]{1,0:T(8,128)S(1)}, u32[]{:S(2)}) copy-start(f32[4096,512]{1,0:T(8,128)S(1)} %fusion.65) | copy-start | bytes 25165828 | tf_op jit(solution)/shard_map/while
  250.9 13.5 %slice-start = ((s8[8388608]{0:T(1024)(128)(4,1)}), s8[4194304]{0:T(1024)(128)(4,1)S(1)}, s32[]{:S(2)}) async-start(s8[8388608]{0:T(1024)(128)(4,1)} %bitcast.34), calls=%async_computation.3 | async-start | bytes 8388608 | tf_op jit(solution)/shard_map/while
  252.3 12.1 %slice-start.1 = ((s8[8388608]{0:T(1024)(128)(4,1)}), s8[4194304]{0:T(1024)(128)(4,1)S(1)}, s32[]{:S(2)}) async-start(s8[8388608]{0:T(1024)(128)(4,1)} %bitcast.34), calls=%async_computation.4 | async-start | bytes 8388608 | tf_op jit(solution)/shard_map/while
  271.6 3.2 %copy-start.1 = (f32[4096,512]{1,0:T(8,128)}, f32[4096,512]{1,0:T(8,128)S(1)}, u32[]{:S(2)}) copy-start(f32[4096,512]{1,0:T(8,128)S(1)} %fusion.65) | copy-start | bytes 25165828 | tf_op jit(solution)/shard_map/while
  276.5 13.5 %slice-start = ((s8[8388608]{0:T(1024)(128)(4,1)}), s8[4194304]{0:T(1024)(128)(4,1)S(1)}, s32[]{:S(2)}) async-start(s8[8388608]{0:T(1024)(128)(4,1)} %bitcast.34), calls=%async_computation.3 | async-start | bytes 8388608 | tf_op jit(solution)/shard_map/while
  277.9 12.1 %slice-start.1 = ((s8[8388608]{0:T(1024)(128)(4,1)}), s8[4194304]{0:T(1024)(128)(4,1)S(1)}, s32[]{:S(2)}) async-start(s8[8388608]{0:T(1024)(128)(4,1)} %bitcast.34), calls=%async_computation.4 | async-start | bytes 8388608 | tf_op jit(solution)/shard_map/while
  297.2 3.2 %copy-start.1 = (f32[4096,512]{1,0:T(8,128)}, f32[4096,512]{1,0:T(8,128)S(1)}, u32[]{:S(2)}) copy-start(f32[4096,512]{1,0:T(8,128)S(1)} %fusion.65) | copy-start | bytes 25165828 | tf_op jit(solution)/shard_map/while
Sparse Core Ops, SparseCore 0:
  9.9 103.8 all-gather.2
  120.7 77.3 all-gather.4
where the time goes:
time: 314 us; the launch traced here: 312 us
  waiting for transfers between devices  172 us (55%)
  matrix products  64.3 us (20%)
  other arithmetic  30.9 us (10%)
  local copies, waits for them, and re-layouts  26.1 us (8%)
  between operations  14.2 us (5%)
  starting transfers between devices  4.34 us (1%)
    all_gather x1, waiting for transfers between devices, shards(): lax.all_gather(kv_down, 'ctx', axis=0, tiled=True)  91.6 us
    all_gather x1, waiting for transfers between devices, shards(): gathered = lax.all_gather(key_block, 'ctx', axis=0, tiled=True)  76.3 us
    dot_general x4, matrix products, absorb(): lax.dot_general(key_rows, query_rows, (((1,), (1,)), ((), ())), preferred...  30.1 us
    dot_general x4, matrix products, absorb(): lax.dot_general(weights.astype(jnp.bfloat16), key_rows[:, :value_width],...  29 us
    reduce_sum x4, other arithmetic, absorb(): total = running_total * factor + jnp.sum(weights, axis=0)  18 us
    while x28, local copies, waits for them, and re-layouts  12.8 us
  transfers between devices with their start and end apart: 3, of which 3 were waited for; matrix products, arithmetic and copies ran while one was open for 2% of the time, Pallas kernels for 0%

commit v1 on v0

v1 whole, which is shorter than its diff:
```python
import functools
import math

import jax
import jax.numpy as jnp
from jax import lax
from jax.experimental import pallas as pl
from jax.experimental.pallas import tpu as pltpu
from jax.sharding import PartitionSpec as P

PAGE = 32
CAP = 2
score_scale = 192.0 ** (-0.5)
rope_base = 10000.0
norm_eps = 1e-06
exp2_scale = score_scale * math.log2(math.e)
masked = -1e30

REQ, Y, Z = 8, 4, 8
SLICE = 32
WORKERS = 7
TOK = 64
HEADS = 64
LAT = 576
VAL = 512
AUG = LAT + TOK

Z_GROUPS = [[y * Z + z for z in range(Z)] for y in range(Y)]
X_GROUPS = [[2 * x + core for x in range(REQ // 2)] for core in range(2)]


def y_shift(d):
    return [(i, (i + Z * d) % (Y * Z)) for i in range(Y * Z)]


def mm(a, b):
    return jnp.dot(a, b, preferred_element_type=jnp.float32)


def partial_kernel(info, h_ref, *refs):
    kv_refs, (keep_ref, give_ref) = refs[:Y], refs[Y:]
    y, core = info[0], info[1]
    for half, out in ((core, keep_ref), (1 - core, give_ref)):
        total = None
        for d in range(Y):
            at = pl.multiple_of(lax.rem(y + Y - d, Y) * (Z * SLICE), Z * SLICE)
            rows = [h_ref[2 * j + half, :, pl.ds(at, Z * SLICE)] for j in range(REQ // 2)]
            term = mm(jnp.concatenate(rows, 0), kv_refs[d][...])
            total = term if total is None else total + term
        out[...] = total.reshape(out.shape)


def partial_latents(info, hidden, kvs):
    shape = jax.ShapeDtypeStruct((REQ // 2, TOK, LAT), jnp.float32)
    vmem = pl.BlockSpec(memory_space=pltpu.VMEM)
    return pl.pallas_call(
        partial_kernel,
        in_specs=[pl.BlockSpec(memory_space=pltpu.SMEM)] + [vmem] * (1 + Y),
        out_specs=[vmem, vmem],
        out_shape=[shape, shape],
        compiler_params=pltpu.CompilerParams(vmem_limit_bytes=24 * 2**20),
        name="partial_latents",
    )(info, hidden, *kvs)


def finish_kernel(parts_ref, gain_ref, cos_ref, sin_ref, out_ref):
    latent = parts_ref[0]
    for x in range(1, REQ // 2):
        latent = latent + parts_ref[x]
    compressed = latent[:, :VAL]
    mean_square = jnp.mean(compressed * compressed, axis=1, keepdims=True)
    normed = compressed * lax.rsqrt(mean_square + norm_eps) * gain_ref[...]
    half = (LAT - VAL) // 2
    first, second = latent[:, VAL : VAL + half], latent[:, VAL + half :]
    cosine, sine = cos_ref[...], sin_ref[...]
    keys = jnp.concatenate(
        [normed, first * cosine - second * sine, second * cosine + first * sine], 1
    ).astype(jnp.bfloat16)
    for z in range(Z):
        out_ref[z] = keys


def finish_keys(parts, gain, cosine, sine):
    vmem = pl.BlockSpec(memory_space=pltpu.VMEM)
    return pl.pallas_call(
        finish_kernel,
        in_specs=[vmem] * 4,
        out_specs=vmem,
        out_shape=jax.ShapeDtypeStruct((Z, TOK, LAT), jnp.bfloat16),
        name="finish_keys",
    )(parts, gain, cosine, sine)


def attend_kernel(sub, blocks, bias_of, carry, final, info, *refs):
    q_ref, ahead_ref = refs[:2]
    refs = refs[2:]
    if carry:
        acc_ref, stat_ref = refs[:2]
        refs = refs[2:]
    k_refs, refs = refs[:blocks], refs[blocks:]
    outs, (kt, s_even, s_odd) = refs[:-3], refs[-3:]
    step = pl.program_id(0)
    tile = q_ref.shape[0]
    subs = tile // sub
    scores = (s_even, s_odd)

    def product(rows, row0):
        token = (row0 + lax.broadcasted_iota(jnp.int32, (sub, TOK), 0)) // HEADS
        place = lax.broadcasted_iota(jnp.int32, (sub, TOK), 1)
        mark = jnp.where(token == place, 1.0, 0.0).astype(jnp.bfloat16)
        return mm(jnp.concatenate([rows, mark], 1), kt[...])

    @pl.when(step == 0)
    def prepare():
        at = 0
        for n, k in enumerate(k_refs):
            size = k.shape[0]
            kt[:LAT, at : at + size] = k[...].T
            kt[LAT:, at : at + size] = bias_of(info, n, size).astype(jnp.bfloat16)
            at += size
        s_even[...] = product(q_ref[:sub, :], 0)

    for s in range(subs):
        here, later = scores[s % 2], scores[(s + 1) % 2]
        if s + 1 < subs:
            rows = q_ref[(s + 1) * sub : (s + 2) * sub, :]
        else:
            rows = ahead_ref[...]
        later[...] = product(rows, step * tile + (s + 1) * sub)
        at = slice(s * sub, (s + 1) * sub)
        score = here[...]
        peak = jnp.max(score, axis=1, keepdims=True)
        if carry:
            stat = stat_ref[at, :]
            old_peak, old_total = stat[:, :1], stat[:, 64:65]
            peak = jnp.maximum(peak, old_peak)
        shift = peak * exp2_scale
        weights = jnp.exp2(score * exp2_scale - shift)
        total = jnp.sum(weights, axis=1, keepdims=True)
        rounded = weights.astype(jnp.bfloat16)
        accum, place = None, 0
        for k in k_refs:
            size = k.shape[0]
            term = mm(rounded[:, place : place + size], k[:, :VAL])
            accum = term if accum is None else accum + term
            place += size
        if carry:
            factor = jnp.exp2(old_peak * exp2_scale - shift)
            total = total + old_total * factor
            accum = accum + acc_ref[at, :] * factor
        if final:
            outs[0][at, :] = (accum / total).astype(jnp.bfloat16)
        else:
            outs[0][at, :] = accum
            outs[1][at, :] = jnp.concatenate(
                [jnp.broadcast_to(peak, (sub, 64)), jnp.broadcast_to(total, (sub, 64))], 1
            )


def attend(info, queries, carry, keys, bias_of, final, tile=1024, sub=256):
    rows = queries.shape[0]
    steps, subs = rows // tile, tile // sub
    total = sum(k.shape[0] for k in keys)
    row = lambda width: pl.BlockSpec((tile, width), lambda i, s: (i, 0))
    ahead = pl.BlockSpec((sub, LAT), lambda i, s: (jnp.minimum((i + 1) * subs, rows // sub - 1), 0))
    whole = lambda a: pl.BlockSpec(a.shape, lambda i, s: (0, 0))
    carry = [] if carry is None else list(carry)
    if final:
        shapes = [jax.ShapeDtypeStruct((rows, VAL), jnp.bfloat16)]
        out_specs = [row(VAL)]
    else:
        shapes = [
            jax.ShapeDtypeStruct((rows, VAL), jnp.float32),
            jax.ShapeDtypeStruct((rows, 128), jnp.float32),
        ]
        out_specs = [row(VAL), row(128)]
    return pl.pallas_call(
        functools.partial(attend_kernel, sub, len(keys), bias_of, bool(carry), final),
        grid_spec=pltpu.PrefetchScalarGridSpec(
            num_scalar_prefetch=1,
            grid=(steps,),
            in_specs=[row(LAT), ahead]
            + [row(VAL), row(128)][: len(carry)]
            + [whole(k) for k in keys],
            out_specs=out_specs,
            scratch_shapes=[
                pltpu.VMEM((AUG, total), jnp.bfloat16),
                pltpu.VMEM((sub, total), jnp.float32),
                pltpu.VMEM((sub, total), jnp.float32),
            ],
        ),
        out_shape=shapes,
        compiler_params=pltpu.CompilerParams(vmem_limit_bytes=44 * 2**20),
        cost_estimate=pl.CostEstimate(
            flops=2 * rows * total * (LAT + VAL),
            bytes_accessed=rows * 2048,
            transcendentals=rows * total,
        ),
        name="attend_last" if final else "attend_first",
    )(info, queries, queries, *carry, *keys)


def near_bias(info, n, size):
    key = lax.broadcasted_iota(jnp.int32, (TOK, size), 1)
    token = lax.broadcasted_iota(jnp.int32, (TOK, size), 0)
    if n == 0:
        allowed = lax.rem(key, 8) < info[2]
    else:
        allowed = key <= info[1] * TOK + token
    return jnp.where(allowed, 0.0, masked)


def far_bias(info, n, size):
    bias = jnp.where(info[0] >= n + 1, 0.0, masked)
    return jnp.full((TOK, size), bias, jnp.float32)


def shards(suffix_hidden, kv_down, kv_gain, queries, pool, hit_holder, hit_slot, hit_count):
    req = lax.axis_index("req")
    ctx = lax.axis_index("ctx")
    y, z = ctx // Z, ctx % Z
    count = lax.dynamic_index_in_dim(hit_count, req, 0, keepdims=False)

    hidden = suffix_hidden[0].reshape(TOK, Y * Z, WORKERS, SLICE)
    hidden = hidden.transpose(2, 0, 1, 3).reshape(WORKERS, TOK, Y * Z * SLICE)
    hidden = jnp.concatenate([hidden, jnp.zeros((REQ - WORKERS,) + hidden.shape[1:], hidden.dtype)], 0)
    hidden = lax.all_to_all(hidden, "req", 0, 0)

    piece = lax.dynamic_slice(
        kv_down, (jnp.minimum(req, WORKERS - 1) * SLICE, 0), (SLICE, LAT)
    )
    row = lax.all_to_all(
        jnp.broadcast_to(piece[None], (Z, SLICE, LAT)), "ctx", 0, 0, axis_index_groups=Z_GROUPS
    ).reshape(Z * SLICE, LAT)
    kvs = [row] + [lax.ppermute(row, "ctx", y_shift(d)) for d in (1, 2, 3)]

    keep, give = partial_latents(jnp.stack([y, req % 2]), hidden, kvs)
    swapped = lax.ppermute(give, "req", [(i, i ^ 1) for i in range(REQ)])
    parts = lax.all_to_all(keep + swapped, "req", 0, 0, axis_index_groups=X_GROUPS)

    half = (LAT - VAL) // 2
    steps = jnp.arange(half, dtype=jnp.float32) * (2.0 / (LAT - VAL))
    freqs = jnp.exp(-steps * jnp.log(rope_base))
    first = count * PAGE + ctx * TOK
    positions = (first + jnp.arange(TOK, dtype=jnp.int32)).astype(jnp.float32)
    angles = positions[:, None] * freqs[None, :]
    fresh = finish_keys(parts, kv_gain[None], jnp.cos(angles), jnp.sin(angles))

    entries = jnp.arange(hit_holder.shape[1], dtype=jnp.int32)
    used = entries[None, :] < hit_count[:, None]
    earlier = (
        (hit_holder[:, :, None] == hit_holder[:, None, :])
        & used[:, None, :]
        & (entries[None, None, :] < entries[None, :, None])
    )
    rank = jnp.sum(earlier.astype(jnp.int32), axis=2)
    cap_ids = jnp.arange(CAP, dtype=jnp.int32)
    pick = (
        used[:, None, :]
        & (hit_holder[:, None, :] == req)
        & (rank[:, None, :] == cap_ids[None, :, None])
    )
    place = jnp.sum(jnp.where(pick, hit_slot[:, None, :], 0), axis=2)
    outgoing = jnp.take(pool[:, 0], place.reshape(-1), axis=0).reshape(REQ, CAP, LAT)
    incoming = lax.all_to_all(outgoing, "req", 0, 0).reshape(REQ * CAP, LAT)
    holder = lax.dynamic_index_in_dim(hit_holder, req, 0, keepdims=False)
    my_rank = lax.dynamic_index_in_dim(rank, req, 0, keepdims=False)
    cached = jnp.take(incoming, holder * CAP + jnp.minimum(my_rank, CAP - 1), axis=0)
    cached, kvs[3] = lax.optimization_barrier((cached, kvs[3]))
    cached = lax.all_to_all(
        jnp.broadcast_to(cached[None], (Y * Z,) + cached.shape), "ctx", 0, 0
    ).reshape(-1, LAT)

    near = lax.all_to_all(fresh, "ctx", 0, 0, axis_index_groups=Z_GROUPS).reshape(-1, LAT)
    far = [lax.ppermute(near, "ctx", y_shift(d)) for d in (1, 2, 3)]

    info = jnp.stack([y, z, count]).astype(jnp.int32)
    rows = queries[0].reshape(-1, LAT)
    carry = attend(info, rows, None, [cached, near], near_bias, False)
    (out,) = attend(info, rows, carry, far, far_bias, True)
    return out.reshape(1, TOK, HEADS, VAL)


def solution(mesh):
    in_specs = (
        P("req", "ctx", None),
        P("ctx", None),
        P(),
        P("req", "ctx", None, None),
        P("req", "ctx", None),
        P(),
        P(),
        P(),
    )
    out_specs = P("req", "ctx", None, None)
    return jax.shard_map(shards, mesh=mesh, in_specs=in_specs, out_specs=out_specs, check_vma=False)
```

time: 314 us -> 172 us (0.55)
  the two profiles are of different devices: /device:TPU:8 before, /device:TPU:1 now
where the time goes in v1:
time: 172 us; the launch traced here: 171 us
  waiting for transfers between devices  61.9 us (36%)
  starting transfers between devices  41.8 us (24%)
  Pallas kernels  41.6 us (24%)
  local copies, waits for them, and re-layouts  20.9 us (12%)
  other arithmetic  3.78 us (2%)
    pallas_call x2, Pallas kernels, attend(): pl.pallas_call(functools.partial(attend_kernel, sub, len(keys), bias_of,...  37.1 us
    all_to_all x1, waiting for transfers between devices, shards(): lax.all_to_all(fresh, 'ctx', 0, 0, axis_index_groups=Z_GROUPS)  19.9 us
    ppermute x3, waiting for transfers between devices, shards(): kvs = [row] + [lax.ppermute(row, 'ctx', y_shift(d)) for d in (1, 2, 3)]  12.3 us
    unnamed x21, local copies, waits for them, and re-layouts  11.4 us
    all_to_all x1, waiting for transfers between devices, shards(): lax.all_to_all(keep + swapped, 'req', 0, 0, axis_index_groups=X_GROUPS)  9.95 us
    all_to_all x1, starting transfers between devices, shards(): lax.all_to_all(jnp.broadcast_to(piece[None], (Z, SLICE, LAT)), 'ctx', 0,...  9.01 us
    all_to_all x1, starting transfers between devices, shards(): hidden = lax.all_to_all(hidden, 'req', 0, 0)  6.61 us
    ppermute x3, waiting for transfers between devices, shards(): far = [lax.ppermute(near, 'ctx', y_shift(d)) for d in (1, 2, 3)]  6.53 us
  transfers between devices with their start and end apart: 13, of which 9 were waited for; matrix products, arithmetic and copies ran while one was open for 8% of the time, Pallas kernels for 9%

profile of v1, /device:TPU:1, one launch (start us, length us, event | category | flops | bytes accessed | tf_op | source)
XLA Modules:
  0.0 170.8 jit_solution(15624644275850676159)
XLA Ops:
  0.0 1.0 copy-done
  1.0 0.8 broadcast_in_dim.68
  1.7 9.0 %all-to-all-start.1 = ((bf16[8,32,576]{2,1,0:T(8,128)(2,1)}), bf16[8,32,576]{2,1,0:T(8,128)(2,1)S(1)}, u32[]{:S(2)}, u32[]{:S(2)}) async-start(bf16[8,32,576]{2,1,0:T(8,128)(2,1)} %broadcast_in_dim.68), calls=%async_computation.1 | async-start | bytes 655360 | tf_op jit(solution)/shard_map/all_to_all | solution.py:232
  10.7 2.6 %copy.24 = bf16[1,64,7168]{1,2,0:T(8,128)(2,1)} copy(bf16[1,64,7168]{2,1,0:T(8,128)(2,1)} %param.8) | data formatting | bytes 1835008 | tf_op args[0]
  13.3 1.9 %copy.25 = bf16[7,64,32,32]{1,3,2,0:T(8,128)(2,1)S(1)} copy(bf16[7,64,32,32]{1,3,0,2:T(8,128)(2,1)} %bitcast.35) | data formatting | bytes 1835008 | tf_op jit(solution)/shard_map/transpose | solution.py:225
  15.2 0.8 copy.26
  16.0 1.1 concatenate.3
  17.1 5.6 %all-to-all-done.1 = bf16[8,32,576]{2,1,0:T(8,128)(2,1)S(1)} async-done(((bf16[8,32,576]{2,1,0:T(8,128)(2,1)}), bf16[8,32,576]{2,1,0:T(8,128)(2,1)S(1)}, u32[]{:S(2)}, u32[]{:S(2)}) %all-to-all-start.1) | async-done | bytes 294944 | tf_op jit(solution)/shard_map/all_to_all | solution.py:232
  22.7 6.6 %all-to-all-start.3 = ((bf16[8,64,1024]{2,1,0:T(8,128)(2,1)}), bf16[8,64,1024]{2,1,0:T(8,128)(2,1)S(1)}, u32[]{:S(2)}, u32[]{:S(2)}) async-start(bf16[8,64,1024]{2,1,0:T(8,128)(2,1)} %concatenate.3), calls=%async_computation.3 | async-start | bytes 2097152 | tf_op jit(solution)/shard_map/all_to_all | solution.py:227
  29.3 2.9 %collective-permute-start.2 = (bf16[256,576]{1,0:T(8,128)(2,1)S(1)}, bf16[256,576]{1,0:T(8,128)(2,1)S(1)}, u32[]{:S(2)}, u32[]{:S(2)}) collective-permute-start(bf16[256,576]{1,0:T(8,128)(2,1)S(1)} %bitcast.25), channel_id=1, source_target_pairs={{0,16},{1,17},{2,18},{3,19},{4,20},{5,21},{6,22},{7,23},{8,24},{9,... | collective-permute-start | bytes 884744 | tf_op jit(solution)/shard_map/ppermute | solution.py:235
  32.3 0.4 collective-permute-start.1
  32.7 2.3 %collective-permute-start = (bf16[256,576]{1,0:T(8,128)(2,1)S(1)}, bf16[256,576]{1,0:T(8,128)(2,1)S(1)}, u32[]{:S(2)}, u32[]{:S(2)}) collective-permute-start(bf16[256,576]{1,0:T(8,128)(2,1)S(1)} %bitcast.27), channel_id=1, source_target_pairs={{0,24},{1,25},{2,26},{3,27},{4,28},{5,29},{6,30},{7,31},{8,0},{9,1... | collective-permute-start | bytes 884744 | tf_op jit(solution)/shard_map/ppermute | solution.py:235
  35.0 0.3 convert_reduce_fusion
  35.3 4.9 %collective-permute-done.2.refs_2_ = bf16[256,576]{1,0:T(8,128)(2,1)S(1)} collective-permute-done((bf16[256,576]{1,0:T(8,128)(2,1)S(1)}, bf16[256,576]{1,0:T(8,128)(2,1)S(1)}, u32[]{:S(2)}, u32[]{:S(2)}) %collective-permute-start.2) | collective-permute-done | bytes 294944 | tf_op jit(solution)/shard_map/ppermute | solution.py:235
  40.3 7.3 %collective-permute-done.1.refs_1_ = bf16[256,576]{1,0:T(8,128)(2,1)S(1)} collective-permute-done((bf16[256,576]{1,0:T(8,128)(2,1)S(1)}, bf16[256,576]{1,0:T(8,128)(2,1)S(1)}, u32[]{:S(2)}, u32[]{:S(2)}) %collective-permute-start.1) | collective-permute-done | bytes 294944 | tf_op jit(solution)/shard_map/ppermute | solution.py:235
  47.6 2.4 %partial_latents.1 = (f32[4,64,576]{2,1,0:T(8,128)S(1)}, f32[4,64,576]{2,1,0:T(8,128)}) custom-call(s32[2]{0:T(128)S(1)} %pad_add_fusion.1.info, bf16[8,64,1024]{2,1,0:T(8,128)(2,1)S(1)} %all-to-all-done.3.h_ref, bf16[256,576]{1,0:T(8,128)(2,1)S(1)} %bitcast.28, bf16[256,576]{1,0:T(8,128)(2,1)S(1)} %collective-permute-done.1.refs_1_, ...), custom_call_target="tpu_custom_call" | custom-call | tf_op jit(solution)/shard_map/partial_latents/pallas_call | solution.py:56
  50.0 0.8 collective-permute-start.3
  50.9 0.6 dynamic_slice.14
  51.8 0.6 gather_fusion
  53.0 0.9 add.96
  53.9 4.2 %all-to-all-start.4 = ((f32[4,64,576]{2,1,0:T(8,128)}), f32[4,64,576]{2,1,0:T(8,128)S(1)}, u32[]{:S(2)}, u32[]{:S(2)}) async-start(f32[4,64,576]{2,1,0:T(8,128)} %add.96), calls=%async_computation.4 | async-start | bytes 1310720 | tf_op jit(solution)/shard_map/all_to_all | solution.py:239
  58.1 0.7 broadcast_select_fusion
  58.8 9.9 %all-to-all-done.4.parts_ref = f32[4,64,576]{2,1,0:T(8,128)S(1)} async-done(((f32[4,64,576]{2,1,0:T(8,128)}), f32[4,64,576]{2,1,0:T(8,128)S(1)}, u32[]{:S(2)}, u32[]{:S(2)}) %all-to-all-start.4) | async-done | bytes 589856 | tf_op jit(solution)/shard_map/all_to_all | solution.py:239
  68.8 4.4 %all-to-all-start = ((bf16[8,2,576]{2,1,0:T(2,128)(2,1)}), bf16[8,2,576]{2,1,0:T(2,128)(2,1)S(1)}, u32[]{:S(2)}, u32[]{:S(2)}) async-start(bf16[8,2,576]{2,1,0:T(2,128)(2,1)} %broadcast_select_fusion), calls=%async_computation | async-start | bytes 40960 | tf_op jit(solution)/shard_map/all_to_all | solution.py:265
  73.2 0.8 multiply_sine_fusion
  74.0 2.1 %finish_keys.1 = bf16[8,64,576]{2,1,0:T(8,128)(2,1)} custom-call(f32[4,64,576]{2,1,0:T(8,128)} %copy-done.5, f32[1,512]{1,0:T(1,128)} %bitcast.37, f32[64,32]{1,0:T(8,128)} %get-tuple-element.18.cos_ref, f32[64,32]{1,0:T(8,128)} %get-tuple-element.17.sin_ref), custom_call_target="tpu_custom_call" | custom-call | tf_op jit(solution)/shard_map/finish_keys/pallas_call | solution.py:85
  76.1 1.7 %all-to-all-done = bf16[8,2,576]{2,1,0:T(2,128)(2,1)S(1)} async-done(((bf16[8,2,576]{2,1,0:T(2,128)(2,1)}), bf16[8,2,576]{2,1,0:T(2,128)(2,1)S(1)}, u32[]{:S(2)}, u32[]{:S(2)}) %all-to-all-start) | async-done | bytes 18464 | tf_op jit(solution)/shard_map/all_to_all | solution.py:265
  77.8 3.5 %all-to-all-start.5 = ((bf16[8,64,576]{2,1,0:T(8,128)(2,1)}), bf16[8,64,576]{2,1,0:T(8,128)(2,1)S(1)}, u32[]{:S(2)}, u32[]{:S(2)}) async-start(bf16[8,64,576]{2,1,0:T(8,128)(2,1)} %finish_keys.1), calls=%async_computation.5 | async-start | bytes 1310720 | tf_op jit(solution)/shard_map/all_to_all | solution.py:274
  81.5 0.6 gather_fusion.1
  82.1 19.9 %all-to-all-done.5 = bf16[8,64,576]{2,1,0:T(8,128)(2,1)S(1)} async-done(((bf16[8,64,576]{2,1,0:T(8,128)(2,1)}), bf16[8,64,576]{2,1,0:T(8,128)(2,1)S(1)}, u32[]{:S(2)}, u32[]{:S(2)}) %all-to-all-start.5) | async-done | bytes 589856 | tf_op jit(solution)/shard_map/all_to_all | solution.py:274
  102.1 0.8 broadcast_in_dim.69
  102.8 4.0 %all-to-all-start.2 = ((bf16[32,8,576]{2,1,0:T(8,128)(2,1)}), bf16[32,8,576]{2,1,0:T(8,128)(2,1)S(1)}, u32[]{:S(2)}, u32[]{:S(2)}) async-start(bf16[32,8,576]{2,1,0:T(8,128)(2,1)} %broadcast_in_dim.69), calls=%async_computation.2 | async-start | bytes 655360 | tf_op jit(solution)/shard_map/all_to_all | solution.py:270
  106.9 0.6 pad_add_fusion.info
  107.5 0.3 copy.27
  107.8 2.6 %collective-permute-start.6 = (bf16[512,576]{0,1:T(8,128)(2,1)S(1)}, bf16[512,576]{0,1:T(8,128)(2,1)}, u32[]{:S(2)}, u32[]{:S(2)}) collective-permute-start(bf16[512,576]{0,1:T(8,128)(2,1)S(1)} %copy.27), channel_id=1, source_target_pairs={{0,24},{1,25},{2,26},{3,27},{4,28},{5,29},{6,30},{7,31},{8,0},{9,1... | collective-permute-start | bytes 1769480 | tf_op jit(solution)/shard_map/ppermute | solution.py:275
  110.3 0.5 collective-permute-start.5
  110.9 0.6 collective-permute-start.4
  111.4 5.9 %all-to-all-done.2 = bf16[32,8,576]{2,1,0:T(8,128)(2,1)S(1)} async-done(((bf16[32,8,576]{2,1,0:T(8,128)(2,1)}), bf16[32,8,576]{2,1,0:T(8,128)(2,1)S(1)}, u32[]{:S(2)}, u32[]{:S(2)}) %all-to-all-start.2) | async-done | bytes 294944 | tf_op jit(solution)/shard_map/all_to_all | solution.py:270
  117.3 2.5 %copy-done.1 = bf16[1,64,64,576]{3,2,1,0:T(8,128)(2,1)S(1)} copy-done((bf16[1,64,64,576]{3,2,1,0:T(8,128)(2,1)S(1)}, bf16[1,64,64,576]{3,2,1,0:T(8,128)(2,1)}, u32[]{:S(2)}) %copy-start.1) | copy-done | bytes 4718616
  119.8 12.8 %attend_first.1 = (f32[4096,512]{1,0:T(8,128)}, f32[4096,128]{1,0:T(8,128)S(1)}) custom-call(s32[3]{0:T(128)S(1)} %pad_add_fusion.info, bf16[4096,576]{1,0:T(8,128)(2,1)S(1)} %bitcast.30, bf16[4096,576]{1,0:T(8,128)(2,1)S(1)} %bitcast.31, bf16[256,576]{1,0:T(8,128)(2,1)S(1)} %bitcast.29, bf16[512,576]{1,0:T(8,128)(2,1)S(1)} %bitcast.24), custom_call_target="tpu_custom_call" | custom-call | flops 6845104128 | bytes 8388608 | tf_op jit(solution)/shard_map/attend_first/pallas_call | solution.py:177
  132.6 1.3 copy-done.3
  133.9 1.4 copy.32.refs_6_
  135.3 0.3 copy.31.refs_5_
  135.6 6.5 %collective-permute-done.4 = bf16[512,576]{0,1:T(8,128)(2,1)S(1)} collective-permute-done((bf16[512,576]{0,1:T(8,128)(2,1)S(1)}, bf16[512,576]{0,1:T(8,128)(2,1)S(1)}, u32[]{:S(2)}, u32[]{:S(2)}) %collective-permute-start.4) | collective-permute-done | bytes 589856 | tf_op jit(solution)/shard_map/ppermute | solution.py:275
  142.1 0.3 copy.30.refs_4_
  142.5 2.5 %copy-done.2 = bf16[1,64,64,576]{3,2,1,0:T(8,128)(2,1)S(1)} copy-done((bf16[1,64,64,576]{3,2,1,0:T(8,128)(2,1)S(1)}, bf16[1,64,64,576]{3,2,1,0:T(8,128)(2,1)}, u32[]{:S(2)}) %copy-start.2) | copy-done | bytes 4718616
  144.9 1.6 copy-done.4
  146.5 24.3 %attend_last.1 = bf16[4096,512]{1,0:T(8,128)(2,1)} custom-call(s32[3]{0:T(128)S(1)} %pad_add_fusion.info, bf16[4096,576]{1,0:T(8,128)(2,1)S(1)} %bitcast.32, bf16[4096,576]{1,0:T(8,128)(2,1)S(1)} %bitcast.33, f32[4096,512]{1,0:T(8,128)} %get-tuple-element.13.refs_2_, f32[4096,128]{1,0:T(8,128)S(1)} %copy-done.4, bf16[512,576]{1,0:T(8,128)(2,1)S(1)} %copy.30.refs_4_, ...), custom_call_target="tpu_custom_call" | custom-call | flops 13690208256 | bytes 8388608 | tf_op jit(solution)/shard_map/attend_last/pallas_call | solution.py:177
  (38 shorter events, 0.9 us)
Async XLA Ops:
  0.0 1.0 copy-start
  1.7 20.9 %all-to-all-start.1 = ((bf16[8,32,576]{2,1,0:T(8,128)(2,1)}), bf16[8,32,576]{2,1,0:T(8,128)(2,1)S(1)}, u32[]{:S(2)}, u32[]{:S(2)}) async-start(bf16[8,32,576]{2,1,0:T(8,128)(2,1)} %broadcast_in_dim.68), calls=%async_computation.1 | async-start | bytes 655360 | tf_op jit(solution)/shard_map/all_to_all | solution.py:232
  15.2 19.8 %copy-start.7 = (s32[8,8]{1,0:T(8,128)S(1)}, s32[8,8]{1,0:T(8,128)}, u32[]{:S(2)}) copy-start(s32[8,8]{1,0:T(8,128)} %param.13) | copy-start | bytes 772
  15.2 19.8 %copy-start.9 = (s32[8]{0:T(128)S(1)}, s32[8]{0:T(128)}, u32[]{:S(2)}) copy-start(s32[8]{0:T(128)} %param.15) | copy-start | bytes 100
  15.2 35.6 %copy-start.8 = (s32[8,8]{1,0:T(8,128)S(1)}, s32[8,8]{1,0:T(8,128)}, u32[]{:S(2)}) copy-start(s32[8,8]{1,0:T(8,128)} %param.14) | copy-start | bytes 772
  15.2 36.6 %copy-start.6 = (bf16[12,1,576]{2,0,1:T(8,128)(2,1)S(1)}, bf16[12,1,576]{2,0,1:T(8,128)(2,1)}, u32[]{:S(2)}) copy-start(bf16[12,1,576]{2,0,1:T(8,128)(2,1)} %param.12) | copy-start | bytes 41476
  22.7 25.0 %all-to-all-start.3 = ((bf16[8,64,1024]{2,1,0:T(8,128)(2,1)}), bf16[8,64,1024]{2,1,0:T(8,128)(2,1)S(1)}, u32[]{:S(2)}, u32[]{:S(2)}) async-start(bf16[8,64,1024]{2,1,0:T(8,128)(2,1)} %concatenate.3), calls=%async_computation.3 | async-start | bytes 2097152 | tf_op jit(solution)/shard_map/all_to_all | solution.py:227
  29.3 10.9 %collective-permute-start.2 = (bf16[256,576]{1,0:T(8,128)(2,1)S(1)}, bf16[256,576]{1,0:T(8,128)(2,1)S(1)}, u32[]{:S(2)}, u32[]{:S(2)}) collective-permute-start(bf16[256,576]{1,0:T(8,128)(2,1)S(1)} %bitcast.25), channel_id=1, source_target_pairs={{0,16},{1,17},{2,18},{3,19},{4,20},{5,21},{6,22},{7,23},{8,24},{9,... | collective-permute-start | bytes 884744 | tf_op jit(solution)/shard_map/ppermute | solution.py:235
  32.3 15.3 %collective-permute-start.1 = (bf16[256,576]{1,0:T(8,128)(2,1)S(1)}, bf16[256,576]{1,0:T(8,128)(2,1)S(1)}, u32[]{:S(2)}, u32[]{:S(2)}) collective-permute-start(bf16[256,576]{1,0:T(8,128)(2,1)S(1)} %bitcast.26), channel_id=1, source_target_pairs={{0,8},{1,9},{2,10},{3,11},{4,12},{5,13},{6,14},{7,15},{8,16},{9,17... | collective-permute-start | bytes 884744 | tf_op jit(solution)/shard_map/ppermute | solution.py:235
  32.7 14.9 %collective-permute-start = (bf16[256,576]{1,0:T(8,128)(2,1)S(1)}, bf16[256,576]{1,0:T(8,128)(2,1)S(1)}, u32[]{:S(2)}, u32[]{:S(2)}) collective-permute-start(bf16[256,576]{1,0:T(8,128)(2,1)S(1)} %bitcast.27), channel_id=1, source_target_pairs={{0,24},{1,25},{2,26},{3,27},{4,28},{5,29},{6,30},{7,31},{8,0},{9,1... | collective-permute-start | bytes 884744 | tf_op jit(solution)/shard_map/ppermute | solution.py:235
  50.0 3.0 %collective-permute-start.3 = (f32[4,64,576]{2,1,0:T(8,128)}, f32[4,64,576]{2,1,0:T(8,128)S(1)}, u32[]{:S(2)}, u32[]{:S(2)}) collective-permute-start(f32[4,64,576]{2,1,0:T(8,128)} %get-tuple-element.12), channel_id=1, source_target_pairs={{0,32},{32,0},{64,96},{96,64},{128,160},{160,128},{192,224},{224,1... | collective-permute-start | bytes 1769480 | tf_op jit(solution)/shard_map/ppermute | solution.py:238
  53.9 14.8 %all-to-all-start.4 = ((f32[4,64,576]{2,1,0:T(8,128)}), f32[4,64,576]{2,1,0:T(8,128)S(1)}, u32[]{:S(2)}, u32[]{:S(2)}) async-start(f32[4,64,576]{2,1,0:T(8,128)} %add.96), calls=%async_computation.4 | async-start | bytes 1310720 | tf_op jit(solution)/shard_map/all_to_all | solution.py:239
  68.8 5.2 %copy-start.5 = (f32[4,64,576]{2,1,0:T(8,128)}, f32[4,64,576]{2,1,0:T(8,128)S(1)}, u32[]{:S(2)}) copy-start(f32[4,64,576]{2,1,0:T(8,128)S(1)} %all-to-all-done.4.parts_ref) | copy-start | bytes 1769476
  68.8 9.1 %all-to-all-start = ((bf16[8,2,576]{2,1,0:T(2,128)(2,1)}), bf16[8,2,576]{2,1,0:T(2,128)(2,1)S(1)}, u32[]{:S(2)}, u32[]{:S(2)}) async-start(bf16[8,2,576]{2,1,0:T(2,128)(2,1)} %broadcast_select_fusion), calls=%async_computation | async-start | bytes 40960 | tf_op jit(solution)/shard_map/all_to_all | solution.py:265
  77.8 24.2 %all-to-all-start.5 = ((bf16[8,64,576]{2,1,0:T(8,128)(2,1)}), bf16[8,64,576]{2,1,0:T(8,128)(2,1)S(1)}, u32[]{:S(2)}, u32[]{:S(2)}) async-start(bf16[8,64,576]{2,1,0:T(8,128)(2,1)} %finish_keys.1), calls=%async_computation.5 | async-start | bytes 1310720 | tf_op jit(solution)/shard_map/all_to_all | solution.py:274
  102.8 14.5 %all-to-all-start.2 = ((bf16[32,8,576]{2,1,0:T(8,128)(2,1)}), bf16[32,8,576]{2,1,0:T(8,128)(2,1)S(1)}, u32[]{:S(2)}, u32[]{:S(2)}) async-start(bf16[32,8,576]{2,1,0:T(8,128)(2,1)} %broadcast_in_dim.69), calls=%async_computation.2 | async-start | bytes 655360 | tf_op jit(solution)/shard_map/all_to_all | solution.py:270
  107.8 26.2 %collective-permute-start.6 = (bf16[512,576]{0,1:T(8,128)(2,1)S(1)}, bf16[512,576]{0,1:T(8,128)(2,1)}, u32[]{:S(2)}, u32[]{:S(2)}) collective-permute-start(bf16[512,576]{0,1:T(8,128)(2,1)S(1)} %copy.27), channel_id=1, source_target_pairs={{0,24},{1,25},{2,26},{3,27},{4,28},{5,29},{6,30},{7,31},{8,0},{9,1... | collective-permute-start | bytes 1769480 | tf_op jit(solution)/shard_map/ppermute | solution.py:275
  110.3 25.0 %collective-permute-start.5 = (bf16[512,576]{0,1:T(8,128)(2,1)S(1)}, bf16[512,576]{0,1:T(8,128)(2,1)S(1)}, u32[]{:S(2)}, u32[]{:S(2)}) collective-permute-start(bf16[512,576]{0,1:T(8,128)(2,1)S(1)} %copy.27), channel_id=1, source_target_pairs={{0,16},{1,17},{2,18},{3,19},{4,20},{5,21},{6,22},{7,23},{8,24},{9,... | collective-permute-start | bytes 1769480 | tf_op jit(solution)/shard_map/ppermute | solution.py:275
  110.9 31.3 %collective-permute-start.4 = (bf16[512,576]{0,1:T(8,128)(2,1)S(1)}, bf16[512,576]{0,1:T(8,128)(2,1)S(1)}, u32[]{:S(2)}, u32[]{:S(2)}) collective-permute-start(bf16[512,576]{0,1:T(8,128)(2,1)S(1)} %copy.27), channel_id=1, source_target_pairs={{0,8},{1,9},{2,10},{3,11},{4,12},{5,13},{6,14},{7,15},{8,16},{9,17... | collective-permute-start | bytes 1769480 | tf_op jit(solution)/shard_map/ppermute | solution.py:275
  117.3 2.5 %copy-start.1 = (bf16[1,64,64,576]{3,2,1,0:T(8,128)(2,1)S(1)}, bf16[1,64,64,576]{3,2,1,0:T(8,128)(2,1)}, u32[]{:S(2)}) copy-start(bf16[1,64,64,576]{3,2,1,0:T(8,128)(2,1)} %param.11) | copy-start | bytes 14155780
  132.6 1.3 copy-start.3
  142.4 2.5 %copy-start.2 = (bf16[1,64,64,576]{3,2,1,0:T(8,128)(2,1)S(1)}, bf16[1,64,64,576]{3,2,1,0:T(8,128)(2,1)}, u32[]{:S(2)}) copy-start(bf16[1,64,64,576]{3,2,1,0:T(8,128)(2,1)} %param.11) | copy-start | bytes 14155780
  144.9 1.6 copy-start.4

commit v2 on v1

v2 whole, which is shorter than its diff:
```python
import functools
import math

import jax
import jax.numpy as jnp
from jax import lax
from jax.experimental import pallas as pl
from jax.experimental.pallas import tpu as pltpu
from jax.sharding import PartitionSpec as P

PAGE = 32
CAP = 2
score_scale = 192.0 ** (-0.5)
rope_base = 10000.0
norm_eps = 1e-06
exp2_scale = score_scale * math.log2(math.e)
masked = -1e30

REQ, X, Y, Z = 8, 4, 4, 8
SLICE = 32
WORKERS = 7
TOK = 64
HEADS = 64
LAT = 576
VAL = 512
AUG = 640
DEVICE_LANE, PAGE_LANE = LAT, LAT + Y * Z

Z_GROUPS = [[y * Z + z for z in range(Z)] for y in range(Y)]


def y_shift(d):
    return [(i, (i + Z * d) % (Y * Z)) for i in range(Y * Z)]


def mm(a, b):
    return jnp.dot(a, b, preferred_element_type=jnp.float32)


def cut_kernel(info, h_ref, *refs):
    out_refs, staged = refs[:X], refs[X]
    x = info[0]
    per = 4
    half = Y * Z * SLICE
    staged[x ^ (X - 1), :, half:] = jnp.zeros((TOK, half), jnp.bfloat16)
    for u in range(Y * Z // per):
        base = u * per * WORKERS * SLICE
        block = h_ref[:, base : base + per * WORKERS * SLICE]
        for r in range(WORKERS):
            pieces = [
                block[:, (a * WORKERS + r) * SLICE : (a * WORKERS + r + 1) * SLICE] for a in range(per)
            ]
            at = (r % 2) * half + u * 128
            staged[x ^ (r // 2), :, at : at + 128] = jnp.concatenate(pieces, 1)
    for m in range(X):
        out_refs[m][...] = staged[m]


def cut_hidden(info, hidden):
    vmem = pl.BlockSpec(memory_space=pltpu.VMEM)
    part = (TOK, 2 * Y * Z * SLICE)
    return pl.pallas_call(
        cut_kernel,
        in_specs=[pl.BlockSpec(memory_space=pltpu.SMEM), vmem],
        out_specs=[vmem] * X,
        out_shape=[jax.ShapeDtypeStruct(part, jnp.bfloat16)] * X,
        scratch_shapes=[pltpu.VMEM((X,) + part, jnp.bfloat16)],
        cost_estimate=pl.CostEstimate(flops=2**34, bytes_accessed=2**24, transcendentals=0),
        name="cut_hidden",
    )(info, hidden)


def partial_kernel(info, *refs):
    h_refs, refs = refs[:X], refs[X:]
    own_refs, other_refs, out_refs = refs[:Y], refs[Y : 2 * Y], refs[2 * Y :]
    total = None
    for d in range(Y):
        for core, kv_ref in ((info[1], own_refs[d]), (1 - info[1], other_refs[d])):
            at = core * (Y * Z * SLICE) + lax.rem(info[0] + Y - d, Y) * (Z * SLICE)
            at = pl.multiple_of(at, Z * SLICE)
            rows = [h[:, pl.ds(at, Z * SLICE)] for h in h_refs]
            term = mm(jnp.concatenate(rows, 0), kv_ref[...])
            total = term if total is None else total + term
    for m in range(X):
        out_refs[m][...] = total[m * TOK : (m + 1) * TOK]


def partial_latents(info, hidden, own, other):
    vmem = pl.BlockSpec(memory_space=pltpu.VMEM)
    return pl.pallas_call(
        partial_kernel,
        in_specs=[pl.BlockSpec(memory_space=pltpu.SMEM)] + [vmem] * (X + 2 * Y),
        out_specs=[vmem] * X,
        out_shape=[jax.ShapeDtypeStruct((TOK, LAT), jnp.float32)] * X,
        compiler_params=pltpu.CompilerParams(vmem_limit_bytes=24 * 2**20),
        name="partial_latents",
    )(info, *hidden, *own, *other)


def finish_kernel(info, a_ref, b_ref, c_ref, d_ref, gain_ref, cos_ref, sin_ref, out_ref):
    latent = (a_ref[...] + b_ref[...]) + (c_ref[...] + d_ref[...])
    compressed = latent[:, :VAL]
    mean_square = jnp.mean(compressed * compressed, axis=1, keepdims=True)
    normed = compressed * lax.rsqrt(mean_square + norm_eps) * gain_ref[...]
    half = (LAT - VAL) // 2
    first, second = latent[:, VAL : VAL + half], latent[:, VAL + half :]
    cosine, sine = cos_ref[...], sin_ref[...]
    lane = lax.broadcasted_iota(jnp.int32, (TOK, AUG - LAT), 1)
    origin = jnp.where(lane == info[0], 1.0, 0.0)
    keys = jnp.concatenate(
        [normed, first * cosine - second * sine, second * cosine + first * sine, origin], 1
    ).astype(jnp.bfloat16)
    for z in range(Z):
        out_ref[z] = keys


def finish_keys(info, parts, gain, cosine, sine):
    vmem = pl.BlockSpec(memory_space=pltpu.VMEM)
    return pl.pallas_call(
        finish_kernel,
        in_specs=[pl.BlockSpec(memory_space=pltpu.SMEM)] + [vmem] * 7,
        out_specs=vmem,
        out_shape=jax.ShapeDtypeStruct((Z, TOK, AUG), jnp.bfloat16),
        name="finish_keys",
    )(info, *parts, gain, cosine, sine)


def lanes(x, n):
    return jnp.concatenate([x] * n, 1) if n > 1 else x


def attend_kernel(sub, blocks, causal, carry, final, info, *refs):
    q_ref, refs = refs[0], refs[1:]
    if carry:
        acc_ref, peak_ref, total_ref = refs[:3]
        refs = refs[3:]
    k_refs, outs = refs[:blocks], refs[blocks:]
    step = pl.program_id(0)
    subs = q_ref.shape[0] // sub
    tokens = sub // HEADS

    lane = lax.broadcasted_iota(jnp.int32, (sub, AUG - LAT), 1)
    out_of_reach = (lane > info[0]) & (lane < PAGE_LANE - LAT) | (
        (lane >= PAGE_LANE - LAT + info[1]) & (lane < PAGE_LANE - LAT + 8)
    )
    marks = jnp.where(out_of_reach, masked, 0.0).astype(jnp.bfloat16)

    def product(s):
        rows = jnp.concatenate([q_ref[s * sub : (s + 1) * sub, :], marks], 1)
        return [
            lax.dot_general(rows, k[...], (((1,), (1,)), ((), ())), preferred_element_type=jnp.float32)
            for k in k_refs
        ]

    ahead = product(0)
    for s in range(subs):
        scores = ahead
        if s + 1 < subs:
            ahead = product(s + 1)
        at = slice(s * sub, (s + 1) * sub)
        if causal:
            size = k_refs[0].shape[0]
            key = lax.broadcasted_iota(jnp.int32, (tokens, 1, size), 2)
            token = lax.broadcasted_iota(jnp.int32, (tokens, 1, size), 0)
            token = token + lax.rem(info[0], Z) * TOK + (step * subs + s) * tokens
            bias = jnp.where(key <= token, 0.0, masked)
            scores[0] = (scores[0].reshape(tokens, HEADS, size) + bias).reshape(sub, size)
        peak = None
        for score in scores:
            for j in range(0, score.shape[1], 128):
                part = score[:, j : j + 128]
                peak = part if peak is None else jnp.maximum(peak, part)
        peak = jnp.broadcast_to(jnp.max(peak, axis=1, keepdims=True), (sub, 128))
        if carry:
            peak = jnp.maximum(peak, peak_ref[at, :])
        shift = peak * exp2_scale
        total, accum = None, None
        for score, k in zip(scores, k_refs):
            count = score.shape[1] // 128
            weights = jnp.exp2(score * exp2_scale - lanes(shift, count))
            for j in range(count):
                part = weights[:, j * 128 : (j + 1) * 128]
                total = part if total is None else total + part
            term = mm(weights.astype(jnp.bfloat16), k[:, :VAL])
            accum = term if accum is None else accum + term
        if carry:
            factor = jnp.exp2(peak_ref[at, :] * exp2_scale - shift)
            total = total + total_ref[at, :] * factor
            accum = accum + acc_ref[at, :] * lanes(factor, VAL // 128)
        if final:
            outs[0][at, :] = (accum / jnp.sum(total, axis=1, keepdims=True)).astype(jnp.bfloat16)
        else:
            outs[0][at, :] = accum
            outs[1][at, :] = peak
            outs[2][at, :] = total


def attend(info, queries, carry, keys, causal, final, tile=512, sub=256):
    rows = queries.shape[0]
    row = lambda width: pl.BlockSpec((tile, width), lambda i, s: (i, 0))
    whole = lambda a: pl.BlockSpec(a.shape, lambda i, s: (0, 0))
    carry = [] if carry is None else list(carry)
    carry = [pltpu.with_memory_space_constraint(a, pltpu.VMEM) for a in carry]
    total = sum(k.shape[0] for k in keys)
    state = (VAL, 128, 128)
    if final:
        shapes = [jax.ShapeDtypeStruct((rows, VAL), jnp.bfloat16)]
        out_specs = [row(VAL)]
    else:
        shapes = [pltpu.VMEM((rows, width), jnp.float32) for width in state]
        out_specs = [row(width) for width in state]
    return pl.pallas_call(
        functools.partial(attend_kernel, sub, len(keys), causal, bool(carry), final),
        grid_spec=pltpu.PrefetchScalarGridSpec(
            num_scalar_prefetch=1,
            grid=(rows // tile,),
            in_specs=[row(LAT)]
            + [row(width) for width in state][: len(carry)]
            + [whole(k) for k in keys],
            out_specs=out_specs,
        ),
        out_shape=shapes,
        compiler_params=pltpu.CompilerParams(vmem_limit_bytes=20 * 2**20),
        cost_estimate=pl.CostEstimate(
            flops=2 * rows * total * (LAT + VAL),
            bytes_accessed=rows * 2048,
            transcendentals=rows * total,
        ),
        name="attend_last" if final else "attend_first",
    )(info, queries, *carry, *keys)


def shards(suffix_hidden, kv_down, kv_gain, queries, pool, hit_holder, hit_slot, hit_count):
    req = lax.axis_index("req").astype(jnp.int32)
    ctx = lax.axis_index("ctx").astype(jnp.int32)
    y, z = ctx // Z, ctx % Z
    count = lax.dynamic_index_in_dim(hit_count, req, 0, keepdims=False)

    piece = lax.dynamic_slice(
        kv_down, (jnp.minimum(req, WORKERS - 1) * SLICE, 0), (SLICE, LAT)
    )
    row = lax.all_to_all(
        jnp.broadcast_to(piece[None], (Z, SLICE, LAT)), "ctx", 0, 0, axis_index_groups=Z_GROUPS
    ).reshape(Z * SLICE, LAT)

    parts = cut_hidden((req // 2)[None], suffix_hidden[0])
    hidden = [parts[0]] + [
        lax.ppermute(parts[m], "req", [(i, i ^ (2 * m)) for i in range(REQ)]) for m in range(1, X)
    ]

    pool, row = lax.optimization_barrier((pool, row))
    own = [row] + [lax.ppermute(row, "ctx", y_shift(d)) for d in (1, 2, 3)]
    other = [lax.ppermute(o, "req", [(i, i ^ 1) for i in range(REQ)]) for o in own]

    sums = list(partial_latents(jnp.stack([y, req % 2]), hidden, own, other))
    sums = sums[:1] + [
        lax.ppermute(sums[m], "req", [(i, i ^ (2 * m)) for i in range(REQ)]) for m in range(1, X)
    ]

    half = (LAT - VAL) // 2
    steps = jnp.arange(half, dtype=jnp.float32) * (2.0 / (LAT - VAL))
    freqs = jnp.exp(-steps * jnp.log(rope_base))
    first = count * PAGE + ctx * TOK
    positions = (first + jnp.arange(TOK, dtype=jnp.int32)).astype(jnp.float32)
    angles = positions[:, None] * freqs[None, :]
    entries = jnp.arange(hit_holder.shape[1], dtype=jnp.int32)
    used = entries[None, :] < hit_count[:, None]
    earlier = (
        (hit_holder[:, :, None] == hit_holder[:, None, :])
        & used[:, None, :]
        & (entries[None, None, :] < entries[None, :, None])
    )
    rank = jnp.sum(earlier.astype(jnp.int32), axis=2)
    cap_ids = jnp.arange(CAP, dtype=jnp.int32)
    pick = (
        used[:, None, :]
        & (hit_holder[:, None, :] == req)
        & (rank[:, None, :] == cap_ids[None, :, None])
    )
    place = jnp.sum(jnp.where(pick, hit_slot[:, None, :], 0), axis=2)
    outgoing = jnp.take(pool[:, 0], place.reshape(-1), axis=0).reshape(REQ, CAP, LAT)
    incoming = lax.all_to_all(outgoing, "req", 0, 0).reshape(REQ * CAP, LAT)
    holder = lax.dynamic_index_in_dim(hit_holder, req, 0, keepdims=False)
    my_rank = lax.dynamic_index_in_dim(rank, req, 0, keepdims=False)
    cached = jnp.take(incoming, holder * CAP + jnp.minimum(my_rank, CAP - 1), axis=0)
    tags = jnp.broadcast_to(
        jnp.eye(8, AUG - LAT, PAGE_LANE - LAT, dtype=cached.dtype), (8, AUG - LAT)
    )
    cached = jnp.concatenate([cached, tags], 1)
    cached, sums[0] = lax.optimization_barrier((cached, sums[0]))
    cached = lax.all_to_all(
        jnp.broadcast_to(cached[None], (Y * Z,) + cached.shape), "ctx", 0, 0
    ).reshape(-1, AUG)

    fresh = finish_keys(ctx[None], sums, kv_gain[None], jnp.cos(angles), jnp.sin(angles))
    fresh, cached = lax.optimization_barrier((fresh, cached))
    near = lax.all_to_all(fresh, "ctx", 0, 0, axis_index_groups=Z_GROUPS).reshape(-1, AUG)

    far = [lax.ppermute(near, "ctx", y_shift(d)) for d in (1, 3)]

    info = jnp.stack([ctx, count]).astype(jnp.int32)
    rows = queries[0].reshape(-1, LAT)
    carry = attend(info, rows, None, [near, cached], True, False)
    far, near = lax.optimization_barrier((far, near))
    last = lax.ppermute(near, "ctx", y_shift(2))
    carry = attend(info, rows, carry, far, False, False)
    (out,) = attend(info, rows, carry, [last], False, True)
    return out.reshape(1, TOK, HEADS, VAL)


def solution(mesh):
    in_specs = (
        P("req", "ctx", None),
        P("ctx", None),
        P(),
        P("req", "ctx", None, None),
        P("req", "ctx", None),
        P(),
        P(),
        P(),
    )
    out_specs = P("req", "ctx", None, None)
    return jax.shard_map(shards, mesh=mesh, in_specs=in_specs, out_specs=out_specs, check_vma=False)
```

time: 172 us -> 145 us (0.84)
  the two profiles are of different devices: /device:TPU:1 before, /device:TPU:8 now
where the time goes in v2:
time: 145 us; the launch traced here: 144 us
  Pallas kernels  43.5 us (30%)
  starting transfers between devices  38.7 us (27%)
  blocking collectives  25.6 us (18%)
  waiting for transfers between devices  23.1 us (16%)
  local copies, waits for them, and re-layouts  9.3 us (6%)
  other arithmetic  3 us (2%)
    pallas_call x3, Pallas kernels, attend(): pl.pallas_call(functools.partial(attend_kernel, sub, len(keys), causal, b...  36.9 us
    all_to_all x1, blocking collectives, shards(): lax.all_to_all(fresh, 'ctx', 0, 0, axis_index_groups=Z_GROUPS)  25.6 us
    all_to_all x1, starting transfers between devices, shards(): lax.all_to_all(jnp.broadcast_to(piece[None], (Z, SLICE, LAT)), 'ctx', 0,...  8.47 us
    ppermute x3, waiting for transfers between devices, shards(): lax.ppermute(parts[m], 'req', [(i, i ^ 2 * m) for i in range(REQ)])  7.07 us
    unnamed x22, local copies, waits for them, and re-layouts  5.76 us
    ppermute x3, waiting for transfers between devices, shards(): lax.ppermute(sums[m], 'req', [(i, i ^ 2 * m) for i in range(REQ)])  5.53 us
    ppermute x3, starting transfers between devices, shards(): lax.ppermute(parts[m], 'req', [(i, i ^ 2 * m) for i in range(REQ)])  5.47 us
    all_to_all x1, waiting for transfers between devices, shards(): incoming = lax.all_to_all(outgoing, 'req', 0, 0).reshape(REQ * CAP, LAT)  5.31 us
  transfers between devices with their start and end apart: 19, of which 6 were waited for; matrix products, arithmetic and copies ran while one was open for 3% of the time, Pallas kernels for 23%

profile of v2, /device:TPU:8, one launch (start us, length us, event | category | flops | bytes accessed | tf_op | source)
XLA Modules:
  0.0 144.0 jit_solution(6407933101151176669)
XLA Ops:
  0.0 1.0 copy-done
  1.0 0.8 broadcast_in_dim.44
  1.7 8.5 %all-to-all-start = ((bf16[8,32,576]{2,1,0:T(8,128)(2,1)}), bf16[8,32,576]{2,1,0:T(8,128)(2,1)S(1)}, u32[]{:S(2)}, u32[]{:S(2)}) async-start(bf16[8,32,576]{2,1,0:T(8,128)(2,1)} %broadcast_in_dim.44), calls=%async_computation | async-start | bytes 655360 | tf_op jit(solution)/shard_map/all_to_all | solution.py:242
  10.2 2.9 %cut_hidden.1 = (bf16[64,2048]{1,0:T(8,128)(2,1)}, bf16[64,2048]{1,0:T(8,128)(2,1)}, bf16[64,2048]{1,0:T(8,128)(2,1)}, bf16[64,2048]{1,0:T(8,128)(2,1)}) custom-call(s32[1]{0:T(128)} %bitcast.10.info, bf16[64,7168]{1,0:T(8,128)(2,1)} %bitcast.36), custom_call_target="tpu_custom_call" | custom-call | flops 17179869184 | bytes 16777216 | tf_op jit(solution)/shard_map/cut_hidden/pallas_call | solution.py:62
  13.1 1.5 %collective-permute-start = (bf16[64,2048]{1,0:T(8,128)(2,1)}, bf16[64,2048]{1,0:T(8,128)(2,1)S(1)}, u32[]{:S(2)}, u32[]{:S(2)}) collective-permute-start(bf16[64,2048]{1,0:T(8,128)(2,1)} %get-tuple-element.30), channel_id=1, source_target_pairs={{0,64},{32,96},{64,0},{96,32},{128,192},{160,224},{192,128},{224,1... | collective-permute-start | bytes 786440 | tf_op jit(solution)/shard_map/ppermute | solution.py:248
  14.6 2.7 %collective-permute-start.1 = (bf16[64,2048]{1,0:T(8,128)(2,1)}, bf16[64,2048]{1,0:T(8,128)(2,1)S(1)}, u32[]{:S(2)}, u32[]{:S(2)}) collective-permute-start(bf16[64,2048]{1,0:T(8,128)(2,1)} %get-tuple-element.31), channel_id=1, source_target_pairs={{0,128},{32,160},{64,192},{96,224},{128,0},{160,32},{192,64},{224,... | collective-permute-start | bytes 786440 | tf_op jit(solution)/shard_map/ppermute | solution.py:248
  17.4 0.3 convert_reduce_fusion
  17.7 0.1 select_reduce_fusion
  17.9 0.1 copy.10
  18.0 0.1 copy.9
  18.3 5.2 %all-to-all-done = bf16[8,32,576]{2,1,0:T(8,128)(2,1)S(1)} async-done(((bf16[8,32,576]{2,1,0:T(8,128)(2,1)}), bf16[8,32,576]{2,1,0:T(8,128)(2,1)S(1)}, u32[]{:S(2)}, u32[]{:S(2)}) %all-to-all-start) | async-done | bytes 294944 | tf_op jit(solution)/shard_map/all_to_all | solution.py:242
  23.5 0.4 collective-permute-start.5
  23.9 2.6 %collective-permute-start.4 = (bf16[256,576]{1,0:T(8,128)(2,1)S(1)}, bf16[256,576]{1,0:T(8,128)(2,1)S(1)}, u32[]{:S(2)}, u32[]{:S(2)}) collective-permute-start(bf16[256,576]{1,0:T(8,128)(2,1)S(1)} %bitcast.25), channel_id=1, source_target_pairs={{0,16},{1,17},{2,18},{3,19},{4,20},{5,21},{6,22},{7,23},{8,24},{9,... | collective-permute-start | bytes 884744 | tf_op jit(solution)/shard_map/ppermute | solution.py:252
  26.5 1.9 %collective-permute-start.3 = (bf16[256,576]{1,0:T(8,128)(2,1)S(1)}, bf16[256,576]{1,0:T(8,128)(2,1)S(1)}, u32[]{:S(2)}, u32[]{:S(2)}) collective-permute-start(bf16[256,576]{1,0:T(8,128)(2,1)S(1)} %bitcast.26), channel_id=1, source_target_pairs={{0,8},{1,9},{2,10},{3,11},{4,12},{5,13},{6,14},{7,15},{8,16},{9,17... | collective-permute-start | bytes 884744 | tf_op jit(solution)/shard_map/ppermute | solution.py:252
  28.4 0.6 gather_fusion
  29.0 0.7 broadcast_select_fusion
  29.7 4.3 %all-to-all-start.1 = ((bf16[8,2,576]{2,1,0:T(2,128)(2,1)}), bf16[8,2,576]{2,1,0:T(2,128)(2,1)S(1)}, u32[]{:S(2)}, u32[]{:S(2)}) async-start(bf16[8,2,576]{2,1,0:T(2,128)(2,1)} %broadcast_select_fusion), calls=%async_computation.1 | async-start | bytes 40960 | tf_op jit(solution)/shard_map/all_to_all | solution.py:282
  34.1 5.3 %all-to-all-done.1 = bf16[8,2,576]{2,1,0:T(2,128)(2,1)S(1)} async-done(((bf16[8,2,576]{2,1,0:T(2,128)(2,1)}), bf16[8,2,576]{2,1,0:T(2,128)(2,1)S(1)}, u32[]{:S(2)}, u32[]{:S(2)}) %all-to-all-start.1) | async-done | bytes 18464 | tf_op jit(solution)/shard_map/all_to_all | solution.py:282
  39.4 0.6 gather_fusion.1
  40.0 1.3 collective-permute-start.2
  41.3 0.5 collective-permute-start.9
  41.8 0.1 collective-permute-start.8
  41.9 0.4 collective-permute-start.7
  42.4 7.1 %collective-permute-done.2.refs_3_ = bf16[64,2048]{1,0:T(8,128)(2,1)S(1)} collective-permute-done((bf16[64,2048]{1,0:T(8,128)(2,1)}, bf16[64,2048]{1,0:T(8,128)(2,1)S(1)}, u32[]{:S(2)}, u32[]{:S(2)}) %collective-permute-start.2) | collective-permute-done | bytes 262176 | tf_op jit(solution)/shard_map/ppermute | solution.py:248
  49.5 0.9 copy-done.2
  50.5 1.5 %partial_latents.1 = (f32[64,576]{1,0:T(8,128)S(1)}, f32[64,576]{1,0:T(8,128)S(1)}, f32[64,576]{1,0:T(8,128)S(1)}, f32[64,576]{1,0:T(8,128)S(1)}) custom-call(s32[2]{0:T(128)S(1)} %pad_add_fusion.1.info, bf16[64,2048]{1,0:T(8,128)(2,1)S(1)} %copy-done.2, bf16[64,2048]{1,0:T(8,128)(2,1)S(1)} %collective-permute-done.refs_1_, ...), custom_call_target="tpu_custom_call" | custom-call | tf_op jit(solution)/shard_map/partial_latents/pallas_call | solution.py:90
  52.0 0.7 copy-done.3
  52.7 0.8 broadcast_in_dim.74
  53.5 4.1 %all-to-all-start.2 = ((bf16[32,8,640]{2,1,0:T(8,128)(2,1)}), bf16[32,8,640]{2,1,0:T(8,128)(2,1)S(1)}, u32[]{:S(2)}, u32[]{:S(2)}) async-start(bf16[32,8,640]{2,1,0:T(8,128)(2,1)} %broadcast_in_dim.74), calls=%async_computation.2 | async-start | bytes 655360 | tf_op jit(solution)/shard_map/all_to_all | solution.py:291
  57.6 0.6 dynamic_slice.14
  58.7 0.1 collective-permute-start.10
  58.8 2.6 %collective-permute-start.11 = (f32[64,576]{1,0:T(8,128)S(1)}, f32[64,576]{1,0:T(8,128)S(1)}, u32[]{:S(2)}, u32[]{:S(2)}) collective-permute-start(f32[64,576]{1,0:T(8,128)S(1)} %get-tuple-element.37), channel_id=1, source_target_pairs={{0,128},{32,160},{64,192},{96,224},{128,0},{160,32},{192,64},{224,... | collective-permute-start | bytes 442376 | tf_op jit(solution)/shard_map/ppermute | solution.py:257
  61.5 2.1 %collective-permute-start.12 = (f32[64,576]{1,0:T(8,128)S(1)}, f32[64,576]{1,0:T(8,128)S(1)}, u32[]{:S(2)}, u32[]{:S(2)}) collective-permute-start(f32[64,576]{1,0:T(8,128)S(1)} %get-tuple-element.38), channel_id=1, source_target_pairs={{0,192},{32,224},{64,128},{96,160},{128,64},{160,96},{192,0},{224,... | collective-permute-start | bytes 442376 | tf_op jit(solution)/shard_map/ppermute | solution.py:257
  63.5 0.8 multiply_sine_fusion
  64.3 1.0 collective-permute-done.10.b_ref
  65.4 2.6 %collective-permute-done.11.c_ref = f32[64,576]{1,0:T(8,128)S(1)} collective-permute-done((f32[64,576]{1,0:T(8,128)S(1)}, f32[64,576]{1,0:T(8,128)S(1)}, u32[]{:S(2)}, u32[]{:S(2)}) %collective-permute-start.11) | collective-permute-done | bytes 147488 | tf_op jit(solution)/shard_map/ppermute | solution.py:257
  68.0 1.9 %collective-permute-done.12.d_ref = f32[64,576]{1,0:T(8,128)S(1)} collective-permute-done((f32[64,576]{1,0:T(8,128)S(1)}, f32[64,576]{1,0:T(8,128)S(1)}, u32[]{:S(2)}, u32[]{:S(2)}) %collective-permute-start.12) | collective-permute-done | bytes 147488 | tf_op jit(solution)/shard_map/ppermute | solution.py:257
  69.9 0.7 copy-done.7
  70.6 2.2 %finish_keys.1 = bf16[8,64,640]{2,1,0:T(8,128)(2,1)} custom-call(s32[1]{0:T(128)} %bitcast.info, f32[64,576]{1,0:T(8,128)} %copy-done.3, f32[64,576]{1,0:T(8,128)} %copy-done.5, f32[64,576]{1,0:T(8,128)} %copy-done.6, f32[64,576]{1,0:T(8,128)} %copy-done.7, f32[1,512]{1,0:T(1,128)} %bitcast.35, f32[64,32]{1,0:T(8,128)} %get-tuple-element.54.cos_ref, ...), custom_call_target="tpu_custom_call" | custom-call | tf_op jit(solution)/shard_map/finish_keys/pallas_call | solution.py:119
  72.7 25.6 %all_to_all.20 = bf16[8,64,640]{2,1,0:T(8,128)(2,1)S(1)} all-to-all(bf16[8,64,640]{2,1,0:T(8,128)(2,1)} %finish_keys.1), channel_id=1, replica_groups={{0,1,2,3,4,5,6,7},{8,9,10,11,12,13,14,15},{16,17,18,19,20,21,22,23},{24..., dimensions={0} | all-to-all | bytes 1310720 | tf_op jit(solution)/shard_map/all_to_all | solution.py:297
  98.4 0.4 collective-permute-start.14
  98.8 1.6 %collective-permute-start.13 = (bf16[512,640]{1,0:T(8,128)(2,1)S(1)}, bf16[512,640]{1,0:T(8,128)(2,1)S(1)}, u32[]{:S(2)}, u32[]{:S(2)}) collective-permute-start(bf16[512,640]{1,0:T(8,128)(2,1)S(1)} %bitcast.30), channel_id=1, source_target_pairs={{0,8},{1,9},{2,10},{3,11},{4,12},{5,13},{6,14},{7,15},{8,16},{9,17... | collective-permute-start | bytes 1966088 | tf_op jit(solution)/shard_map/ppermute | solution.py:299
  100.4 0.6 pad_add_fusion.info
  101.0 2.5 %copy-done.1 = bf16[1,64,64,576]{3,2,1,0:T(8,128)(2,1)S(1)} copy-done((bf16[1,64,64,576]{3,2,1,0:T(8,128)(2,1)S(1)}, bf16[1,64,64,576]{3,2,1,0:T(8,128)(2,1)}, u32[]{:S(2)}) %copy-start.1) | copy-done | bytes 4718616
  103.5 11.5 %attend_first.2 = (f32[4096,512]{1,0:T(8,128)S(1)}, f32[4096,128]{1,0:T(8,128)S(1)}, f32[4096,128]{1,0:T(8,128)S(1)}) custom-call(s32[2]{0:T(128)S(1)} %pad_add_fusion.info, bf16[4096,576]{1,0:T(8,128)(2,1)S(1)} %bitcast.21, bf16[512,640]{1,0:T(8,128)(2,1)S(1)} %bitcast.31, bf16[256,640]{1,0:T(8,128)(2,1)S(1)} %bitcast.33), custom_call_target="tpu_custom_call" | custom-call | flops 6845104128 | bytes 8388608 | tf_op jit(solution)/shard_map/attend_first/pallas_call | solution.py:212
  115.0 3.6 %collective-permute-start.15 = (bf16[512,640]{1,0:T(8,128)(2,1)S(1)}, bf16[512,640]{1,0:T(8,128)(2,1)S(1)}, u32[]{:S(2)}, u32[]{:S(2)}) collective-permute-start(bf16[512,640]{1,0:T(8,128)(2,1)S(1)} %bitcast.32), channel_id=1, source_target_pairs={{0,16},{1,17},{2,18},{3,19},{4,20},{5,21},{6,22},{7,23},{8,24},{9,... | collective-permute-start | bytes 1966088 | tf_op jit(solution)/shard_map/ppermute | solution.py:305
  118.6 15.9 %attend_first.3 = (f32[4096,512]{1,0:T(8,128)S(1)}, f32[4096,128]{1,0:T(8,128)S(1)}, f32[4096,128]{1,0:T(8,128)S(1)}) custom-call(s32[2]{0:T(128)S(1)} %pad_add_fusion.info, bf16[4096,576]{1,0:T(8,128)(2,1)S(1)} %bitcast.22, f32[4096,512]{1,0:T(8,128)S(1)} %get-tuple-element.42.refs_1_, f32[4096,128]{1,0:T(8,128)S(1)} %get-tuple-element.43.refs_2_, ...), custom_call_target="tpu_custom_call" | custom-call | flops 9126805504 | bytes 8388608 | tf_op jit(solution)/shard_map/attend_first/pallas_call | solution.py:212
  134.5 9.5 %attend_last.1 = bf16[4096,512]{1,0:T(8,128)(2,1)} custom-call(s32[2]{0:T(128)S(1)} %pad_add_fusion.info, bf16[4096,576]{1,0:T(8,128)(2,1)S(1)} %bitcast.23, f32[4096,512]{1,0:T(8,128)S(1)} %get-tuple-element.47.refs_1_, f32[4096,128]{1,0:T(8,128)S(1)} %get-tuple-element.48.refs_2_, f32[4096,128]{1,0:T(8,128)S(1)} %get-tuple-element.49.refs_3_, ...), custom_call_target="tpu_custom_call" | custom-call | flops 4563402752 | bytes 8388608 | tf_op jit(solution)/shard_map/attend_last/pallas_call | solution.py:212
  (49 shorter events, 0.6 us)
Async XLA Ops:
  0.0 1.0 copy-start
  1.7 21.7 %all-to-all-start = ((bf16[8,32,576]{2,1,0:T(8,128)(2,1)}), bf16[8,32,576]{2,1,0:T(8,128)(2,1)S(1)}, u32[]{:S(2)}, u32[]{:S(2)}) async-start(bf16[8,32,576]{2,1,0:T(8,128)(2,1)} %broadcast_in_dim.44), calls=%async_computation | async-start | bytes 655360 | tf_op jit(solution)/shard_map/all_to_all | solution.py:242
  10.2 7.2 %copy-start.8 = (s32[8,8]{1,0:T(8,128)S(1)}, s32[8,8]{1,0:T(8,128)}, u32[]{:S(2)}) copy-start(s32[8,8]{1,0:T(8,128)} %param.13) | copy-start | bytes 772
  10.2 7.2 %copy-start.10 = (s32[8]{0:T(128)S(1)}, s32[8]{0:T(128)}, u32[]{:S(2)}) copy-start(s32[8]{0:T(128)} %param.15) | copy-start | bytes 100
  10.2 7.5 %copy-start.9 = (s32[8,8]{1,0:T(8,128)S(1)}, s32[8,8]{1,0:T(8,128)}, u32[]{:S(2)}) copy-start(s32[8,8]{1,0:T(8,128)} %param.14) | copy-start | bytes 772
  10.2 18.2 %copy-start.4 = (bf16[12,1,576]{2,0,1:T(8,128)(2,1)S(1)}, bf16[12,1,576]{2,0,1:T(8,128)(2,1)}, u32[]{:S(2)}) copy-start(bf16[12,1,576]{2,0,1:T(8,128)(2,1)} %param.12) | copy-start | bytes 41476
  13.1 26.9 %collective-permute-start = (bf16[64,2048]{1,0:T(8,128)(2,1)}, bf16[64,2048]{1,0:T(8,128)(2,1)S(1)}, u32[]{:S(2)}, u32[]{:S(2)}) collective-permute-start(bf16[64,2048]{1,0:T(8,128)(2,1)} %get-tuple-element.30), channel_id=1, source_target_pairs={{0,64},{32,96},{64,0},{96,32},{128,192},{160,224},{192,128},{224,1... | collective-permute-start | bytes 786440 | tf_op jit(solution)/shard_map/ppermute | solution.py:248
  14.6 26.6 %collective-permute-start.1 = (bf16[64,2048]{1,0:T(8,128)(2,1)}, bf16[64,2048]{1,0:T(8,128)(2,1)S(1)}, u32[]{:S(2)}, u32[]{:S(2)}) collective-permute-start(bf16[64,2048]{1,0:T(8,128)(2,1)} %get-tuple-element.31), channel_id=1, source_target_pairs={{0,128},{32,160},{64,192},{96,224},{128,0},{160,32},{192,64},{224,... | collective-permute-start | bytes 786440 | tf_op jit(solution)/shard_map/ppermute | solution.py:248
  23.5 17.8 %collective-permute-start.5 = (bf16[256,576]{1,0:T(8,128)(2,1)S(1)}, bf16[256,576]{1,0:T(8,128)(2,1)S(1)}, u32[]{:S(2)}, u32[]{:S(2)}) collective-permute-start(bf16[256,576]{1,0:T(8,128)(2,1)S(1)} %bitcast.24), channel_id=1, source_target_pairs={{0,24},{1,25},{2,26},{3,27},{4,28},{5,29},{6,30},{7,31},{8,0},{9,1... | collective-permute-start | bytes 884744 | tf_op jit(solution)/shard_map/ppermute | solution.py:252
  23.9 17.9 %collective-permute-start.4 = (bf16[256,576]{1,0:T(8,128)(2,1)S(1)}, bf16[256,576]{1,0:T(8,128)(2,1)S(1)}, u32[]{:S(2)}, u32[]{:S(2)}) collective-permute-start(bf16[256,576]{1,0:T(8,128)(2,1)S(1)} %bitcast.25), channel_id=1, source_target_pairs={{0,16},{1,17},{2,18},{3,19},{4,20},{5,21},{6,22},{7,23},{8,24},{9,... | collective-permute-start | bytes 884744 | tf_op jit(solution)/shard_map/ppermute | solution.py:252
  26.5 15.4 %collective-permute-start.3 = (bf16[256,576]{1,0:T(8,128)(2,1)S(1)}, bf16[256,576]{1,0:T(8,128)(2,1)S(1)}, u32[]{:S(2)}, u32[]{:S(2)}) collective-permute-start(bf16[256,576]{1,0:T(8,128)(2,1)S(1)} %bitcast.26), channel_id=1, source_target_pairs={{0,8},{1,9},{2,10},{3,11},{4,12},{5,13},{6,14},{7,15},{8,16},{9,17... | collective-permute-start | bytes 884744 | tf_op jit(solution)/shard_map/ppermute | solution.py:252
  29.7 9.7 %all-to-all-start.1 = ((bf16[8,2,576]{2,1,0:T(2,128)(2,1)}), bf16[8,2,576]{2,1,0:T(2,128)(2,1)S(1)}, u32[]{:S(2)}, u32[]{:S(2)}) async-start(bf16[8,2,576]{2,1,0:T(2,128)(2,1)} %broadcast_select_fusion), calls=%async_computation.1 | async-start | bytes 40960 | tf_op jit(solution)/shard_map/all_to_all | solution.py:282
  40.0 9.5 %collective-permute-start.2 = (bf16[64,2048]{1,0:T(8,128)(2,1)}, bf16[64,2048]{1,0:T(8,128)(2,1)S(1)}, u32[]{:S(2)}, u32[]{:S(2)}) collective-permute-start(bf16[64,2048]{1,0:T(8,128)(2,1)} %get-tuple-element.32), channel_id=1, source_target_pairs={{0,192},{32,224},{64,128},{96,160},{128,64},{160,96},{192,0},{224,... | collective-permute-start | bytes 786440 | tf_op jit(solution)/shard_map/ppermute | solution.py:248
  41.3 8.3 %collective-permute-start.6 = (bf16[256,576]{1,0:T(8,128)(2,1)S(1)}, bf16[256,576]{1,0:T(8,128)(2,1)S(1)}, u32[]{:S(2)}, u32[]{:S(2)}) collective-permute-start(bf16[256,576]{1,0:T(8,128)(2,1)S(1)} %bitcast.27), channel_id=1, source_target_pairs={{0,32},{32,0},{64,96},{96,64},{128,160},{160,128},{192,224},{224,1... | collective-permute-start | bytes 884744 | tf_op jit(solution)/shard_map/ppermute | solution.py:253
  41.3 8.3 %collective-permute-start.9 = (bf16[256,576]{1,0:T(8,128)(2,1)S(1)}, bf16[256,576]{1,0:T(8,128)(2,1)S(1)}, u32[]{:S(2)}, u32[]{:S(2)}) collective-permute-start(bf16[256,576]{1,0:T(8,128)(2,1)S(1)} %collective-permute-done.5.refs_7_), channel_id=1, source_target_pairs={{0,32},{32,0},{64,96},{96,64},{128,160},{160,128},{192,224},{224,1... | collective-permute-start | bytes 884744 | tf_op jit(solution)/shard_map/ppermute | solution.py:253
  41.8 7.7 %collective-permute-start.8 = (bf16[256,576]{1,0:T(8,128)(2,1)S(1)}, bf16[256,576]{1,0:T(8,128)(2,1)S(1)}, u32[]{:S(2)}, u32[]{:S(2)}) collective-permute-start(bf16[256,576]{1,0:T(8,128)(2,1)S(1)} %collective-permute-done.4.refs_6_), channel_id=1, source_target_pairs={{0,32},{32,0},{64,96},{96,64},{128,160},{160,128},{192,224},{224,1... | collective-permute-start | bytes 884744 | tf_op jit(solution)/shard_map/ppermute | solution.py:253
  41.9 7.7 %collective-permute-start.7 = (bf16[256,576]{1,0:T(8,128)(2,1)S(1)}, bf16[256,576]{1,0:T(8,128)(2,1)S(1)}, u32[]{:S(2)}, u32[]{:S(2)}) collective-permute-start(bf16[256,576]{1,0:T(8,128)(2,1)S(1)} %collective-permute-done.3.refs_5_), channel_id=1, source_target_pairs={{0,32},{32,0},{64,96},{96,64},{128,160},{160,128},{192,224},{224,1... | collective-permute-start | bytes 884744 | tf_op jit(solution)/shard_map/ppermute | solution.py:253
  49.5 1.0 copy-start.2
  52.0 0.7 copy-start.3
  53.5 19.3 %all-to-all-start.2 = ((bf16[32,8,640]{2,1,0:T(8,128)(2,1)}), bf16[32,8,640]{2,1,0:T(8,128)(2,1)S(1)}, u32[]{:S(2)}, u32[]{:S(2)}) async-start(bf16[32,8,640]{2,1,0:T(8,128)(2,1)} %broadcast_in_dim.74), calls=%async_computation.2 | async-start | bytes 655360 | tf_op jit(solution)/shard_map/all_to_all | solution.py:291
  58.7 6.6 %collective-permute-start.10 = (f32[64,576]{1,0:T(8,128)S(1)}, f32[64,576]{1,0:T(8,128)S(1)}, u32[]{:S(2)}, u32[]{:S(2)}) collective-permute-start(f32[64,576]{1,0:T(8,128)S(1)} %get-tuple-element.36), channel_id=1, source_target_pairs={{0,64},{32,96},{64,0},{96,32},{128,192},{160,224},{192,128},{224,1... | collective-permute-start | bytes 442376 | tf_op jit(solution)/shard_map/ppermute | solution.py:257
  58.8 9.1 %collective-permute-start.11 = (f32[64,576]{1,0:T(8,128)S(1)}, f32[64,576]{1,0:T(8,128)S(1)}, u32[]{:S(2)}, u32[]{:S(2)}) collective-permute-start(f32[64,576]{1,0:T(8,128)S(1)} %get-tuple-element.37), channel_id=1, source_target_pairs={{0,128},{32,160},{64,192},{96,224},{128,0},{160,32},{192,64},{224,... | collective-permute-start | bytes 442376 | tf_op jit(solution)/shard_map/ppermute | solution.py:257
  61.5 8.4 %collective-permute-start.12 = (f32[64,576]{1,0:T(8,128)S(1)}, f32[64,576]{1,0:T(8,128)S(1)}, u32[]{:S(2)}, u32[]{:S(2)}) collective-permute-start(f32[64,576]{1,0:T(8,128)S(1)} %get-tuple-element.38), channel_id=1, source_target_pairs={{0,192},{32,224},{64,128},{96,160},{128,64},{160,96},{192,0},{224,... | collective-permute-start | bytes 442376 | tf_op jit(solution)/shard_map/ppermute | solution.py:257
  65.4 4.5 %copy-start.5 = (f32[64,576]{1,0:T(8,128)}, f32[64,576]{1,0:T(8,128)S(1)}, u32[]{:S(2)}) copy-start(f32[64,576]{1,0:T(8,128)S(1)} %collective-permute-done.10.b_ref) | copy-start | bytes 442372
  68.0 1.9 %copy-start.6 = (f32[64,576]{1,0:T(8,128)}, f32[64,576]{1,0:T(8,128)S(1)}, u32[]{:S(2)}) copy-start(f32[64,576]{1,0:T(8,128)S(1)} %collective-permute-done.11.c_ref) | copy-start | bytes 442372
  69.9 0.7 copy-start.7
  98.4 16.7 %collective-permute-start.14 = (bf16[512,640]{1,0:T(8,128)(2,1)S(1)}, bf16[512,640]{1,0:T(8,128)(2,1)S(1)}, u32[]{:S(2)}, u32[]{:S(2)}) collective-permute-start(bf16[512,640]{1,0:T(8,128)(2,1)S(1)} %bitcast.29), channel_id=1, source_target_pairs={{0,24},{1,25},{2,26},{3,27},{4,28},{5,29},{6,30},{7,31},{8,0},{9,1... | collective-permute-start | bytes 1966088 | tf_op jit(solution)/shard_map/ppermute | solution.py:299
  98.8 16.2 %collective-permute-start.13 = (bf16[512,640]{1,0:T(8,128)(2,1)S(1)}, bf16[512,640]{1,0:T(8,128)(2,1)S(1)}, u32[]{:S(2)}, u32[]{:S(2)}) collective-permute-start(bf16[512,640]{1,0:T(8,128)(2,1)S(1)} %bitcast.30), channel_id=1, source_target_pairs={{0,8},{1,9},{2,10},{3,11},{4,12},{5,13},{6,14},{7,15},{8,16},{9,17... | collective-permute-start | bytes 1966088 | tf_op jit(solution)/shard_map/ppermute | solution.py:299
  101.0 2.5 %copy-start.1 = (bf16[1,64,64,576]{3,2,1,0:T(8,128)(2,1)S(1)}, bf16[1,64,64,576]{3,2,1,0:T(8,128)(2,1)}, u32[]{:S(2)}) copy-start(bf16[1,64,64,576]{3,2,1,0:T(8,128)(2,1)} %param.11) | copy-start | bytes 14155780
  115.0 19.4 %collective-permute-start.15 = (bf16[512,640]{1,0:T(8,128)(2,1)S(1)}, bf16[512,640]{1,0:T(8,128)(2,1)S(1)}, u32[]{:S(2)}, u32[]{:S(2)}) collective-permute-start(bf16[512,640]{1,0:T(8,128)(2,1)S(1)} %bitcast.32), channel_id=1, source_target_pairs={{0,16},{1,17},{2,18},{3,19},{4,20},{5,21},{6,22},{7,23},{8,24},{9,... | collective-permute-start | bytes 1966088 | tf_op jit(solution)/shard_map/ppermute | solution.py:305

commit v3 on v2

--- a/solution.py
+++ b/solution.py
@@ -63,7 +63,7 @@
         cut_kernel,
         in_specs=[pl.BlockSpec(memory_space=pltpu.SMEM), vmem],
         out_specs=[vmem] * X,
-        out_shape=[jax.ShapeDtypeStruct(part, jnp.bfloat16)] * X,
+        out_shape=[pltpu.VMEM(part, jnp.bfloat16)] + [jax.ShapeDtypeStruct(part, jnp.bfloat16)] * (X - 1),
         scratch_shapes=[pltpu.VMEM((X,) + part, jnp.bfloat16)],
         cost_estimate=pl.CostEstimate(flops=2**34, bytes_accessed=2**24, transcendentals=0),
         name="cut_hidden",
@@ -86,12 +86,14 @@
 
 
 def partial_latents(info, hidden, own, other):
+    hidden = [pltpu.with_memory_space_constraint(h, pltpu.VMEM) for h in hidden]
     vmem = pl.BlockSpec(memory_space=pltpu.VMEM)
     return pl.pallas_call(
         partial_kernel,
         in_specs=[pl.BlockSpec(memory_space=pltpu.SMEM)] + [vmem] * (X + 2 * Y),
         out_specs=[vmem] * X,
-        out_shape=[jax.ShapeDtypeStruct((TOK, LAT), jnp.float32)] * X,
+        out_shape=[pltpu.VMEM((TOK, LAT), jnp.float32)]
+        + [jax.ShapeDtypeStruct((TOK, LAT), jnp.float32)] * (X - 1),
         compiler_params=pltpu.CompilerParams(vmem_limit_bytes=24 * 2**20),
         name="partial_latents",
     )(info, *hidden, *own, *other)
@@ -115,6 +117,7 @@
 
 
 def finish_keys(info, parts, gain, cosine, sine):
+    parts = [pltpu.with_memory_space_constraint(p, pltpu.VMEM) for p in parts]
     vmem = pl.BlockSpec(memory_space=pltpu.VMEM)
     return pl.pallas_call(
         finish_kernel,
@@ -243,18 +246,9 @@
         jnp.broadcast_to(piece[None], (Z, SLICE, LAT)), "ctx", 0, 0, axis_index_groups=Z_GROUPS
     ).reshape(Z * SLICE, LAT)
 
-    parts = cut_hidden((req // 2)[None], suffix_hidden[0])
-    hidden = [parts[0]] + [
+    parts = list(cut_hidden((req // 2)[None], suffix_hidden[0]))
+    hidden = parts[:1] + [
         lax.ppermute(parts[m], "req", [(i, i ^ (2 * m)) for i in range(REQ)]) for m in range(1, X)
-    ]
-
-    pool, row = lax.optimization_barrier((pool, row))
-    own = [row] + [lax.ppermute(row, "ctx", y_shift(d)) for d in (1, 2, 3)]
-    other = [lax.ppermute(o, "req", [(i, i ^ 1) for i in range(REQ)]) for o in own]
-
-    sums = list(partial_latents(jnp.stack([y, req % 2]), hidden, own, other))
-    sums = sums[:1] + [
-        lax.ppermute(sums[m], "req", [(i, i ^ (2 * m)) for i in range(REQ)]) for m in range(1, X)
     ]
 
     half = (LAT - VAL) // 2
@@ -263,6 +257,19 @@
     first = count * PAGE + ctx * TOK
     positions = (first + jnp.arange(TOK, dtype=jnp.int32)).astype(jnp.float32)
     angles = positions[:, None] * freqs[None, :]
+    cosine, sine = jnp.cos(angles), jnp.sin(angles)
+    info = jnp.stack([ctx, count]).astype(jnp.int32)
+    info, cosine, sine, hidden[0] = lax.optimization_barrier((info, cosine, sine, hidden[0]))
+
+    pool, row = lax.optimization_barrier((pool, row))
+    own = [row] + [lax.ppermute(row, "ctx", y_shift(d)) for d in (1, 2, 3)]
+    other = [lax.ppermute(o, "req", [(i, i ^ 1) for i in range(REQ)]) for o in own]
+
+    sums = list(partial_latents(jnp.stack([y, req % 2]), hidden, own, other))
+    sums = sums[:1] + [
+        lax.ppermute(sums[m], "req", [(i, i ^ (2 * m)) for i in range(REQ)]) for m in range(1, X)
+    ]
+
     entries = jnp.arange(hit_holder.shape[1], dtype=jnp.int32)
     used = entries[None, :] < hit_count[:, None]
     earlier = (
@@ -292,13 +299,12 @@
         jnp.broadcast_to(cached[None], (Y * Z,) + cached.shape), "ctx", 0, 0
     ).reshape(-1, AUG)
 
-    fresh = finish_keys(ctx[None], sums, kv_gain[None], jnp.cos(angles), jnp.sin(angles))
+    fresh = finish_keys(info, sums, kv_gain[None], cosine, sine)
     fresh, cached = lax.optimization_barrier((fresh, cached))
     near = lax.all_to_all(fresh, "ctx", 0, 0, axis_index_groups=Z_GROUPS).reshape(-1, AUG)
 
     far = [lax.ppermute(near, "ctx", y_shift(d)) for d in (1, 3)]
 
-    info = jnp.stack([ctx, count]).astype(jnp.int32)
     rows = queries[0].reshape(-1, LAT)
     carry = attend(info, rows, None, [near, cached], True, False)
     far, near = lax.optimization_barrier((far, near))

time: 145 us -> 142 us (0.979)
  waiting for transfers between devices: 23.1 us -> 20.4 us
  starting transfers between devices: 38.7 us -> 41 us
  local copies, waits for them, and re-layouts: 9.3 us -> 7.07 us
    all_to_all x1, waiting for transfers between devices: 5.17 us -> 1.93 us  [shards(): lax.all_to_all(jnp.broadcast_to(piece[None], (Z, SLICE, LAT)), 'ctx', 0,...]
    all_to_all x1, starting transfers between devices: 4.14 us -> 6.54 us  [shards(): lax.all_to_all(jnp.broadcast_to(cached[None], (Y * Z,) + cached.shape), '...]
    unnamed x22 -> x14, local copies, waits for them, and re-layouts: 5.76 us -> 3.47 us
  transfers between devices with their start and end apart: 19 -> 19, of which waited for: 6 -> 6; matrix products, arithmetic and copies ran while one was open for 3% -> 4% of each run, Pallas kernels for 23% -> 23%
where the time goes in v3:
time: 142 us
  Pallas kernels  43.2 us (30%)
  starting transfers between devices  41 us (29%)
  blocking collectives  25.4 us (18%)
  waiting for transfers between devices  20.4 us (14%)
  local copies, waits for them, and re-layouts  7.07 us (5%)
  other arithmetic  3.6 us (3%)
    pallas_call x3, Pallas kernels, attend(): pl.pallas_call(functools.partial(attend_kernel, sub, len(keys), causal, b...  37 us
    all_to_all x1, blocking collectives, shards(): lax.all_to_all(fresh, 'ctx', 0, 0, axis_index_groups=Z_GROUPS)  25.4 us
    all_to_all x1, starting transfers between devices, shards(): lax.all_to_all(jnp.broadcast_to(piece[None], (Z, SLICE, LAT)), 'ctx', 0,...  8.47 us
    ppermute x3, waiting for transfers between devices, shards(): lax.ppermute(parts[m], 'req', [(i, i ^ 2 * m) for i in range(REQ)])  7.07 us
    all_to_all x1, starting transfers between devices, shards(): lax.all_to_all(jnp.broadcast_to(cached[None], (Y * Z,) + cached.shape), '...  6.54 us
    ppermute x3, waiting for transfers between devices, shards(): lax.ppermute(sums[m], 'req', [(i, i ^ 2 * m) for i in range(REQ)])  6.11 us
    ppermute x3, starting transfers between devices, shards(): lax.ppermute(parts[m], 'req', [(i, i ^ 2 * m) for i in range(REQ)])  5.47 us
    all_to_all x1, waiting for transfers between devices, shards(): incoming = lax.all_to_all(outgoing, 'req', 0, 0).reshape(REQ * CAP, LAT)  5.31 us
  transfers between devices with their start and end apart: 19, of which 6 were waited for; matrix products, arithmetic and copies ran while one was open for 4% of the time, Pallas kernels for 23%

profile of v3, /device:TPU:8, one launch (start us, length us, event | category | flops | bytes accessed | tf_op | source)
XLA Modules:
  0.0 141.5 jit_solution(10491375185347422191)
XLA Ops:
  0.0 1.0 copy-done
  1.0 0.8 broadcast_in_dim.69
  1.7 8.5 %all-to-all-start = ((bf16[8,32,576]{2,1,0:T(8,128)(2,1)}), bf16[8,32,576]{2,1,0:T(8,128)(2,1)S(1)}, u32[]{:S(2)}, u32[]{:S(2)}) async-start(bf16[8,32,576]{2,1,0:T(8,128)(2,1)} %broadcast_in_dim.69), calls=%async_computation | async-start | bytes 655360 | tf_op jit(solution)/shard_map/all_to_all | solution.py:245
  10.2 2.8 %cut_hidden.1 = (bf16[64,2048]{1,0:T(8,128)(2,1)S(1)}, bf16[64,2048]{1,0:T(8,128)(2,1)}, bf16[64,2048]{1,0:T(8,128)(2,1)}, bf16[64,2048]{1,0:T(8,128)(2,1)}) custom-call(s32[1]{0:T(128)} %bitcast.2.info, bf16[64,7168]{1,0:T(8,128)(2,1)} %bitcast.36), custom_call_target="tpu_custom_call" | custom-call | flops 17179869184 | bytes 16777216 | tf_op jit(solution)/shard_map/cut_hidden/pallas_call | solution.py:62
  13.0 1.5 %collective-permute-start = (bf16[64,2048]{1,0:T(8,128)(2,1)}, bf16[64,2048]{1,0:T(8,128)(2,1)S(1)}, u32[]{:S(2)}, u32[]{:S(2)}) collective-permute-start(bf16[64,2048]{1,0:T(8,128)(2,1)} %get-tuple-element.36), channel_id=1, source_target_pairs={{0,64},{32,96},{64,0},{96,32},{128,192},{160,224},{192,128},{224,1... | collective-permute-start | bytes 786440 | tf_op jit(solution)/shard_map/ppermute | solution.py:251
  14.5 2.7 %collective-permute-start.1 = (bf16[64,2048]{1,0:T(8,128)(2,1)}, bf16[64,2048]{1,0:T(8,128)(2,1)S(1)}, u32[]{:S(2)}, u32[]{:S(2)}) collective-permute-start(bf16[64,2048]{1,0:T(8,128)(2,1)} %get-tuple-element.37), channel_id=1, source_target_pairs={{0,128},{32,160},{64,192},{96,224},{128,0},{160,32},{192,64},{224,... | collective-permute-start | bytes 786440 | tf_op jit(solution)/shard_map/ppermute | solution.py:251
  17.3 0.6 dynamic_slice.14
  18.0 0.3 convert_reduce_fusion
  18.3 0.1 select_reduce_fusion
  18.5 0.1 copy.10
  19.2 1.2 pad_add_fusion.info
  20.4 0.1 copy.9
  20.5 0.1 reshape.164
  20.7 0.8 multiply_sine_fusion
  21.5 1.9 %all-to-all-done = bf16[8,32,576]{2,1,0:T(8,128)(2,1)S(1)} async-done(((bf16[8,32,576]{2,1,0:T(8,128)(2,1)}), bf16[8,32,576]{2,1,0:T(8,128)(2,1)S(1)}, u32[]{:S(2)}, u32[]{:S(2)}) %all-to-all-start) | async-done | bytes 294944 | tf_op jit(solution)/shard_map/all_to_all | solution.py:245
  23.5 0.4 collective-permute-start.5
  23.9 2.6 %collective-permute-start.4 = (bf16[256,576]{1,0:T(8,128)(2,1)S(1)}, bf16[256,576]{1,0:T(8,128)(2,1)S(1)}, u32[]{:S(2)}, u32[]{:S(2)}) collective-permute-start(bf16[256,576]{1,0:T(8,128)(2,1)S(1)} %bitcast.25), channel_id=1, source_target_pairs={{0,16},{1,17},{2,18},{3,19},{4,20},{5,21},{6,22},{7,23},{8,24},{9,... | collective-permute-start | bytes 884744 | tf_op jit(solution)/shard_map/ppermute | solution.py:265
  26.5 1.9 %collective-permute-start.3 = (bf16[256,576]{1,0:T(8,128)(2,1)S(1)}, bf16[256,576]{1,0:T(8,128)(2,1)S(1)}, u32[]{:S(2)}, u32[]{:S(2)}) collective-permute-start(bf16[256,576]{1,0:T(8,128)(2,1)S(1)} %bitcast.26), channel_id=1, source_target_pairs={{0,8},{1,9},{2,10},{3,11},{4,12},{5,13},{6,14},{7,15},{8,16},{9,17... | collective-permute-start | bytes 884744 | tf_op jit(solution)/shard_map/ppermute | solution.py:265
  28.4 0.6 gather_fusion
  29.0 0.7 broadcast_select_fusion
  29.7 4.3 %all-to-all-start.1 = ((bf16[8,2,576]{2,1,0:T(2,128)(2,1)}), bf16[8,2,576]{2,1,0:T(2,128)(2,1)S(1)}, u32[]{:S(2)}, u32[]{:S(2)}) async-start(bf16[8,2,576]{2,1,0:T(2,128)(2,1)} %broadcast_select_fusion), calls=%async_computation.1 | async-start | bytes 40960 | tf_op jit(solution)/shard_map/all_to_all | solution.py:289
  34.0 0.1 pad_add_fusion.1.info
  34.1 5.3 %all-to-all-done.1 = bf16[8,2,576]{2,1,0:T(2,128)(2,1)S(1)} async-done(((bf16[8,2,576]{2,1,0:T(2,128)(2,1)}), bf16[8,2,576]{2,1,0:T(2,128)(2,1)S(1)}, u32[]{:S(2)}, u32[]{:S(2)}) %all-to-all-start.1) | async-done | bytes 18464 | tf_op jit(solution)/shard_map/all_to_all | solution.py:289
  39.4 0.6 gather_fusion.1
  40.0 1.3 collective-permute-start.2
  41.3 0.5 collective-permute-start.9
  41.8 0.1 collective-permute-start.8
  41.9 0.4 collective-permute-start.7
  42.4 0.1 pad_maximum_fusion
  42.4 7.1 %collective-permute-done.2.refs_3_ = bf16[64,2048]{1,0:T(8,128)(2,1)S(1)} collective-permute-done((bf16[64,2048]{1,0:T(8,128)(2,1)}, bf16[64,2048]{1,0:T(8,128)(2,1)S(1)}, u32[]{:S(2)}, u32[]{:S(2)}) %collective-permute-start.2) | collective-permute-done | bytes 262176 | tf_op jit(solution)/shard_map/ppermute | solution.py:251
  49.5 1.5 %partial_latents.1 = (f32[64,576]{1,0:T(8,128)S(1)}, f32[64,576]{1,0:T(8,128)S(1)}, f32[64,576]{1,0:T(8,128)S(1)}, f32[64,576]{1,0:T(8,128)S(1)}) custom-call(s32[2]{0:T(128)S(1)} %pad_add_fusion.1.info, bf16[64,2048]{1,0:T(8,128)(2,1)S(1)} %get-tuple-element.35.refs_0_, bf16[64,2048]{1,0:T(8,128)(2,1)S(1)} %collective-permute-done.refs_1_, ...), custom_call_target="tpu_custom_call" | custom-call | tf_op jit(solution)/shard_map/partial_latents/pallas_call | solution.py:91
  51.1 0.8 broadcast_in_dim.73
  51.8 6.5 %all-to-all-start.2 = ((bf16[32,8,640]{2,1,0:T(8,128)(2,1)}), bf16[32,8,640]{2,1,0:T(8,128)(2,1)S(1)}, u32[]{:S(2)}, u32[]{:S(2)}) async-start(bf16[32,8,640]{2,1,0:T(8,128)(2,1)} %broadcast_in_dim.73), calls=%async_computation.2 | async-start | bytes 655360 | tf_op jit(solution)/shard_map/all_to_all | solution.py:298
  58.4 0.1 collective-permute-start.10
  58.5 2.6 %collective-permute-start.11 = (f32[64,576]{1,0:T(8,128)S(1)}, f32[64,576]{1,0:T(8,128)S(1)}, u32[]{:S(2)}, u32[]{:S(2)}) collective-permute-start(f32[64,576]{1,0:T(8,128)S(1)} %get-tuple-element.43), channel_id=1, source_target_pairs={{0,128},{32,160},{64,192},{96,224},{128,0},{160,32},{192,64},{224,... | collective-permute-start | bytes 442376 | tf_op jit(solution)/shard_map/ppermute | solution.py:270
  61.1 2.1 %collective-permute-start.12 = (f32[64,576]{1,0:T(8,128)S(1)}, f32[64,576]{1,0:T(8,128)S(1)}, u32[]{:S(2)}, u32[]{:S(2)}) collective-permute-start(f32[64,576]{1,0:T(8,128)S(1)} %get-tuple-element.44), channel_id=1, source_target_pairs={{0,192},{32,224},{64,128},{96,160},{128,64},{160,96},{192,0},{224,... | collective-permute-start | bytes 442376 | tf_op jit(solution)/shard_map/ppermute | solution.py:270
  63.2 1.8 %collective-permute-done.10.b_ref = f32[64,576]{1,0:T(8,128)S(1)} collective-permute-done((f32[64,576]{1,0:T(8,128)S(1)}, f32[64,576]{1,0:T(8,128)S(1)}, u32[]{:S(2)}, u32[]{:S(2)}) %collective-permute-start.10) | collective-permute-done | bytes 147488 | tf_op jit(solution)/shard_map/ppermute | solution.py:270
  65.0 2.4 %collective-permute-done.11.c_ref = f32[64,576]{1,0:T(8,128)S(1)} collective-permute-done((f32[64,576]{1,0:T(8,128)S(1)}, f32[64,576]{1,0:T(8,128)S(1)}, u32[]{:S(2)}, u32[]{:S(2)}) %collective-permute-start.11) | collective-permute-done | bytes 147488 | tf_op jit(solution)/shard_map/ppermute | solution.py:270
  67.5 1.8 %collective-permute-done.12.d_ref = f32[64,576]{1,0:T(8,128)S(1)} collective-permute-done((f32[64,576]{1,0:T(8,128)S(1)}, f32[64,576]{1,0:T(8,128)S(1)}, u32[]{:S(2)}, u32[]{:S(2)}) %collective-permute-start.12) | collective-permute-done | bytes 147488 | tf_op jit(solution)/shard_map/ppermute | solution.py:270
  69.3 1.8 %finish_keys.1 = bf16[8,64,640]{2,1,0:T(8,128)(2,1)} custom-call(s32[2]{0:T(128)} %pad_add_fusion.info, f32[64,576]{1,0:T(8,128)S(1)} %get-tuple-element.41.a_ref, f32[64,576]{1,0:T(8,128)S(1)} %collective-permute-done.10.b_ref, f32[64,576]{1,0:T(8,128)S(1)} %collective-permute-done.11.c_ref, f32[64,576]{1,0:T(8,128)S(1)} %collective-permute-done.12.d_ref, ...), custom_call_target="tpu_custom_call" | custom-call | tf_op jit(solution)/shard_map/finish_keys/pallas_call | solution.py:122
  71.1 25.4 %all_to_all.20 = bf16[8,64,640]{2,1,0:T(8,128)(2,1)S(1)} all-to-all(bf16[8,64,640]{2,1,0:T(8,128)(2,1)} %finish_keys.1), channel_id=1, replica_groups={{0,1,2,3,4,5,6,7},{8,9,10,11,12,13,14,15},{16,17,18,19,20,21,22,23},{24..., dimensions={0} | all-to-all | bytes 1310720 | tf_op jit(solution)/shard_map/all_to_all | solution.py:304
  96.5 0.7 collective-permute-start.14
  97.1 1.3 collective-permute-start.13
  98.5 2.5 %copy-done.1 = bf16[1,64,64,576]{3,2,1,0:T(8,128)(2,1)S(1)} copy-done((bf16[1,64,64,576]{3,2,1,0:T(8,128)(2,1)S(1)}, bf16[1,64,64,576]{3,2,1,0:T(8,128)(2,1)}, u32[]{:S(2)}) %copy-start.1) | copy-done | bytes 4718616
  101.0 11.5 %attend_first.2 = (f32[4096,512]{1,0:T(8,128)S(1)}, f32[4096,128]{1,0:T(8,128)S(1)}, f32[4096,128]{1,0:T(8,128)S(1)}) custom-call(s32[2]{0:T(128)S(1)} %copy-done.2, bf16[4096,576]{1,0:T(8,128)(2,1)S(1)} %bitcast.21, bf16[512,640]{1,0:T(8,128)(2,1)S(1)} %bitcast.31, bf16[256,640]{1,0:T(8,128)(2,1)S(1)} %bitcast.33), custom_call_target="tpu_custom_call" | custom-call | flops 6845104128 | bytes 8388608 | tf_op jit(solution)/shard_map/attend_first/pallas_call | solution.py:215
  112.5 3.4 %collective-permute-start.15 = (bf16[512,640]{1,0:T(8,128)(2,1)S(1)}, bf16[512,640]{1,0:T(8,128)(2,1)S(1)}, u32[]{:S(2)}, u32[]{:S(2)}) collective-permute-start(bf16[512,640]{1,0:T(8,128)(2,1)S(1)} %bitcast.32), channel_id=1, source_target_pairs={{0,16},{1,17},{2,18},{3,19},{4,20},{5,21},{6,22},{7,23},{8,24},{9,... | collective-permute-start | bytes 1966088 | tf_op jit(solution)/shard_map/ppermute | solution.py:311
  115.9 16.0 %attend_first.3 = (f32[4096,512]{1,0:T(8,128)S(1)}, f32[4096,128]{1,0:T(8,128)S(1)}, f32[4096,128]{1,0:T(8,128)S(1)}) custom-call(s32[2]{0:T(128)S(1)} %copy-done.2, bf16[4096,576]{1,0:T(8,128)(2,1)S(1)} %bitcast.22, f32[4096,512]{1,0:T(8,128)S(1)} %get-tuple-element.50.refs_1_, f32[4096,128]{1,0:T(8,128)S(1)} %get-tuple-element.51.refs_2_, ...), custom_call_target="tpu_custom_call" | custom-call | flops 9126805504 | bytes 8388608 | tf_op jit(solution)/shard_map/attend_first/pallas_call | solution.py:215
  132.0 9.5 %attend_last.1 = bf16[4096,512]{1,0:T(8,128)(2,1)} custom-call(s32[2]{0:T(128)S(1)} %copy-done.2, bf16[4096,576]{1,0:T(8,128)(2,1)S(1)} %bitcast.23, f32[4096,512]{1,0:T(8,128)S(1)} %get-tuple-element.55.refs_1_, f32[4096,128]{1,0:T(8,128)S(1)} %get-tuple-element.56.refs_2_, f32[4096,128]{1,0:T(8,128)S(1)} %get-tuple-element.57.refs_3_, ...), custom_call_target="tpu_custom_call" | custom-call | flops 4563402752 | bytes 8388608 | tf_op jit(solution)/shard_map/attend_last/pallas_call | solution.py:215
  (41 shorter events, 0.4 us)
Async XLA Ops:
  0.0 1.0 copy-start
  1.7 21.7 %all-to-all-start = ((bf16[8,32,576]{2,1,0:T(8,128)(2,1)}), bf16[8,32,576]{2,1,0:T(8,128)(2,1)S(1)}, u32[]{:S(2)}, u32[]{:S(2)}) async-start(bf16[8,32,576]{2,1,0:T(8,128)(2,1)} %broadcast_in_dim.69), calls=%async_computation | async-start | bytes 655360 | tf_op jit(solution)/shard_map/all_to_all | solution.py:245
  10.2 7.1 %copy-start.6 = (s32[8]{0:T(128)S(1)}, s32[8]{0:T(128)}, u32[]{:S(2)}) copy-start(s32[8]{0:T(128)} %param.15) | copy-start | bytes 100
  10.2 7.7 %copy-start.4 = (s32[8,8]{1,0:T(8,128)S(1)}, s32[8,8]{1,0:T(8,128)}, u32[]{:S(2)}) copy-start(s32[8,8]{1,0:T(8,128)} %param.13) | copy-start | bytes 772
  10.2 8.1 %copy-start.5 = (s32[8,8]{1,0:T(8,128)S(1)}, s32[8,8]{1,0:T(8,128)}, u32[]{:S(2)}) copy-start(s32[8,8]{1,0:T(8,128)} %param.14) | copy-start | bytes 772
  10.2 18.2 %copy-start.3 = (bf16[12,1,576]{2,0,1:T(8,128)(2,1)S(1)}, bf16[12,1,576]{2,0,1:T(8,128)(2,1)}, u32[]{:S(2)}) copy-start(bf16[12,1,576]{2,0,1:T(8,128)(2,1)} %param.12) | copy-start | bytes 41476
  13.0 27.0 %collective-permute-start = (bf16[64,2048]{1,0:T(8,128)(2,1)}, bf16[64,2048]{1,0:T(8,128)(2,1)S(1)}, u32[]{:S(2)}, u32[]{:S(2)}) collective-permute-start(bf16[64,2048]{1,0:T(8,128)(2,1)} %get-tuple-element.36), channel_id=1, source_target_pairs={{0,64},{32,96},{64,0},{96,32},{128,192},{160,224},{192,128},{224,1... | collective-permute-start | bytes 786440 | tf_op jit(solution)/shard_map/ppermute | solution.py:251
  14.5 26.7 %collective-permute-start.1 = (bf16[64,2048]{1,0:T(8,128)(2,1)}, bf16[64,2048]{1,0:T(8,128)(2,1)S(1)}, u32[]{:S(2)}, u32[]{:S(2)}) collective-permute-start(bf16[64,2048]{1,0:T(8,128)(2,1)} %get-tuple-element.37), channel_id=1, source_target_pairs={{0,128},{32,160},{64,192},{96,224},{128,0},{160,32},{192,64},{224,... | collective-permute-start | bytes 786440 | tf_op jit(solution)/shard_map/ppermute | solution.py:251
  20.4 78.1 %copy-start.2 = (s32[2]{0:T(128)S(1)}, s32[2]{0:T(128)}, u32[]{:S(2)}) copy-start(s32[2]{0:T(128)} %pad_add_fusion.info) | copy-start | bytes 28
  23.5 17.8 %collective-permute-start.5 = (bf16[256,576]{1,0:T(8,128)(2,1)S(1)}, bf16[256,576]{1,0:T(8,128)(2,1)S(1)}, u32[]{:S(2)}, u32[]{:S(2)}) collective-permute-start(bf16[256,576]{1,0:T(8,128)(2,1)S(1)} %bitcast.24), channel_id=1, source_target_pairs={{0,24},{1,25},{2,26},{3,27},{4,28},{5,29},{6,30},{7,31},{8,0},{9,1... | collective-permute-start | bytes 884744 | tf_op jit(solution)/shard_map/ppermute | solution.py:265
  23.9 17.9 %collective-permute-start.4 = (bf16[256,576]{1,0:T(8,128)(2,1)S(1)}, bf16[256,576]{1,0:T(8,128)(2,1)S(1)}, u32[]{:S(2)}, u32[]{:S(2)}) collective-permute-start(bf16[256,576]{1,0:T(8,128)(2,1)S(1)} %bitcast.25), channel_id=1, source_target_pairs={{0,16},{1,17},{2,18},{3,19},{4,20},{5,21},{6,22},{7,23},{8,24},{9,... | collective-permute-start | bytes 884744 | tf_op jit(solution)/shard_map/ppermute | solution.py:265
  26.5 15.4 %collective-permute-start.3 = (bf16[256,576]{1,0:T(8,128)(2,1)S(1)}, bf16[256,576]{1,0:T(8,128)(2,1)S(1)}, u32[]{:S(2)}, u32[]{:S(2)}) collective-permute-start(bf16[256,576]{1,0:T(8,128)(2,1)S(1)} %bitcast.26), channel_id=1, source_target_pairs={{0,8},{1,9},{2,10},{3,11},{4,12},{5,13},{6,14},{7,15},{8,16},{9,17... | collective-permute-start | bytes 884744 | tf_op jit(solution)/shard_map/ppermute | solution.py:265
  29.7 9.7 %all-to-all-start.1 = ((bf16[8,2,576]{2,1,0:T(2,128)(2,1)}), bf16[8,2,576]{2,1,0:T(2,128)(2,1)S(1)}, u32[]{:S(2)}, u32[]{:S(2)}) async-start(bf16[8,2,576]{2,1,0:T(2,128)(2,1)} %broadcast_select_fusion), calls=%async_computation.1 | async-start | bytes 40960 | tf_op jit(solution)/shard_map/all_to_all | solution.py:289
  40.0 9.5 %collective-permute-start.2 = (bf16[64,2048]{1,0:T(8,128)(2,1)}, bf16[64,2048]{1,0:T(8,128)(2,1)S(1)}, u32[]{:S(2)}, u32[]{:S(2)}) collective-permute-start(bf16[64,2048]{1,0:T(8,128)(2,1)} %get-tuple-element.38), channel_id=1, source_target_pairs={{0,192},{32,224},{64,128},{96,160},{128,64},{160,96},{192,0},{224,... | collective-permute-start | bytes 786440 | tf_op jit(solution)/shard_map/ppermute | solution.py:251
  41.3 8.3 %collective-permute-start.6 = (bf16[256,576]{1,0:T(8,128)(2,1)S(1)}, bf16[256,576]{1,0:T(8,128)(2,1)S(1)}, u32[]{:S(2)}, u32[]{:S(2)}) collective-permute-start(bf16[256,576]{1,0:T(8,128)(2,1)S(1)} %bitcast.27), channel_id=1, source_target_pairs={{0,32},{32,0},{64,96},{96,64},{128,160},{160,128},{192,224},{224,1... | collective-permute-start | bytes 884744 | tf_op jit(solution)/shard_map/ppermute | solution.py:266
  41.3 8.3 %collective-permute-start.9 = (bf16[256,576]{1,0:T(8,128)(2,1)S(1)}, bf16[256,576]{1,0:T(8,128)(2,1)S(1)}, u32[]{:S(2)}, u32[]{:S(2)}) collective-permute-start(bf16[256,576]{1,0:T(8,128)(2,1)S(1)} %collective-permute-done.5.refs_7_), channel_id=1, source_target_pairs={{0,32},{32,0},{64,96},{96,64},{128,160},{160,128},{192,224},{224,1... | collective-permute-start | bytes 884744 | tf_op jit(solution)/shard_map/ppermute | solution.py:266
  41.8 7.7 %collective-permute-start.8 = (bf16[256,576]{1,0:T(8,128)(2,1)S(1)}, bf16[256,576]{1,0:T(8,128)(2,1)S(1)}, u32[]{:S(2)}, u32[]{:S(2)}) collective-permute-start(bf16[256,576]{1,0:T(8,128)(2,1)S(1)} %collective-permute-done.4.refs_6_), channel_id=1, source_target_pairs={{0,32},{32,0},{64,96},{96,64},{128,160},{160,128},{192,224},{224,1... | collective-permute-start | bytes 884744 | tf_op jit(solution)/shard_map/ppermute | solution.py:266
  41.9 7.7 %collective-permute-start.7 = (bf16[256,576]{1,0:T(8,128)(2,1)S(1)}, bf16[256,576]{1,0:T(8,128)(2,1)S(1)}, u32[]{:S(2)}, u32[]{:S(2)}) collective-permute-start(bf16[256,576]{1,0:T(8,128)(2,1)S(1)} %collective-permute-done.3.refs_5_), channel_id=1, source_target_pairs={{0,32},{32,0},{64,96},{96,64},{128,160},{160,128},{192,224},{224,1... | collective-permute-start | bytes 884744 | tf_op jit(solution)/shard_map/ppermute | solution.py:266
  51.8 19.3 %all-to-all-start.2 = ((bf16[32,8,640]{2,1,0:T(8,128)(2,1)}), bf16[32,8,640]{2,1,0:T(8,128)(2,1)S(1)}, u32[]{:S(2)}, u32[]{:S(2)}) async-start(bf16[32,8,640]{2,1,0:T(8,128)(2,1)} %broadcast_in_dim.73), calls=%async_computation.2 | async-start | bytes 655360 | tf_op jit(solution)/shard_map/all_to_all | solution.py:298
  58.4 6.6 %collective-permute-start.10 = (f32[64,576]{1,0:T(8,128)S(1)}, f32[64,576]{1,0:T(8,128)S(1)}, u32[]{:S(2)}, u32[]{:S(2)}) collective-permute-start(f32[64,576]{1,0:T(8,128)S(1)} %get-tuple-element.42), channel_id=1, source_target_pairs={{0,64},{32,96},{64,0},{96,32},{128,192},{160,224},{192,128},{224,1... | collective-permute-start | bytes 442376 | tf_op jit(solution)/shard_map/ppermute | solution.py:270
  58.5 9.0 %collective-permute-start.11 = (f32[64,576]{1,0:T(8,128)S(1)}, f32[64,576]{1,0:T(8,128)S(1)}, u32[]{:S(2)}, u32[]{:S(2)}) collective-permute-start(f32[64,576]{1,0:T(8,128)S(1)} %get-tuple-element.43), channel_id=1, source_target_pairs={{0,128},{32,160},{64,192},{96,224},{128,0},{160,32},{192,64},{224,... | collective-permute-start | bytes 442376 | tf_op jit(solution)/shard_map/ppermute | solution.py:270
  61.1 8.2 %collective-permute-start.12 = (f32[64,576]{1,0:T(8,128)S(1)}, f32[64,576]{1,0:T(8,128)S(1)}, u32[]{:S(2)}, u32[]{:S(2)}) collective-permute-start(f32[64,576]{1,0:T(8,128)S(1)} %get-tuple-element.44), channel_id=1, source_target_pairs={{0,192},{32,224},{64,128},{96,160},{128,64},{160,96},{192,0},{224,... | collective-permute-start | bytes 442376 | tf_op jit(solution)/shard_map/ppermute | solution.py:270
  96.5 16.0 %collective-permute-start.14 = (bf16[512,640]{1,0:T(8,128)(2,1)S(1)}, bf16[512,640]{1,0:T(8,128)(2,1)S(1)}, u32[]{:S(2)}, u32[]{:S(2)}) collective-permute-start(bf16[512,640]{1,0:T(8,128)(2,1)S(1)} %bitcast.29), channel_id=1, source_target_pairs={{0,24},{1,25},{2,26},{3,27},{4,28},{5,29},{6,30},{7,31},{8,0},{9,1... | collective-permute-start | bytes 1966088 | tf_op jit(solution)/shard_map/ppermute | solution.py:306
  97.1 15.4 %collective-permute-start.13 = (bf16[512,640]{1,0:T(8,128)(2,1)S(1)}, bf16[512,640]{1,0:T(8,128)(2,1)S(1)}, u32[]{:S(2)}, u32[]{:S(2)}) collective-permute-start(bf16[512,640]{1,0:T(8,128)(2,1)S(1)} %bitcast.30), channel_id=1, source_target_pairs={{0,8},{1,9},{2,10},{3,11},{4,12},{5,13},{6,14},{7,15},{8,16},{9,17... | collective-permute-start | bytes 1966088 | tf_op jit(solution)/shard_map/ppermute | solution.py:306
  98.5 2.5 %copy-start.1 = (bf16[1,64,64,576]{3,2,1,0:T(8,128)(2,1)S(1)}, bf16[1,64,64,576]{3,2,1,0:T(8,128)(2,1)}, u32[]{:S(2)}) copy-start(bf16[1,64,64,576]{3,2,1,0:T(8,128)(2,1)} %param.11) | copy-start | bytes 14155780
  112.5 19.4 %collective-permute-start.15 = (bf16[512,640]{1,0:T(8,128)(2,1)S(1)}, bf16[512,640]{1,0:T(8,128)(2,1)S(1)}, u32[]{:S(2)}, u32[]{:S(2)}) collective-permute-start(bf16[512,640]{1,0:T(8,128)(2,1)S(1)} %bitcast.32), channel_id=1, source_target_pairs={{0,16},{1,17},{2,18},{3,19},{4,20},{5,21},{6,22},{7,23},{8,24},{9,... | collective-permute-start | bytes 1966088 | tf_op jit(solution)/shard_map/ppermute | solution.py:311

commit v4 on v3

--- a/solution.py
+++ b/solution.py
@@ -262,6 +262,7 @@
     info, cosine, sine, hidden[0] = lax.optimization_barrier((info, cosine, sine, hidden[0]))
 
     pool, row = lax.optimization_barrier((pool, row))
+    pool = lax.optimization_barrier((pool, hidden[3]))[0]
     own = [row] + [lax.ppermute(row, "ctx", y_shift(d)) for d in (1, 2, 3)]
     other = [lax.ppermute(o, "req", [(i, i ^ 1) for i in range(REQ)]) for o in own]
 

time: 142 us -> 141 us (level)
  waiting for transfers between devices: 20.4 us -> 17.7 us
    ppermute x3, waiting for transfers between devices: 7.07 us -> 0.01 us  [shards(): lax.ppermute(parts[m], 'req', [(i, i ^ 2 * m) for i in range(REQ)])]
    ppermute x3, waiting for transfers between devices: 6.11 us -> 9.06 us  [shards(): lax.ppermute(sums[m], 'req', [(i, i ^ 2 * m) for i in range(REQ)])]
    ppermute x4, waiting for transfers between devices: 0.01 us -> 1.84 us  [shards(): lax.ppermute(o, 'req', [(i, i ^ 1) for i in range(REQ)])]
    all_to_all x1, starting transfers between devices: 6.54 us -> 8.03 us  [shards(): lax.all_to_all(jnp.broadcast_to(cached[None], (Y * Z,) + cached.shape), '...]
  transfers between devices with their start and end apart: 19 -> 19, of which waited for: 6 -> 9; matrix products, arithmetic and copies ran while one was open for 4% -> 4% of each run, Pallas kernels for 23% -> 23%
where the time goes in v4:
time: 141 us; the launch traced here: 140 us
  Pallas kernels  43.2 us (31%)
  starting transfers between devices  41.8 us (30%)
  blocking collectives  26.2 us (19%)
  waiting for transfers between devices  17.7 us (13%)
  local copies, waits for them, and re-layouts  7.08 us (5%)
  other arithmetic  3.59 us (3%)
    pallas_call x3, Pallas kernels, attend(): pl.pallas_call(functools.partial(attend_kernel, sub, len(keys), causal, b...  37.1 us
    all_to_all x1, blocking collectives, shards(): lax.all_to_all(fresh, 'ctx', 0, 0, axis_index_groups=Z_GROUPS)  26.2 us
    ppermute x3, waiting for transfers between devices, shards(): lax.ppermute(sums[m], 'req', [(i, i ^ 2 * m) for i in range(REQ)])  9.06 us
    all_to_all x1, starting transfers between devices, shards(): lax.all_to_all(jnp.broadcast_to(piece[None], (Z, SLICE, LAT)), 'ctx', 0,...  8.47 us
    all_to_all x1, starting transfers between devices, shards(): lax.all_to_all(jnp.broadcast_to(cached[None], (Y * Z,) + cached.shape), '...  8.03 us
    all_to_all x1, waiting for transfers between devices, shards(): incoming = lax.all_to_all(outgoing, 'req', 0, 0).reshape(REQ * CAP, LAT)  5.31 us
    ppermute x3, starting transfers between devices, shards(): own = [row] + [lax.ppermute(row, 'ctx', y_shift(d)) for d in (1, 2, 3)]  4.93 us
    ppermute x3, starting transfers between devices, shards(): lax.ppermute(sums[m], 'req', [(i, i ^ 2 * m) for i in range(REQ)])  4.79 us
  transfers between devices with their start and end apart: 19, of which 9 were waited for; matrix products, arithmetic and copies ran while one was open for 4% of the time, Pallas kernels for 23%

profile of v4, /device:TPU:8, one launch (start us, length us, event | category | flops | bytes accessed | tf_op | source)
XLA Modules:
  0.0 140.4 jit_solution(6542750862553823648)
XLA Ops:
  0.0 1.0 copy-done
  1.0 0.8 broadcast_in_dim.69
  1.7 8.5 %all-to-all-start = ((bf16[8,32,576]{2,1,0:T(8,128)(2,1)}), bf16[8,32,576]{2,1,0:T(8,128)(2,1)S(1)}, u32[]{:S(2)}, u32[]{:S(2)}) async-start(bf16[8,32,576]{2,1,0:T(8,128)(2,1)} %broadcast_in_dim.69), calls=%async_computation | async-start | bytes 655360 | tf_op jit(solution)/shard_map/all_to_all | solution.py:245
  10.2 2.8 %cut_hidden.1 = (bf16[64,2048]{1,0:T(8,128)(2,1)S(1)}, bf16[64,2048]{1,0:T(8,128)(2,1)}, bf16[64,2048]{1,0:T(8,128)(2,1)}, bf16[64,2048]{1,0:T(8,128)(2,1)}) custom-call(s32[1]{0:T(128)} %bitcast.2.info, bf16[64,7168]{1,0:T(8,128)(2,1)} %bitcast.36), custom_call_target="tpu_custom_call" | custom-call | flops 17179869184 | bytes 16777216 | tf_op jit(solution)/shard_map/cut_hidden/pallas_call | solution.py:62
  13.0 2.8 %collective-permute-start = (bf16[64,2048]{1,0:T(8,128)(2,1)}, bf16[64,2048]{1,0:T(8,128)(2,1)S(1)}, u32[]{:S(2)}, u32[]{:S(2)}) collective-permute-start(bf16[64,2048]{1,0:T(8,128)(2,1)} %get-tuple-element.36), channel_id=1, source_target_pairs={{0,192},{32,224},{64,128},{96,160},{128,64},{160,96},{192,0},{224,... | collective-permute-start | bytes 786440 | tf_op jit(solution)/shard_map/ppermute | solution.py:251
  15.8 0.2 collective-permute-start.1
  16.0 1.7 %collective-permute-start.2 = (bf16[64,2048]{1,0:T(8,128)(2,1)}, bf16[64,2048]{1,0:T(8,128)(2,1)S(1)}, u32[]{:S(2)}, u32[]{:S(2)}) collective-permute-start(bf16[64,2048]{1,0:T(8,128)(2,1)} %get-tuple-element.40), channel_id=1, source_target_pairs={{0,128},{32,160},{64,192},{96,224},{128,0},{160,32},{192,64},{224,... | collective-permute-start | bytes 786440 | tf_op jit(solution)/shard_map/ppermute | solution.py:251
  17.8 0.6 dynamic_slice.14
  19.0 1.2 pad_add_fusion.info
  20.4 0.3 convert_reduce_fusion
  20.7 0.1 select_reduce_fusion
  21.1 0.1 copy.9
  21.2 0.8 multiply_sine_fusion
  22.0 1.4 %all-to-all-done = bf16[8,32,576]{2,1,0:T(8,128)(2,1)S(1)} async-done(((bf16[8,32,576]{2,1,0:T(8,128)(2,1)}), bf16[8,32,576]{2,1,0:T(8,128)(2,1)S(1)}, u32[]{:S(2)}, u32[]{:S(2)}) %all-to-all-start) | async-done | bytes 294944 | tf_op jit(solution)/shard_map/all_to_all | solution.py:245
  23.5 0.4 collective-permute-start.5
  23.9 2.6 %collective-permute-start.4 = (bf16[256,576]{1,0:T(8,128)(2,1)S(1)}, bf16[256,576]{1,0:T(8,128)(2,1)S(1)}, u32[]{:S(2)}, u32[]{:S(2)}) collective-permute-start(bf16[256,576]{1,0:T(8,128)(2,1)S(1)} %bitcast.25), channel_id=1, source_target_pairs={{0,16},{1,17},{2,18},{3,19},{4,20},{5,21},{6,22},{7,23},{8,24},{9,... | collective-permute-start | bytes 884744 | tf_op jit(solution)/shard_map/ppermute | solution.py:266
  26.5 1.9 %collective-permute-start.3 = (bf16[256,576]{1,0:T(8,128)(2,1)S(1)}, bf16[256,576]{1,0:T(8,128)(2,1)S(1)}, u32[]{:S(2)}, u32[]{:S(2)}) collective-permute-start(bf16[256,576]{1,0:T(8,128)(2,1)S(1)} %bitcast.26), channel_id=1, source_target_pairs={{0,8},{1,9},{2,10},{3,11},{4,12},{5,13},{6,14},{7,15},{8,16},{9,17... | collective-permute-start | bytes 884744 | tf_op jit(solution)/shard_map/ppermute | solution.py:266
  28.4 0.6 gather_fusion
  29.0 0.7 broadcast_select_fusion
  29.7 4.3 %all-to-all-start.1 = ((bf16[8,2,576]{2,1,0:T(2,128)(2,1)}), bf16[8,2,576]{2,1,0:T(2,128)(2,1)S(1)}, u32[]{:S(2)}, u32[]{:S(2)}) async-start(bf16[8,2,576]{2,1,0:T(2,128)(2,1)} %broadcast_select_fusion), calls=%async_computation.1 | async-start | bytes 40960 | tf_op jit(solution)/shard_map/all_to_all | solution.py:290
  34.1 5.3 %all-to-all-done.1 = bf16[8,2,576]{2,1,0:T(2,128)(2,1)S(1)} async-done(((bf16[8,2,576]{2,1,0:T(2,128)(2,1)}), bf16[8,2,576]{2,1,0:T(2,128)(2,1)S(1)}, u32[]{:S(2)}, u32[]{:S(2)}) %all-to-all-start.1) | async-done | bytes 18464 | tf_op jit(solution)/shard_map/all_to_all | solution.py:290
  39.4 0.6 gather_fusion.1
  40.0 0.1 collective-permute-start.6
  40.1 0.5 collective-permute-start.9
  40.6 0.1 collective-permute-start.8
  40.7 0.4 collective-permute-start.7
  41.3 0.4 collective-permute-done.6.refs_8_
  41.7 0.5 collective-permute-done.9.refs_11_
  42.2 0.5 collective-permute-done.8.refs_10_
  42.7 0.5 collective-permute-done.7.refs_9_
  43.1 1.5 %partial_latents.1 = (f32[64,576]{1,0:T(8,128)S(1)}, f32[64,576]{1,0:T(8,128)S(1)}, f32[64,576]{1,0:T(8,128)S(1)}, f32[64,576]{1,0:T(8,128)S(1)}) custom-call(s32[2]{0:T(128)S(1)} %pad_add_fusion.1.info, bf16[64,2048]{1,0:T(8,128)(2,1)S(1)} %get-tuple-element.38.refs_0_, bf16[64,2048]{1,0:T(8,128)(2,1)S(1)} %collective-permute-done.1.refs_1_, ...), custom_call_target="tpu_custom_call" | custom-call | tf_op jit(solution)/shard_map/partial_latents/pallas_call | solution.py:91
  44.7 0.8 broadcast_in_dim.73
  45.4 8.0 %all-to-all-start.2 = ((bf16[32,8,640]{2,1,0:T(8,128)(2,1)}), bf16[32,8,640]{2,1,0:T(8,128)(2,1)S(1)}, u32[]{:S(2)}, u32[]{:S(2)}) async-start(bf16[32,8,640]{2,1,0:T(8,128)(2,1)} %broadcast_in_dim.73), calls=%async_computation.2 | async-start | bytes 655360 | tf_op jit(solution)/shard_map/all_to_all | solution.py:299
  53.5 0.5 collective-permute-start.10
  53.9 3.8 %collective-permute-start.11 = (f32[64,576]{1,0:T(8,128)S(1)}, f32[64,576]{1,0:T(8,128)S(1)}, u32[]{:S(2)}, u32[]{:S(2)}) collective-permute-start(f32[64,576]{1,0:T(8,128)S(1)} %get-tuple-element.45), channel_id=1, source_target_pairs={{0,128},{32,160},{64,192},{96,224},{128,0},{160,32},{192,64},{224,... | collective-permute-start | bytes 442376 | tf_op jit(solution)/shard_map/ppermute | solution.py:271
  57.8 0.5 collective-permute-start.12
  58.3 2.4 %collective-permute-done.10.b_ref = f32[64,576]{1,0:T(8,128)S(1)} collective-permute-done((f32[64,576]{1,0:T(8,128)S(1)}, f32[64,576]{1,0:T(8,128)S(1)}, u32[]{:S(2)}, u32[]{:S(2)}) %collective-permute-start.10) | collective-permute-done | bytes 147488 | tf_op jit(solution)/shard_map/ppermute | solution.py:271
  60.7 4.4 %collective-permute-done.11.c_ref = f32[64,576]{1,0:T(8,128)S(1)} collective-permute-done((f32[64,576]{1,0:T(8,128)S(1)}, f32[64,576]{1,0:T(8,128)S(1)}, u32[]{:S(2)}, u32[]{:S(2)}) %collective-permute-start.11) | collective-permute-done | bytes 147488 | tf_op jit(solution)/shard_map/ppermute | solution.py:271
  65.0 2.3 %collective-permute-done.12.d_ref = f32[64,576]{1,0:T(8,128)S(1)} collective-permute-done((f32[64,576]{1,0:T(8,128)S(1)}, f32[64,576]{1,0:T(8,128)S(1)}, u32[]{:S(2)}, u32[]{:S(2)}) %collective-permute-start.12) | collective-permute-done | bytes 147488 | tf_op jit(solution)/shard_map/ppermute | solution.py:271
  67.3 1.8 %finish_keys.1 = bf16[8,64,640]{2,1,0:T(8,128)(2,1)} custom-call(s32[2]{0:T(128)} %pad_add_fusion.info, f32[64,576]{1,0:T(8,128)S(1)} %get-tuple-element.43.a_ref, f32[64,576]{1,0:T(8,128)S(1)} %collective-permute-done.10.b_ref, f32[64,576]{1,0:T(8,128)S(1)} %collective-permute-done.11.c_ref, f32[64,576]{1,0:T(8,128)S(1)} %collective-permute-done.12.d_ref, ...), custom_call_target="tpu_custom_call" | custom-call | tf_op jit(solution)/shard_map/finish_keys/pallas_call | solution.py:122
  69.1 26.2 %all_to_all.20 = bf16[8,64,640]{2,1,0:T(8,128)(2,1)S(1)} all-to-all(bf16[8,64,640]{2,1,0:T(8,128)(2,1)} %finish_keys.1), channel_id=1, replica_groups={{0,1,2,3,4,5,6,7},{8,9,10,11,12,13,14,15},{16,17,18,19,20,21,22,23},{24..., dimensions={0} | all-to-all | bytes 1310720 | tf_op jit(solution)/shard_map/all_to_all | solution.py:305
  95.3 0.6 collective-permute-start.14
  95.9 1.5 %collective-permute-start.13 = (bf16[512,640]{1,0:T(8,128)(2,1)S(1)}, bf16[512,640]{1,0:T(8,128)(2,1)S(1)}, u32[]{:S(2)}, u32[]{:S(2)}) collective-permute-start(bf16[512,640]{1,0:T(8,128)(2,1)S(1)} %bitcast.30), channel_id=1, source_target_pairs={{0,8},{1,9},{2,10},{3,11},{4,12},{5,13},{6,14},{7,15},{8,16},{9,17... | collective-permute-start | bytes 1966088 | tf_op jit(solution)/shard_map/ppermute | solution.py:307
  97.3 2.5 %copy-done.1 = bf16[1,64,64,576]{3,2,1,0:T(8,128)(2,1)S(1)} copy-done((bf16[1,64,64,576]{3,2,1,0:T(8,128)(2,1)S(1)}, bf16[1,64,64,576]{3,2,1,0:T(8,128)(2,1)}, u32[]{:S(2)}) %copy-start.1) | copy-done | bytes 4718616
  99.8 11.5 %attend_first.2 = (f32[4096,512]{1,0:T(8,128)S(1)}, f32[4096,128]{1,0:T(8,128)S(1)}, f32[4096,128]{1,0:T(8,128)S(1)}) custom-call(s32[2]{0:T(128)S(1)} %copy-done.2, bf16[4096,576]{1,0:T(8,128)(2,1)S(1)} %bitcast.21, bf16[512,640]{1,0:T(8,128)(2,1)S(1)} %bitcast.31, bf16[256,640]{1,0:T(8,128)(2,1)S(1)} %bitcast.33), custom_call_target="tpu_custom_call" | custom-call | flops 6845104128 | bytes 8388608 | tf_op jit(solution)/shard_map/attend_first/pallas_call | solution.py:215
  111.4 3.4 %collective-permute-start.15 = (bf16[512,640]{1,0:T(8,128)(2,1)S(1)}, bf16[512,640]{1,0:T(8,128)(2,1)S(1)}, u32[]{:S(2)}, u32[]{:S(2)}) collective-permute-start(bf16[512,640]{1,0:T(8,128)(2,1)S(1)} %bitcast.32), channel_id=1, source_target_pairs={{0,16},{1,17},{2,18},{3,19},{4,20},{5,21},{6,22},{7,23},{8,24},{9,... | collective-permute-start | bytes 1966088 | tf_op jit(solution)/shard_map/ppermute | solution.py:312
  114.8 16.0 %attend_first.3 = (f32[4096,512]{1,0:T(8,128)S(1)}, f32[4096,128]{1,0:T(8,128)S(1)}, f32[4096,128]{1,0:T(8,128)S(1)}) custom-call(s32[2]{0:T(128)S(1)} %copy-done.2, bf16[4096,576]{1,0:T(8,128)(2,1)S(1)} %bitcast.22, f32[4096,512]{1,0:T(8,128)S(1)} %get-tuple-element.52.refs_1_, f32[4096,128]{1,0:T(8,128)S(1)} %get-tuple-element.53.refs_2_, ...), custom_call_target="tpu_custom_call" | custom-call | flops 9126805504 | bytes 8388608 | tf_op jit(solution)/shard_map/attend_first/pallas_call | solution.py:215
  130.8 9.5 %attend_last.1 = bf16[4096,512]{1,0:T(8,128)(2,1)} custom-call(s32[2]{0:T(128)S(1)} %copy-done.2, bf16[4096,576]{1,0:T(8,128)(2,1)S(1)} %bitcast.23, f32[4096,512]{1,0:T(8,128)S(1)} %get-tuple-element.57.refs_1_, f32[4096,128]{1,0:T(8,128)S(1)} %get-tuple-element.58.refs_2_, f32[4096,128]{1,0:T(8,128)S(1)} %get-tuple-element.59.refs_3_, ...), custom_call_target="tpu_custom_call" | custom-call | flops 4563402752 | bytes 8388608 | tf_op jit(solution)/shard_map/attend_last/pallas_call | solution.py:215
  (41 shorter events, 0.7 us)
Async XLA Ops:
  0.0 1.0 copy-start
  1.7 21.7 %all-to-all-start = ((bf16[8,32,576]{2,1,0:T(8,128)(2,1)}), bf16[8,32,576]{2,1,0:T(8,128)(2,1)S(1)}, u32[]{:S(2)}, u32[]{:S(2)}) async-start(bf16[8,32,576]{2,1,0:T(8,128)(2,1)} %broadcast_in_dim.69), calls=%async_computation | async-start | bytes 655360 | tf_op jit(solution)/shard_map/all_to_all | solution.py:245
  10.2 7.6 %copy-start.6 = (s32[8]{0:T(128)S(1)}, s32[8]{0:T(128)}, u32[]{:S(2)}) copy-start(s32[8]{0:T(128)} %param.15) | copy-start | bytes 100
  10.2 10.1 %copy-start.4 = (s32[8,8]{1,0:T(8,128)S(1)}, s32[8,8]{1,0:T(8,128)}, u32[]{:S(2)}) copy-start(s32[8,8]{1,0:T(8,128)} %param.13) | copy-start | bytes 772
  10.2 10.5 %copy-start.5 = (s32[8,8]{1,0:T(8,128)S(1)}, s32[8,8]{1,0:T(8,128)}, u32[]{:S(2)}) copy-start(s32[8,8]{1,0:T(8,128)} %param.14) | copy-start | bytes 772
  10.2 18.2 %copy-start.3 = (bf16[12,1,576]{2,0,1:T(8,128)(2,1)S(1)}, bf16[12,1,576]{2,0,1:T(8,128)(2,1)}, u32[]{:S(2)}) copy-start(bf16[12,1,576]{2,0,1:T(8,128)(2,1)} %param.12) | copy-start | bytes 41476
  13.0 13.5 %collective-permute-start = (bf16[64,2048]{1,0:T(8,128)(2,1)}, bf16[64,2048]{1,0:T(8,128)(2,1)S(1)}, u32[]{:S(2)}, u32[]{:S(2)}) collective-permute-start(bf16[64,2048]{1,0:T(8,128)(2,1)} %get-tuple-element.36), channel_id=1, source_target_pairs={{0,192},{32,224},{64,128},{96,160},{128,64},{160,96},{192,0},{224,... | collective-permute-start | bytes 786440 | tf_op jit(solution)/shard_map/ppermute | solution.py:251
  15.8 24.2 %collective-permute-start.1 = (bf16[64,2048]{1,0:T(8,128)(2,1)}, bf16[64,2048]{1,0:T(8,128)(2,1)S(1)}, u32[]{:S(2)}, u32[]{:S(2)}) collective-permute-start(bf16[64,2048]{1,0:T(8,128)(2,1)} %get-tuple-element.39), channel_id=1, source_target_pairs={{0,64},{32,96},{64,0},{96,32},{128,192},{160,224},{192,128},{224,1... | collective-permute-start | bytes 786440 | tf_op jit(solution)/shard_map/ppermute | solution.py:251
  16.0 25.3 %collective-permute-start.2 = (bf16[64,2048]{1,0:T(8,128)(2,1)}, bf16[64,2048]{1,0:T(8,128)(2,1)S(1)}, u32[]{:S(2)}, u32[]{:S(2)}) collective-permute-start(bf16[64,2048]{1,0:T(8,128)(2,1)} %get-tuple-element.40), channel_id=1, source_target_pairs={{0,128},{32,160},{64,192},{96,224},{128,0},{160,32},{192,64},{224,... | collective-permute-start | bytes 786440 | tf_op jit(solution)/shard_map/ppermute | solution.py:251
  20.2 77.1 %copy-start.2 = (s32[2]{0:T(128)S(1)}, s32[2]{0:T(128)}, u32[]{:S(2)}) copy-start(s32[2]{0:T(128)} %pad_add_fusion.info) | copy-start | bytes 28
  23.5 16.6 %collective-permute-start.5 = (bf16[256,576]{1,0:T(8,128)(2,1)S(1)}, bf16[256,576]{1,0:T(8,128)(2,1)S(1)}, u32[]{:S(2)}, u32[]{:S(2)}) collective-permute-start(bf16[256,576]{1,0:T(8,128)(2,1)S(1)} %bitcast.24), channel_id=1, source_target_pairs={{0,24},{1,25},{2,26},{3,27},{4,28},{5,29},{6,30},{7,31},{8,0},{9,1... | collective-permute-start | bytes 884744 | tf_op jit(solution)/shard_map/ppermute | solution.py:266
  23.9 16.7 %collective-permute-start.4 = (bf16[256,576]{1,0:T(8,128)(2,1)S(1)}, bf16[256,576]{1,0:T(8,128)(2,1)S(1)}, u32[]{:S(2)}, u32[]{:S(2)}) collective-permute-start(bf16[256,576]{1,0:T(8,128)(2,1)S(1)} %bitcast.25), channel_id=1, source_target_pairs={{0,16},{1,17},{2,18},{3,19},{4,20},{5,21},{6,22},{7,23},{8,24},{9,... | collective-permute-start | bytes 884744 | tf_op jit(solution)/shard_map/ppermute | solution.py:266
  26.5 14.2 %collective-permute-start.3 = (bf16[256,576]{1,0:T(8,128)(2,1)S(1)}, bf16[256,576]{1,0:T(8,128)(2,1)S(1)}, u32[]{:S(2)}, u32[]{:S(2)}) collective-permute-start(bf16[256,576]{1,0:T(8,128)(2,1)S(1)} %bitcast.26), channel_id=1, source_target_pairs={{0,8},{1,9},{2,10},{3,11},{4,12},{5,13},{6,14},{7,15},{8,16},{9,17... | collective-permute-start | bytes 884744 | tf_op jit(solution)/shard_map/ppermute | solution.py:266
  29.7 9.7 %all-to-all-start.1 = ((bf16[8,2,576]{2,1,0:T(2,128)(2,1)}), bf16[8,2,576]{2,1,0:T(2,128)(2,1)S(1)}, u32[]{:S(2)}, u32[]{:S(2)}) async-start(bf16[8,2,576]{2,1,0:T(2,128)(2,1)} %broadcast_select_fusion), calls=%async_computation.1 | async-start | bytes 40960 | tf_op jit(solution)/shard_map/all_to_all | solution.py:290
  40.0 1.7 %collective-permute-start.6 = (bf16[256,576]{1,0:T(8,128)(2,1)S(1)}, bf16[256,576]{1,0:T(8,128)(2,1)S(1)}, u32[]{:S(2)}, u32[]{:S(2)}) collective-permute-start(bf16[256,576]{1,0:T(8,128)(2,1)S(1)} %bitcast.27), channel_id=1, source_target_pairs={{0,32},{32,0},{64,96},{96,64},{128,160},{160,128},{192,224},{224,1... | collective-permute-start | bytes 884744 | tf_op jit(solution)/shard_map/ppermute | solution.py:267
  40.1 2.1 %collective-permute-start.9 = (bf16[256,576]{1,0:T(8,128)(2,1)S(1)}, bf16[256,576]{1,0:T(8,128)(2,1)S(1)}, u32[]{:S(2)}, u32[]{:S(2)}) collective-permute-start(bf16[256,576]{1,0:T(8,128)(2,1)S(1)} %collective-permute-done.5.refs_7_), channel_id=1, source_target_pairs={{0,32},{32,0},{64,96},{96,64},{128,160},{160,128},{192,224},{224,1... | collective-permute-start | bytes 884744 | tf_op jit(solution)/shard_map/ppermute | solution.py:267
  40.6 2.0 %collective-permute-start.8 = (bf16[256,576]{1,0:T(8,128)(2,1)S(1)}, bf16[256,576]{1,0:T(8,128)(2,1)S(1)}, u32[]{:S(2)}, u32[]{:S(2)}) collective-permute-start(bf16[256,576]{1,0:T(8,128)(2,1)S(1)} %collective-permute-done.4.refs_6_), channel_id=1, source_target_pairs={{0,32},{32,0},{64,96},{96,64},{128,160},{160,128},{192,224},{224,1... | collective-permute-start | bytes 884744 | tf_op jit(solution)/shard_map/ppermute | solution.py:267
  40.7 2.4 %collective-permute-start.7 = (bf16[256,576]{1,0:T(8,128)(2,1)S(1)}, bf16[256,576]{1,0:T(8,128)(2,1)S(1)}, u32[]{:S(2)}, u32[]{:S(2)}) collective-permute-start(bf16[256,576]{1,0:T(8,128)(2,1)S(1)} %collective-permute-done.3.refs_5_), channel_id=1, source_target_pairs={{0,32},{32,0},{64,96},{96,64},{128,160},{160,128},{192,224},{224,1... | collective-permute-start | bytes 884744 | tf_op jit(solution)/shard_map/ppermute | solution.py:267
  45.4 23.7 %all-to-all-start.2 = ((bf16[32,8,640]{2,1,0:T(8,128)(2,1)}), bf16[32,8,640]{2,1,0:T(8,128)(2,1)S(1)}, u32[]{:S(2)}, u32[]{:S(2)}) async-start(bf16[32,8,640]{2,1,0:T(8,128)(2,1)} %broadcast_in_dim.73), calls=%async_computation.2 | async-start | bytes 655360 | tf_op jit(solution)/shard_map/all_to_all | solution.py:299
  53.5 7.2 %collective-permute-start.10 = (f32[64,576]{1,0:T(8,128)S(1)}, f32[64,576]{1,0:T(8,128)S(1)}, u32[]{:S(2)}, u32[]{:S(2)}) collective-permute-start(f32[64,576]{1,0:T(8,128)S(1)} %get-tuple-element.44), channel_id=1, source_target_pairs={{0,64},{32,96},{64,0},{96,32},{128,192},{160,224},{192,128},{224,1... | collective-permute-start | bytes 442376 | tf_op jit(solution)/shard_map/ppermute | solution.py:271
  53.9 11.1 %collective-permute-start.11 = (f32[64,576]{1,0:T(8,128)S(1)}, f32[64,576]{1,0:T(8,128)S(1)}, u32[]{:S(2)}, u32[]{:S(2)}) collective-permute-start(f32[64,576]{1,0:T(8,128)S(1)} %get-tuple-element.45), channel_id=1, source_target_pairs={{0,128},{32,160},{64,192},{96,224},{128,0},{160,32},{192,64},{224,... | collective-permute-start | bytes 442376 | tf_op jit(solution)/shard_map/ppermute | solution.py:271
  57.8 9.5 %collective-permute-start.12 = (f32[64,576]{1,0:T(8,128)S(1)}, f32[64,576]{1,0:T(8,128)S(1)}, u32[]{:S(2)}, u32[]{:S(2)}) collective-permute-start(f32[64,576]{1,0:T(8,128)S(1)} %get-tuple-element.46), channel_id=1, source_target_pairs={{0,192},{32,224},{64,128},{96,160},{128,64},{160,96},{192,0},{224,... | collective-permute-start | bytes 442376 | tf_op jit(solution)/shard_map/ppermute | solution.py:271
  95.3 16.0 %collective-permute-start.14 = (bf16[512,640]{1,0:T(8,128)(2,1)S(1)}, bf16[512,640]{1,0:T(8,128)(2,1)S(1)}, u32[]{:S(2)}, u32[]{:S(2)}) collective-permute-start(bf16[512,640]{1,0:T(8,128)(2,1)S(1)} %bitcast.29), channel_id=1, source_target_pairs={{0,24},{1,25},{2,26},{3,27},{4,28},{5,29},{6,30},{7,31},{8,0},{9,1... | collective-permute-start | bytes 1966088 | tf_op jit(solution)/shard_map/ppermute | solution.py:307
  95.9 15.5 %collective-permute-start.13 = (bf16[512,640]{1,0:T(8,128)(2,1)S(1)}, bf16[512,640]{1,0:T(8,128)(2,1)S(1)}, u32[]{:S(2)}, u32[]{:S(2)}) collective-permute-start(bf16[512,640]{1,0:T(8,128)(2,1)S(1)} %bitcast.30), channel_id=1, source_target_pairs={{0,8},{1,9},{2,10},{3,11},{4,12},{5,13},{6,14},{7,15},{8,16},{9,17... | collective-permute-start | bytes 1966088 | tf_op jit(solution)/shard_map/ppermute | solution.py:307
  97.3 2.5 %copy-start.1 = (bf16[1,64,64,576]{3,2,1,0:T(8,128)(2,1)S(1)}, bf16[1,64,64,576]{3,2,1,0:T(8,128)(2,1)}, u32[]{:S(2)}) copy-start(bf16[1,64,64,576]{3,2,1,0:T(8,128)(2,1)} %param.11) | copy-start | bytes 14155780
  111.4 19.5 %collective-permute-start.15 = (bf16[512,640]{1,0:T(8,128)(2,1)S(1)}, bf16[512,640]{1,0:T(8,128)(2,1)S(1)}, u32[]{:S(2)}, u32[]{:S(2)}) collective-permute-start(bf16[512,640]{1,0:T(8,128)(2,1)S(1)} %bitcast.32), channel_id=1, source_target_pairs={{0,16},{1,17},{2,18},{3,19},{4,20},{5,21},{6,22},{7,23},{8,24},{9,... | collective-permute-start | bytes 1966088 | tf_op jit(solution)/shard_map/ppermute | solution.py:312

commit v5 on v4

--- a/solution.py
+++ b/solution.py
@@ -307,7 +307,8 @@
     far = [lax.ppermute(near, "ctx", y_shift(d)) for d in (1, 3)]
 
     rows = queries[0].reshape(-1, LAT)
-    carry = attend(info, rows, None, [near, cached], True, False)
+    streamed = pltpu.with_memory_space_constraint(rows, pltpu.HBM)
+    carry = attend(info, streamed, None, [near, cached], True, False)
     far, near = lax.optimization_barrier((far, near))
     last = lax.ppermute(near, "ctx", y_shift(2))
     carry = attend(info, rows, carry, far, False, False)

time: 141 us -> 143 us (1.014)
  the two profiles are of different devices: /device:TPU:8 before, /device:TPU:18 now
where the time goes in v5:
time: 143 us
  starting transfers between devices  44.7 us (31%)
  Pallas kernels  44.4 us (31%)
  blocking collectives  26.2 us (18%)
  waiting for transfers between devices  18.3 us (13%)
  local copies, waits for them, and re-layouts  4.57 us (3%)
  other arithmetic  3.51 us (2%)
    pallas_call x3, Pallas kernels, attend(): pl.pallas_call(functools.partial(attend_kernel, sub, len(keys), causal, b...  38.3 us
    all_to_all x1, blocking collectives, shards(): lax.all_to_all(fresh, 'ctx', 0, 0, axis_index_groups=Z_GROUPS)  26.2 us
    ppermute x1, starting transfers between devices, shards(): last = lax.ppermute(near, 'ctx', y_shift(2))  9.76 us
    all_to_all x1, starting transfers between devices, shards(): lax.all_to_all(jnp.broadcast_to(piece[None], (Z, SLICE, LAT)), 'ctx', 0,...  8.47 us
    ppermute x3, waiting for transfers between devices, shards(): lax.ppermute(sums[m], 'req', [(i, i ^ 2 * m) for i in range(REQ)])  8.44 us
    all_to_all x1, starting transfers between devices, shards(): lax.all_to_all(jnp.broadcast_to(cached[None], (Y * Z,) + cached.shape), '...  8.17 us
    all_to_all x1, starting transfers between devices, shards(): incoming = lax.all_to_all(outgoing, 'req', 0, 0).reshape(REQ * CAP, LAT)  4.83 us
    ppermute x3, starting transfers between devices, shards(): lax.ppermute(sums[m], 'req', [(i, i ^ 2 * m) for i in range(REQ)])  3.89 us
  transfers between devices with their start and end apart: 19, of which 7 were waited for; matrix products, arithmetic and copies ran while one was open for 4% of the time, Pallas kernels for 23%

profile of v5, /device:TPU:18, one launch (start us, length us, event | category | flops | bytes accessed | tf_op | source)
XLA Modules:
  0.0 142.5 jit_solution(1812570502945081784)
XLA Ops:
  0.0 1.0 copy-done
  1.0 0.8 broadcast_in_dim.69
  1.7 8.5 %all-to-all-start = ((bf16[8,32,576]{2,1,0:T(8,128)(2,1)}), bf16[8,32,576]{2,1,0:T(8,128)(2,1)S(1)}, u32[]{:S(2)}, u32[]{:S(2)}) async-start(bf16[8,32,576]{2,1,0:T(8,128)(2,1)} %broadcast_in_dim.69), calls=%async_computation | async-start | bytes 655360 | tf_op jit(solution)/shard_map/all_to_all | solution.py:245
  10.2 2.8 %cut_hidden.1 = (bf16[64,2048]{1,0:T(8,128)(2,1)S(1)}, bf16[64,2048]{1,0:T(8,128)(2,1)}, bf16[64,2048]{1,0:T(8,128)(2,1)}, bf16[64,2048]{1,0:T(8,128)(2,1)}) custom-call(s32[1]{0:T(128)} %bitcast.2.info, bf16[64,7168]{1,0:T(8,128)(2,1)} %bitcast.38), custom_call_target="tpu_custom_call" | custom-call | flops 17179869184 | bytes 16777216 | tf_op jit(solution)/shard_map/cut_hidden/pallas_call | solution.py:62
  13.1 1.5 %collective-permute-start = (bf16[64,2048]{1,0:T(8,128)(2,1)}, bf16[64,2048]{1,0:T(8,128)(2,1)S(1)}, u32[]{:S(2)}, u32[]{:S(2)}) collective-permute-start(bf16[64,2048]{1,0:T(8,128)(2,1)} %get-tuple-element.36), channel_id=1, source_target_pairs={{0,192},{32,224},{64,128},{96,160},{128,64},{160,96},{192,0},{224,... | collective-permute-start | bytes 786440 | tf_op jit(solution)/shard_map/ppermute | solution.py:251
  14.5 1.8 %collective-permute-start.1 = (bf16[64,2048]{1,0:T(8,128)(2,1)}, bf16[64,2048]{1,0:T(8,128)(2,1)S(1)}, u32[]{:S(2)}, u32[]{:S(2)}) collective-permute-start(bf16[64,2048]{1,0:T(8,128)(2,1)} %get-tuple-element.39), channel_id=1, source_target_pairs={{0,64},{32,96},{64,0},{96,32},{128,192},{160,224},{192,128},{224,1... | collective-permute-start | bytes 786440 | tf_op jit(solution)/shard_map/ppermute | solution.py:251
  16.3 0.2 collective-permute-start.2
  16.6 0.6 dynamic_slice.14
  17.7 1.1 pad_add_fusion.info
  18.9 0.1 compare_and_fusion
  19.0 0.3 convert_reduce_fusion
  19.3 0.1 select_reduce_fusion
  19.5 0.1 copy.10
  19.6 0.1 reshape.164
  19.7 0.1 copy.9
  19.8 0.8 multiply_sine_fusion
  20.7 2.8 %all-to-all-done = bf16[8,32,576]{2,1,0:T(8,128)(2,1)S(1)} async-done(((bf16[8,32,576]{2,1,0:T(8,128)(2,1)}), bf16[8,32,576]{2,1,0:T(8,128)(2,1)S(1)}, u32[]{:S(2)}, u32[]{:S(2)}) %all-to-all-start) | async-done | bytes 294944 | tf_op jit(solution)/shard_map/all_to_all | solution.py:245
  23.5 0.4 collective-permute-start.5
  23.9 2.9 %collective-permute-start.4 = (bf16[256,576]{1,0:T(8,128)(2,1)S(1)}, bf16[256,576]{1,0:T(8,128)(2,1)S(1)}, u32[]{:S(2)}, u32[]{:S(2)}) collective-permute-start(bf16[256,576]{1,0:T(8,128)(2,1)S(1)} %bitcast.27), channel_id=1, source_target_pairs={{0,16},{1,17},{2,18},{3,19},{4,20},{5,21},{6,22},{7,23},{8,24},{9,... | collective-permute-start | bytes 884744 | tf_op jit(solution)/shard_map/ppermute | solution.py:266
  26.8 0.6 gather_fusion
  27.4 0.7 broadcast_select_fusion
  28.1 4.8 %all-to-all-start.1 = ((bf16[8,2,576]{2,1,0:T(2,128)(2,1)}), bf16[8,2,576]{2,1,0:T(2,128)(2,1)S(1)}, u32[]{:S(2)}, u32[]{:S(2)}) async-start(bf16[8,2,576]{2,1,0:T(2,128)(2,1)} %broadcast_select_fusion), calls=%async_computation.1 | async-start | bytes 40960 | tf_op jit(solution)/shard_map/all_to_all | solution.py:290
  33.0 0.1 pad_add_fusion.1.info
  33.0 3.8 %all-to-all-done.1 = bf16[8,2,576]{2,1,0:T(2,128)(2,1)S(1)} async-done(((bf16[8,2,576]{2,1,0:T(2,128)(2,1)}), bf16[8,2,576]{2,1,0:T(2,128)(2,1)S(1)}, u32[]{:S(2)}, u32[]{:S(2)}) %all-to-all-start.1) | async-done | bytes 18464 | tf_op jit(solution)/shard_map/all_to_all | solution.py:290
  36.9 0.6 gather_fusion.1
  37.5 0.1 collective-permute-start.6
  37.6 0.5 collective-permute-start.9
  38.1 0.1 collective-permute-start.8
  38.2 1.7 %collective-permute-done.3.refs_5_ = bf16[256,576]{1,0:T(8,128)(2,1)S(1)} collective-permute-done((bf16[256,576]{1,0:T(8,128)(2,1)S(1)}, bf16[256,576]{1,0:T(8,128)(2,1)S(1)}, u32[]{:S(2)}, u32[]{:S(2)}) %collective-permute-start.3) | collective-permute-done | bytes 294944 | tf_op jit(solution)/shard_map/ppermute | solution.py:266
  40.0 0.1 pad_maximum_fusion
  40.2 1.4 %collective-permute-done.7.refs_9_ = bf16[256,576]{1,0:T(8,128)(2,1)S(1)} collective-permute-done((bf16[256,576]{1,0:T(8,128)(2,1)S(1)}, bf16[256,576]{1,0:T(8,128)(2,1)S(1)}, u32[]{:S(2)}, u32[]{:S(2)}) %collective-permute-start.7) | collective-permute-done | bytes 294944 | tf_op jit(solution)/shard_map/ppermute | solution.py:267
  41.6 1.5 %partial_latents.1 = (f32[64,576]{1,0:T(8,128)S(1)}, f32[64,576]{1,0:T(8,128)S(1)}, f32[64,576]{1,0:T(8,128)S(1)}, f32[64,576]{1,0:T(8,128)S(1)}) custom-call(s32[2]{0:T(128)S(1)} %pad_add_fusion.1.info, bf16[64,2048]{1,0:T(8,128)(2,1)S(1)} %get-tuple-element.38.refs_0_, bf16[64,2048]{1,0:T(8,128)(2,1)S(1)} %collective-permute-done.1.refs_1_, ...), custom_call_target="tpu_custom_call" | custom-call | tf_op jit(solution)/shard_map/partial_latents/pallas_call | solution.py:91
  43.1 0.8 broadcast_in_dim.73
  43.9 8.2 %all-to-all-start.2 = ((bf16[32,8,640]{2,1,0:T(8,128)(2,1)}), bf16[32,8,640]{2,1,0:T(8,128)(2,1)S(1)}, u32[]{:S(2)}, u32[]{:S(2)}) async-start(bf16[32,8,640]{2,1,0:T(8,128)(2,1)} %broadcast_in_dim.73), calls=%async_computation.2 | async-start | bytes 655360 | tf_op jit(solution)/shard_map/all_to_all | solution.py:299
  52.1 1.7 %collective-permute-start.10 = (f32[64,576]{1,0:T(8,128)S(1)}, f32[64,576]{1,0:T(8,128)S(1)}, u32[]{:S(2)}, u32[]{:S(2)}) collective-permute-start(f32[64,576]{1,0:T(8,128)S(1)} %get-tuple-element.44), channel_id=1, source_target_pairs={{0,64},{32,96},{64,0},{96,32},{128,192},{160,224},{192,128},{224,1... | collective-permute-start | bytes 442376 | tf_op jit(solution)/shard_map/ppermute | solution.py:271
  53.8 1.7 %collective-permute-start.11 = (f32[64,576]{1,0:T(8,128)S(1)}, f32[64,576]{1,0:T(8,128)S(1)}, u32[]{:S(2)}, u32[]{:S(2)}) collective-permute-start(f32[64,576]{1,0:T(8,128)S(1)} %get-tuple-element.45), channel_id=1, source_target_pairs={{0,128},{32,160},{64,192},{96,224},{128,0},{160,32},{192,64},{224,... | collective-permute-start | bytes 442376 | tf_op jit(solution)/shard_map/ppermute | solution.py:271
  55.5 0.5 collective-permute-start.12
  56.0 2.5 %collective-permute-done.10.b_ref = f32[64,576]{1,0:T(8,128)S(1)} collective-permute-done((f32[64,576]{1,0:T(8,128)S(1)}, f32[64,576]{1,0:T(8,128)S(1)}, u32[]{:S(2)}, u32[]{:S(2)}) %collective-permute-start.10) | collective-permute-done | bytes 147488 | tf_op jit(solution)/shard_map/ppermute | solution.py:271
  58.5 4.5 %collective-permute-done.11.c_ref = f32[64,576]{1,0:T(8,128)S(1)} collective-permute-done((f32[64,576]{1,0:T(8,128)S(1)}, f32[64,576]{1,0:T(8,128)S(1)}, u32[]{:S(2)}, u32[]{:S(2)}) %collective-permute-start.11) | collective-permute-done | bytes 147488 | tf_op jit(solution)/shard_map/ppermute | solution.py:271
  63.0 1.5 %collective-permute-done.12.d_ref = f32[64,576]{1,0:T(8,128)S(1)} collective-permute-done((f32[64,576]{1,0:T(8,128)S(1)}, f32[64,576]{1,0:T(8,128)S(1)}, u32[]{:S(2)}, u32[]{:S(2)}) %collective-permute-start.12) | collective-permute-done | bytes 147488 | tf_op jit(solution)/shard_map/ppermute | solution.py:271
  64.4 1.8 %finish_keys.1 = bf16[8,64,640]{2,1,0:T(8,128)(2,1)} custom-call(s32[2]{0:T(128)} %pad_add_fusion.info, f32[64,576]{1,0:T(8,128)S(1)} %get-tuple-element.43.a_ref, f32[64,576]{1,0:T(8,128)S(1)} %collective-permute-done.10.b_ref, f32[64,576]{1,0:T(8,128)S(1)} %collective-permute-done.11.c_ref, f32[64,576]{1,0:T(8,128)S(1)} %collective-permute-done.12.d_ref, ...), custom_call_target="tpu_custom_call" | custom-call | tf_op jit(solution)/shard_map/finish_keys/pallas_call | solution.py:122
  66.2 26.2 %all_to_all.20 = bf16[8,64,640]{2,1,0:T(8,128)(2,1)S(1)} all-to-all(bf16[8,64,640]{2,1,0:T(8,128)(2,1)} %finish_keys.1), channel_id=1, replica_groups={{0,1,2,3,4,5,6,7},{8,9,10,11,12,13,14,15},{16,17,18,19,20,21,22,23},{24..., dimensions={0} | all-to-all | bytes 1310720 | tf_op jit(solution)/shard_map/all_to_all | solution.py:305
  92.4 0.6 collective-permute-start.14
  93.0 1.5 %collective-permute-start.13 = (bf16[512,640]{1,0:T(8,128)(2,1)S(1)}, bf16[512,640]{1,0:T(8,128)(2,1)S(1)}, u32[]{:S(2)}, u32[]{:S(2)}) collective-permute-start(bf16[512,640]{1,0:T(8,128)(2,1)S(1)} %bitcast.32), channel_id=1, source_target_pairs={{0,8},{1,9},{2,10},{3,11},{4,12},{5,13},{6,14},{7,15},{8,16},{9,17... | collective-permute-start | bytes 1966088 | tf_op jit(solution)/shard_map/ppermute | solution.py:307
  94.4 12.7 %attend_first.2 = (f32[4096,512]{1,0:T(8,128)S(1)}, f32[4096,128]{1,0:T(8,128)S(1)}, f32[4096,128]{1,0:T(8,128)S(1)}) custom-call(s32[2]{0:T(128)S(1)} %copy-done.1, bf16[4096,576]{1,0:T(8,128)(2,1)} %bitcast.21, bf16[512,640]{1,0:T(8,128)(2,1)S(1)} %bitcast.33, bf16[256,640]{1,0:T(8,128)(2,1)S(1)} %bitcast.35), custom_call_target="tpu_custom_call" | custom-call | flops 6845104128 | bytes 8388608 | tf_op jit(solution)/shard_map/attend_first/pallas_call | solution.py:215
  107.2 9.8 %collective-permute-start.15 = (bf16[512,640]{1,0:T(8,128)(2,1)S(1)}, bf16[512,640]{1,0:T(8,128)(2,1)S(1)}, u32[]{:S(2)}, u32[]{:S(2)}) collective-permute-start(bf16[512,640]{1,0:T(8,128)(2,1)S(1)} %bitcast.34), channel_id=1, source_target_pairs={{0,16},{1,17},{2,18},{3,19},{4,20},{5,21},{6,22},{7,23},{8,24},{9,... | collective-permute-start | bytes 1966088 | tf_op jit(solution)/shard_map/ppermute | solution.py:313
  116.9 16.0 %attend_first.3 = (f32[4096,512]{1,0:T(8,128)S(1)}, f32[4096,128]{1,0:T(8,128)S(1)}, f32[4096,128]{1,0:T(8,128)S(1)}) custom-call(s32[2]{0:T(128)S(1)} %copy-done.1, bf16[4096,576]{1,0:T(8,128)(2,1)S(1)} %bitcast.24, f32[4096,512]{1,0:T(8,128)S(1)} %get-tuple-element.52.refs_1_, f32[4096,128]{1,0:T(8,128)S(1)} %get-tuple-element.53.refs_2_, ...), custom_call_target="tpu_custom_call" | custom-call | flops 9126805504 | bytes 8388608 | tf_op jit(solution)/shard_map/attend_first/pallas_call | solution.py:215
  133.0 9.5 %attend_last.1 = bf16[4096,512]{1,0:T(8,128)(2,1)} custom-call(s32[2]{0:T(128)S(1)} %copy-done.1, bf16[4096,576]{1,0:T(8,128)(2,1)S(1)} %bitcast.25, f32[4096,512]{1,0:T(8,128)S(1)} %get-tuple-element.57.refs_1_, f32[4096,128]{1,0:T(8,128)S(1)} %get-tuple-element.58.refs_2_, f32[4096,128]{1,0:T(8,128)S(1)} %get-tuple-element.59.refs_3_, ...), custom_call_target="tpu_custom_call" | custom-call | flops 4563402752 | bytes 8388608 | tf_op jit(solution)/shard_map/attend_last/pallas_call | solution.py:215
  (44 shorter events, 0.4 us)
Async XLA Ops:
  0.0 1.0 copy-start
  1.7 21.7 %all-to-all-start = ((bf16[8,32,576]{2,1,0:T(8,128)(2,1)}), bf16[8,32,576]{2,1,0:T(8,128)(2,1)S(1)}, u32[]{:S(2)}, u32[]{:S(2)}) async-start(bf16[8,32,576]{2,1,0:T(8,128)(2,1)} %broadcast_in_dim.69), calls=%async_computation | async-start | bytes 655360 | tf_op jit(solution)/shard_map/all_to_all | solution.py:245
  10.2 6.4 %copy-start.5 = (s32[8]{0:T(128)S(1)}, s32[8]{0:T(128)}, u32[]{:S(2)}) copy-start(s32[8]{0:T(128)} %param.15) | copy-start | bytes 100
  10.2 8.8 %copy-start.3 = (s32[8,8]{1,0:T(8,128)S(1)}, s32[8,8]{1,0:T(8,128)}, u32[]{:S(2)}) copy-start(s32[8,8]{1,0:T(8,128)} %param.13) | copy-start | bytes 772
  10.2 9.1 %copy-start.4 = (s32[8,8]{1,0:T(8,128)S(1)}, s32[8,8]{1,0:T(8,128)}, u32[]{:S(2)}) copy-start(s32[8,8]{1,0:T(8,128)} %param.14) | copy-start | bytes 772
  10.2 16.6 %copy-start.2 = (bf16[12,1,576]{2,0,1:T(8,128)(2,1)S(1)}, bf16[12,1,576]{2,0,1:T(8,128)(2,1)}, u32[]{:S(2)}) copy-start(bf16[12,1,576]{2,0,1:T(8,128)(2,1)} %param.12) | copy-start | bytes 41476
  13.1 13.8 %collective-permute-start = (bf16[64,2048]{1,0:T(8,128)(2,1)}, bf16[64,2048]{1,0:T(8,128)(2,1)S(1)}, u32[]{:S(2)}, u32[]{:S(2)}) collective-permute-start(bf16[64,2048]{1,0:T(8,128)(2,1)} %get-tuple-element.36), channel_id=1, source_target_pairs={{0,192},{32,224},{64,128},{96,160},{128,64},{160,96},{192,0},{224,... | collective-permute-start | bytes 786440 | tf_op jit(solution)/shard_map/ppermute | solution.py:251
  14.5 23.0 %collective-permute-start.1 = (bf16[64,2048]{1,0:T(8,128)(2,1)}, bf16[64,2048]{1,0:T(8,128)(2,1)S(1)}, u32[]{:S(2)}, u32[]{:S(2)}) collective-permute-start(bf16[64,2048]{1,0:T(8,128)(2,1)} %get-tuple-element.39), channel_id=1, source_target_pairs={{0,64},{32,96},{64,0},{96,32},{128,192},{160,224},{192,128},{224,1... | collective-permute-start | bytes 786440 | tf_op jit(solution)/shard_map/ppermute | solution.py:251
  16.3 23.8 %collective-permute-start.2 = (bf16[64,2048]{1,0:T(8,128)(2,1)}, bf16[64,2048]{1,0:T(8,128)(2,1)S(1)}, u32[]{:S(2)}, u32[]{:S(2)}) collective-permute-start(bf16[64,2048]{1,0:T(8,128)(2,1)} %get-tuple-element.40), channel_id=1, source_target_pairs={{0,128},{32,160},{64,192},{96,224},{128,0},{160,32},{192,64},{224,... | collective-permute-start | bytes 786440 | tf_op jit(solution)/shard_map/ppermute | solution.py:251
  18.9 75.6 %copy-start.1 = (s32[2]{0:T(128)S(1)}, s32[2]{0:T(128)}, u32[]{:S(2)}) copy-start(s32[2]{0:T(128)} %pad_add_fusion.info) | copy-start | bytes 28
  23.5 14.1 %collective-permute-start.5 = (bf16[256,576]{1,0:T(8,128)(2,1)S(1)}, bf16[256,576]{1,0:T(8,128)(2,1)S(1)}, u32[]{:S(2)}, u32[]{:S(2)}) collective-permute-start(bf16[256,576]{1,0:T(8,128)(2,1)S(1)} %bitcast.26), channel_id=1, source_target_pairs={{0,24},{1,25},{2,26},{3,27},{4,28},{5,29},{6,30},{7,31},{8,0},{9,1... | collective-permute-start | bytes 884744 | tf_op jit(solution)/shard_map/ppermute | solution.py:266
  23.9 14.2 %collective-permute-start.4 = (bf16[256,576]{1,0:T(8,128)(2,1)S(1)}, bf16[256,576]{1,0:T(8,128)(2,1)S(1)}, u32[]{:S(2)}, u32[]{:S(2)}) collective-permute-start(bf16[256,576]{1,0:T(8,128)(2,1)S(1)} %bitcast.27), channel_id=1, source_target_pairs={{0,16},{1,17},{2,18},{3,19},{4,20},{5,21},{6,22},{7,23},{8,24},{9,... | collective-permute-start | bytes 884744 | tf_op jit(solution)/shard_map/ppermute | solution.py:266
  26.8 13.1 %collective-permute-start.3 = (bf16[256,576]{1,0:T(8,128)(2,1)S(1)}, bf16[256,576]{1,0:T(8,128)(2,1)S(1)}, u32[]{:S(2)}, u32[]{:S(2)}) collective-permute-start(bf16[256,576]{1,0:T(8,128)(2,1)S(1)} %bitcast.28), channel_id=1, source_target_pairs={{0,8},{1,9},{2,10},{3,11},{4,12},{5,13},{6,14},{7,15},{8,16},{9,17... | collective-permute-start | bytes 884744 | tf_op jit(solution)/shard_map/ppermute | solution.py:266
  28.1 8.8 %all-to-all-start.1 = ((bf16[8,2,576]{2,1,0:T(2,128)(2,1)}), bf16[8,2,576]{2,1,0:T(2,128)(2,1)S(1)}, u32[]{:S(2)}, u32[]{:S(2)}) async-start(bf16[8,2,576]{2,1,0:T(2,128)(2,1)} %broadcast_select_fusion), calls=%async_computation.1 | async-start | bytes 40960 | tf_op jit(solution)/shard_map/all_to_all | solution.py:290
  37.5 2.6 %collective-permute-start.6 = (bf16[256,576]{1,0:T(8,128)(2,1)S(1)}, bf16[256,576]{1,0:T(8,128)(2,1)S(1)}, u32[]{:S(2)}, u32[]{:S(2)}) collective-permute-start(bf16[256,576]{1,0:T(8,128)(2,1)S(1)} %bitcast.29), channel_id=1, source_target_pairs={{0,32},{32,0},{64,96},{96,64},{128,160},{160,128},{192,224},{224,1... | collective-permute-start | bytes 884744 | tf_op jit(solution)/shard_map/ppermute | solution.py:267
  37.6 2.5 %collective-permute-start.9 = (bf16[256,576]{1,0:T(8,128)(2,1)S(1)}, bf16[256,576]{1,0:T(8,128)(2,1)S(1)}, u32[]{:S(2)}, u32[]{:S(2)}) collective-permute-start(bf16[256,576]{1,0:T(8,128)(2,1)S(1)} %collective-permute-done.5.refs_7_), channel_id=1, source_target_pairs={{0,32},{32,0},{64,96},{96,64},{128,160},{160,128},{192,224},{224,1... | collective-permute-start | bytes 884744 | tf_op jit(solution)/shard_map/ppermute | solution.py:267
  38.1 2.0 %collective-permute-start.8 = (bf16[256,576]{1,0:T(8,128)(2,1)S(1)}, bf16[256,576]{1,0:T(8,128)(2,1)S(1)}, u32[]{:S(2)}, u32[]{:S(2)}) collective-permute-start(bf16[256,576]{1,0:T(8,128)(2,1)S(1)} %collective-permute-done.4.refs_6_), channel_id=1, source_target_pairs={{0,32},{32,0},{64,96},{96,64},{128,160},{160,128},{192,224},{224,1... | collective-permute-start | bytes 884744 | tf_op jit(solution)/shard_map/ppermute | solution.py:267
  40.0 1.6 %collective-permute-start.7 = (bf16[256,576]{1,0:T(8,128)(2,1)S(1)}, bf16[256,576]{1,0:T(8,128)(2,1)S(1)}, u32[]{:S(2)}, u32[]{:S(2)}) collective-permute-start(bf16[256,576]{1,0:T(8,128)(2,1)S(1)} %collective-permute-done.3.refs_5_), channel_id=1, source_target_pairs={{0,32},{32,0},{64,96},{96,64},{128,160},{160,128},{192,224},{224,1... | collective-permute-start | bytes 884744 | tf_op jit(solution)/shard_map/ppermute | solution.py:267
  43.9 22.3 %all-to-all-start.2 = ((bf16[32,8,640]{2,1,0:T(8,128)(2,1)}), bf16[32,8,640]{2,1,0:T(8,128)(2,1)S(1)}, u32[]{:S(2)}, u32[]{:S(2)}) async-start(bf16[32,8,640]{2,1,0:T(8,128)(2,1)} %broadcast_in_dim.73), calls=%async_computation.2 | async-start | bytes 655360 | tf_op jit(solution)/shard_map/all_to_all | solution.py:299
  52.1 6.4 %collective-permute-start.10 = (f32[64,576]{1,0:T(8,128)S(1)}, f32[64,576]{1,0:T(8,128)S(1)}, u32[]{:S(2)}, u32[]{:S(2)}) collective-permute-start(f32[64,576]{1,0:T(8,128)S(1)} %get-tuple-element.44), channel_id=1, source_target_pairs={{0,64},{32,96},{64,0},{96,32},{128,192},{160,224},{192,128},{224,1... | collective-permute-start | bytes 442376 | tf_op jit(solution)/shard_map/ppermute | solution.py:271
  53.8 9.1 %collective-permute-start.11 = (f32[64,576]{1,0:T(8,128)S(1)}, f32[64,576]{1,0:T(8,128)S(1)}, u32[]{:S(2)}, u32[]{:S(2)}) collective-permute-start(f32[64,576]{1,0:T(8,128)S(1)} %get-tuple-element.45), channel_id=1, source_target_pairs={{0,128},{32,160},{64,192},{96,224},{128,0},{160,32},{192,64},{224,... | collective-permute-start | bytes 442376 | tf_op jit(solution)/shard_map/ppermute | solution.py:271
  55.5 8.9 %collective-permute-start.12 = (f32[64,576]{1,0:T(8,128)S(1)}, f32[64,576]{1,0:T(8,128)S(1)}, u32[]{:S(2)}, u32[]{:S(2)}) collective-permute-start(f32[64,576]{1,0:T(8,128)S(1)} %get-tuple-element.46), channel_id=1, source_target_pairs={{0,192},{32,224},{64,128},{96,160},{128,64},{160,96},{192,0},{224,... | collective-permute-start | bytes 442376 | tf_op jit(solution)/shard_map/ppermute | solution.py:271
  66.2 50.7 %slice-start = ((s8[5242880]{0:T(1024)(128)(4,1)}), s8[4194304]{0:T(1024)(128)(4,1)S(1)}, s32[]{:S(2)}) async-start(s8[5242880]{0:T(1024)(128)(4,1)} %bitcast.22), calls=%async_computation.4 | async-start | bytes 8388608
  92.4 14.7 %collective-permute-start.14 = (bf16[512,640]{1,0:T(8,128)(2,1)S(1)}, bf16[512,640]{1,0:T(8,128)(2,1)S(1)}, u32[]{:S(2)}, u32[]{:S(2)}) collective-permute-start(bf16[512,640]{1,0:T(8,128)(2,1)S(1)} %bitcast.31), channel_id=1, source_target_pairs={{0,24},{1,25},{2,26},{3,27},{4,28},{5,29},{6,30},{7,31},{8,0},{9,1... | collective-permute-start | bytes 1966088 | tf_op jit(solution)/shard_map/ppermute | solution.py:307
  93.0 14.2 %collective-permute-start.13 = (bf16[512,640]{1,0:T(8,128)(2,1)S(1)}, bf16[512,640]{1,0:T(8,128)(2,1)S(1)}, u32[]{:S(2)}, u32[]{:S(2)}) collective-permute-start(bf16[512,640]{1,0:T(8,128)(2,1)S(1)} %bitcast.32), channel_id=1, source_target_pairs={{0,8},{1,9},{2,10},{3,11},{4,12},{5,13},{6,14},{7,15},{8,16},{9,17... | collective-permute-start | bytes 1966088 | tf_op jit(solution)/shard_map/ppermute | solution.py:307
  94.4 22.5 %slice-start.1 = ((s8[5242880]{0:T(1024)(128)(4,1)}), s8[1048576]{0:T(1024)(128)(4,1)S(1)}, s32[]{:S(2)}) async-start(s8[5242880]{0:T(1024)(128)(4,1)} %bitcast.22), calls=%async_computation.5 | async-start | bytes 2097152
  107.2 25.8 %collective-permute-start.15 = (bf16[512,640]{1,0:T(8,128)(2,1)S(1)}, bf16[512,640]{1,0:T(8,128)(2,1)S(1)}, u32[]{:S(2)}, u32[]{:S(2)}) collective-permute-start(bf16[512,640]{1,0:T(8,128)(2,1)S(1)} %bitcast.34), channel_id=1, source_target_pairs={{0,16},{1,17},{2,18},{3,19},{4,20},{5,21},{6,22},{7,23},{8,24},{9,... | collective-permute-start | bytes 1966088 | tf_op jit(solution)/shard_map/ppermute | solution.py:313
